TPU v7x, 256 devices: a whole 4x4x8 slice. The times are simulated.
256 devices in a mesh: group: 8 (over x, z_lo), shard: 32 (over y, z_hi, core).
Axes of the slice: x: 4, y: 4, z: 8 (z_hi: 4, z_lo: 2; z = z_hi * 2 + z_lo), core: 2. Of those that a mesh axis runs over, the one named last changes fastest.
Arguments:
- numerators: float32 [8, 128, 5120], P('group', 'shard'), may hold values from -6 to 6
- push_weight: float32 [8], P('group'), may hold values from 0.5 to 2
- keep_share: float32 [8], P('group'), may hold values from 0.25 to 0.75
- momentum: float32 [8, 128, 5120], P('group', 'shard'), may hold values from -4 to 4
- grads: float32 [3, 8, 32, 128, 5120], P(None, 'group', 'shard'), may hold values from -6 to 6
Outputs:
- displacement: float32 [8, 128, 5120], P('group', 'shard')
- momentum_out: float32 [8, 128, 5120], P('group', 'shard')
- weight_out: float32 [8], P('group')
All inputs are finite; a program needn't handle non-finite values.
Results may differ from a plain program's by a relative error of at most 0.0001.
Values sent between devices are 32-bit elements; how exact they have to be, the bound alone decides.
No kernel may reach another device: no remote copies, remote signals or barrier semaphores. Data moves between devices by JAX's collectives and lax.ppermute only.
A program may use at most 64 MiB of HBM per device.

v0:
```python
import jax
from jax import lax
from jax.sharding import PartitionSpec as P

STEPS = 3


learn_rate = 0.5
momentum_factor = 0.9


def passed_along(x, axis, by):
    length = lax.axis_size(axis)
    return lax.ppermute(x, axis, [(i, (i + by) % length) for i in range(length)])


def pass_along(value, distance):
    return passed_along((value[0], value[1]), "group", distance)


def per_device(numerators, push_weight, keep_share, momentum, grads):
    count = lax.axis_size("shard")
    levels = lax.axis_size("group").bit_length() - 1
    values = numerators
    weight = push_weight
    buffer = momentum
    keep_rows = keep_share[:, None, None]
    for step in range(STEPS):
        piece = grads[step, 0, 0]
        total = lax.psum_scatter(piece, "shard", scatter_dimension=0, tiled=True)
        mean = (total / count)[None]
        buffer = momentum_factor * buffer + mean
        values = values - learn_rate * (mean + momentum_factor * buffer)
        distance = 1 << step % levels
        sent_values, sent_weight = pass_along(
            ((1.0 - keep_rows) * values, (1.0 - keep_share) * weight), distance
        )
        values = keep_rows * values + sent_values
        weight = keep_share * weight + sent_weight
    displacement = values / weight[:, None, None] - numerators / push_weight[:, None, None]
    return (displacement, buffer, weight)


def solution(mesh):
    in_specs = (
        P("group", "shard", None),
        P("group"),
        P("group"),
        P("group", "shard", None),
        P(None, "group", "shard", None, None),
    )
    out_specs = (P("group", "shard", None), P("group", "shard", None), P("group"))
    return jax.shard_map(
        per_device, mesh=mesh, in_specs=in_specs, out_specs=out_specs, check_vma=False
    )
```

profile of v0, /device:TPU:0, one launch (start us, length us, event | category | flops | bytes accessed | tf_op | source)
XLA Modules:
  0.0 382.5 jit_solution(13410737813266245204)
XLA Ops:
  7.2 0.0 all-reduce.6.cloned.1.call-start
  7.2 6.6 %slice_bitcast_fusion.2 = (f32[128,5120]{1,0:T(8,128)}, f32[128,5120]{1,0:T(8,128)}, f32[128,5120]{1,0:T(8,128)}) fusion(f32[3,1,1,128,5120]{4,3,2,1,0:T(8,128)} %param.9), kind=kLoop, calls=%fused_computation.2 | loop fusion | bytes 15728640 | tf_op jit(solution)/shard_map/squeeze | solution.py:29
  13.8 0.0 all-reduce.6.cloned.1.call-update
  14.5 0.0 copy-done.2
  14.6 0.6 dynamic-slice
  15.8 321.8 %all-reduce.6.cloned.1.call-done = (f32[128,5120]{1,0:T(8,128)}, f32[128,5120]{1,0:T(8,128)}, f32[128,5120]{1,0:T(8,128)}) async-done(((f32[128,5120]{1,0:T(8,128)}, f32[128,5120]{1,0:T(8,128)}, f32[128,5120]{1,0:T(8,128)}), (f32[128,5120]{1,0:T(8,128)}, f32[128,5120]{1,0:T(8,128)}, f32[128,5120]{1,0:T(8,128)})) %all-reduce.6.cloned.1.call-update) | async-done | bytes 7864336
  337.5 0.0 copy-done
  337.6 0.0 copy-done.1
  337.6 1.0 broadcast_multiply_fusion.2
  338.5 2.4 collective-permute-start
  341.0 5.4 %collective-permute-done = f32[1,4,5120]{2,1,0:T(4,128)S(1)} collective-permute-done((f32[1,4,5120]{2,1,0:T(4,128)S(1)}, f32[1,4,5120]{2,1,0:T(4,128)S(1)}, u32[]{:S(2)}, u32[]{:S(2)}) %collective-permute-start) | collective-permute-done | bytes 81952 | tf_op jit(solution)/shard_map/ppermute | solution.py:14
  346.3 1.1 broadcast_multiply_fusion.1
  347.4 0.3 collective-permute-start.1
  347.7 5.5 %collective-permute-done.1 = f32[1,4,5120]{2,1,0:T(4,128)S(1)} collective-permute-done((f32[1,4,5120]{2,1,0:T(4,128)S(1)}, f32[1,4,5120]{2,1,0:T(4,128)S(1)}, u32[]{:S(2)}, u32[]{:S(2)}) %collective-permute-start.1) | collective-permute-done | bytes 81952 | tf_op jit(solution)/shard_map/ppermute | solution.py:14
  353.2 1.8 broadcast_multiply_fusion
  355.0 0.8 collective-permute-start.2
  356.4 2.0 collective-permute-start.3
  358.4 3.7 collective-permute-done.3
  362.8 1.9 collective-permute-start.4
  364.7 2.8 collective-permute-done.4
  368.2 1.7 collective-permute-start.5
  369.9 3.4 collective-permute-done.5
  373.9 0.0 collective-permute-done.2
  373.9 0.7 divide_subtract_fusion
  (3 shorter events, 0.0 us)
Async XLA Ops:
  7.2 330.4 %all-reduce.6.cloned.1.call-start = ((), (), s32[]{:S(2)}) async-start(), calls=%async_computation | async-start | bytes 15728640
  13.8 0.7 copy-start.2
  13.8 323.7 %copy-start = (f32[1,4,5120]{2,1,0:T(4,128)S(1)}, f32[1,4,5120]{2,1,0:T(4,128)}, u32[]{:S(2)}) copy-start(f32[1,4,5120]{2,1,0:T(4,128)} %param.8) | copy-start | bytes 245764
  13.8 323.7 %copy-start.1 = (f32[1,4,5120]{2,1,0:T(4,128)S(1)}, f32[1,4,5120]{2,1,0:T(4,128)}, u32[]{:S(2)}) copy-start(f32[1,4,5120]{2,1,0:T(4,128)} %param.5) | copy-start | bytes 245764
  338.5 7.8 %collective-permute-start = (f32[1,4,5120]{2,1,0:T(4,128)S(1)}, f32[1,4,5120]{2,1,0:T(4,128)S(1)}, u32[]{:S(2)}, u32[]{:S(2)}) collective-permute-start(f32[1,4,5120]{2,1,0:T(4,128)S(1)} %broadcast_multiply_fusion.2), channel_id=1, source_target_pairs={{0,32},{32,64},{64,96},{96,128},{128,160},{160,192},{192,224},{224... | collective-permute-start | bytes 245768 | tf_op jit(solution)/shard_map/ppermute | solution.py:14
  347.4 5.7 %collective-permute-start.1 = (f32[1,4,5120]{2,1,0:T(4,128)S(1)}, f32[1,4,5120]{2,1,0:T(4,128)S(1)}, u32[]{:S(2)}, u32[]{:S(2)}) collective-permute-start(f32[1,4,5120]{2,1,0:T(4,128)S(1)} %get-tuple-element.9), channel_id=1, source_target_pairs={{0,64},{32,96},{64,128},{96,160},{128,192},{160,224},{192,0},{224,... | collective-permute-start | bytes 245768 | tf_op jit(solution)/shard_map/ppermute | solution.py:14
  355.0 18.9 %collective-permute-start.2 = (f32[1,4,5120]{2,1,0:T(4,128)S(1)}, f32[1,4,5120]{2,1,0:T(4,128)S(1)}, u32[]{:S(2)}, u32[]{:S(2)}) collective-permute-start(f32[1,4,5120]{2,1,0:T(4,128)S(1)} %get-tuple-element.6), channel_id=1, source_target_pairs={{0,128},{32,160},{64,192},{96,224},{128,0},{160,32},{192,64},{224,... | collective-permute-start | bytes 245768 | tf_op jit(solution)/shard_map/ppermute | solution.py:14
  356.4 5.7 %collective-permute-start.3 = (f32[1]{0:T(128)}, f32[1]{0:T(128)}, u32[]{:S(2)}, u32[]{:S(2)}) collective-permute-start(f32[1]{0:T(128)} %mul.103), channel_id=1, source_target_pairs={{0,32},{32,64},{64,96},{96,128},{128,160},{160,192},{192,224},{224... | collective-permute-start | bytes 20 | tf_op jit(solution)/shard_map/ppermute | solution.py:14
  362.8 4.8 %collective-permute-start.4 = (f32[1]{0:T(128)}, f32[1]{0:T(128)}, u32[]{:S(2)}, u32[]{:S(2)}) collective-permute-start(f32[1]{0:T(128)} %mul.105), channel_id=1, source_target_pairs={{0,64},{32,96},{64,128},{96,160},{128,192},{160,224},{192,0},{224,... | collective-permute-start | bytes 20 | tf_op jit(solution)/shard_map/ppermute | solution.py:14
  368.2 5.1 %collective-permute-start.5 = (f32[1]{0:T(128)}, f32[1]{0:T(128)}, u32[]{:S(2)}, u32[]{:S(2)}) collective-permute-start(f32[1]{0:T(128)} %mul.107), channel_id=1, source_target_pairs={{0,128},{32,160},{64,192},{96,224},{128,0},{160,32},{192,64},{224,... | collective-permute-start | bytes 20 | tf_op jit(solution)/shard_map/ppermute | solution.py:14
Sparse Core Ops, SparseCore 0:
  14.0 323.5 all-reduce.5
where the time goes:
time: 383 us
  waiting for transfers between devices  342 us (89%)
  between operations  19.1 us (5%)
  starting transfers between devices  9.17 us (2%)
  local copies, waits for them, and re-layouts  7.2 us (2%)
  other arithmetic  4.6 us (1%)
    unnamed x2, waiting for transfers between devices  322 us
    ppermute x6, waiting for transfers between devices, passed_along(): lax.ppermute(x, axis, [(i, (i + by) % length) for i in range(length)])  20.7 us
    ppermute x6, starting transfers between devices, passed_along(): lax.ppermute(x, axis, [(i, (i + by) % length) for i in range(length)])  9.14 us
  transfers between devices with their start and end apart: 7, of which 6 were waited for; matrix products, arithmetic and copies ran while one was open for 0% of the time, Pallas kernels for 0%

commit v1 on v0

v1 whole, which is shorter than its diff:
```python
import jax
import jax.numpy as jnp
from jax import lax
from jax.experimental import pallas as pl
from jax.experimental.pallas import tpu as pltpu
from jax.sharding import Mesh, PartitionSpec as P

STEPS = 3
ROWS = 128
D = 5120
HALF = D // 2
X, ZL, Y, ZH, CORE = 4, 2, 4, 4, 2
GROUP = ("x", "zl")
SHARD = ("y", "zh", "core")

learn_rate = 0.5
momentum_factor = 0.9


def ring(x, axis, by):
    n = lax.axis_size(axis)
    return lax.ppermute(x, axis, [(i, (i + by) % n) for i in range(n)])


def split_kernel(where_ref, g_ref, other_ref, own_ref):
    core = where_ref[1]
    row = lax.broadcasted_iota(jnp.int32, (8, D), 0)
    for m in range(2):
        low = g_ref[0, 0, 0, 16 * m : 16 * m + 8, :]
        high = g_ref[0, 0, 0, 16 * m + 8 : 16 * m + 16, :]
        first = jnp.where(row < 4, low, pltpu.roll(high, 4, 0))
        second = jnp.where(row < 4, pltpu.roll(low, 4, 0), high)
        own_ref[0, 8 * m : 8 * m + 8, :] = jnp.where(core == 0, first, second)
        other_ref[0, 8 * m : 8 * m + 8, :] = jnp.where(core == 0, second, first)


def split_cores(where, grads, step):
    shape = jax.ShapeDtypeStruct((Y, 16, D), jnp.float32)
    out = pl.BlockSpec((1, 16, D), lambda r, w: (r, 0, 0))
    return pl.pallas_call(
        split_kernel,
        out_shape=(shape, shape),
        grid_spec=pltpu.PrefetchScalarGridSpec(
            num_scalar_prefetch=1,
            grid=(Y,),
            in_specs=[
                pl.BlockSpec((1, 1, 1, 32, D), lambda r, w: (step, 0, 0, lax.rem(w[0] + r, Y), 0))
            ],
            out_specs=(out, out),
        ),
        cost_estimate=pl.CostEstimate(flops=0, bytes_accessed=2 * ROWS * D * 4, transcendentals=0),
    )(where, grads)


def shard_mean(where, grads, step):
    zh = lax.axis_index("zh")
    other, own = split_cores(where, grads, step)
    part = own + ring(other, "core", 1)
    from_low = ring(part[2, :, :HALF], "y", 1)
    from_high = ring(part[2, :, HALF:], "y", -1)
    up = jnp.concatenate([part[1, :, :HALF] + from_low, part[1, :, HALF:]], axis=1)
    down = jnp.concatenate([part[3, :, :HALF], part[3, :, HALF:] + from_high], axis=1)
    total = part[0] + ring(up, "y", 1) + ring(down, "y", -1)
    rows = [
        lax.dynamic_slice_in_dim(total, 4 * ((zh + k) % ZH), 4, 0) for k in range(ZH)
    ]
    out = rows[0]
    for k in range(1, ZH):
        out = out + ring(rows[k], "zh", k)
    return (out / (Y * ZH * CORE))[None]


def group_weights(push_weight, keep_share):
    both = lax.all_gather(jnp.stack([push_weight, keep_share], axis=1), GROUP, axis=0, tiled=True)
    weights, keep = both[:, 0], both[:, 1]
    levels = (X * ZL).bit_length() - 1
    for step in range(STEPS):
        distance = 1 << step % levels
        weights = keep * weights + jnp.roll((1.0 - keep) * weights, distance)
    me = lax.axis_index("x") * ZL + lax.axis_index("zl")
    return lax.dynamic_slice_in_dim(weights, me, 1)


def per_device(numerators, push_weight, keep_share, momentum, grads):
    levels = (X * ZL).bit_length() - 1
    where = jnp.stack([lax.axis_index("y"), lax.axis_index("core")]).astype(jnp.int32)
    weight = group_weights(push_weight, keep_share)
    means = [shard_mean(where, grads, step) for step in range(STEPS)]
    values = numerators
    buffer = momentum
    keep_rows = keep_share[:, None, None]
    for step in range(STEPS):
        mean = means[step]
        buffer = momentum_factor * buffer + mean
        values = values - learn_rate * (mean + momentum_factor * buffer)
        sent = ring((1.0 - keep_rows) * values, GROUP, 1 << step % levels)
        values = keep_rows * values + sent
    displacement = values / weight[:, None, None] - numerators / push_weight[:, None, None]
    return (displacement, buffer, weight)


def solution(mesh):
    fine = Mesh(mesh.devices.reshape(X, ZL, Y, ZH, CORE), GROUP + SHARD)
    in_specs = (
        P(GROUP, SHARD, None),
        P(GROUP),
        P(GROUP),
        P(GROUP, SHARD, None),
        P(None, GROUP, SHARD, None, None),
    )
    out_specs = (P(GROUP, SHARD, None), P(GROUP, SHARD, None), P(GROUP))
    return jax.shard_map(
        per_device, mesh=fine, in_specs=in_specs, out_specs=out_specs, check_vma=False
    )
```

time: 383 us -> 108 us (0.28)
  the two profiles are of different devices: /device:TPU:0 before, /device:TPU:24 now
where the time goes in v1:
time: 108 us
  starting transfers between devices  39.8 us (37%)
  waiting for transfers between devices  24.3 us (22%)
  blocking collectives  19.1 us (18%)
  Pallas kernels  14.3 us (13%)
  other arithmetic  6.43 us (6%)
  between operations  2.14 us (2%)
  local copies, waits for them, and re-layouts  1.71 us (2%)
    ppermute x27, starting transfers between devices, ring(): return lax.ppermute(x, axis, [(i, (i + by) % n) for i in range(n)])  39.8 us
    ppermute x27, waiting for transfers between devices, ring(): return lax.ppermute(x, axis, [(i, (i + by) % n) for i in range(n)])  24.3 us
    all_gather x1, blocking collectives, group_weights(): lax.all_gather(jnp.stack([push_weight, keep_share], axis=1), GROUP, axis=...  19.1 us
    pallas_call x3, Pallas kernels, split_cores(): pl.pallas_call(split_kernel, out_shape=(shape, shape), grid_spec=pltpu.Pr...  14.3 us
    add x3, other arithmetic, shard_mean(): part = own + ring(other, 'core', 1)  2.22 us
  transfers between devices with their start and end apart: 27, of which 10 were waited for; matrix products, arithmetic and copies ran while one was open for 5% of the time, Pallas kernels for 9%

profile of v1, /device:TPU:24, one launch (start us, length us, event | category | flops | bytes accessed | tf_op | source)
XLA Modules:
  0.0 107.7 jit_solution(15977512795596134151)
XLA Ops:
  1.2 4.7 %shard_map.76 = (f32[4,16,5120]{2,1,0:T(8,128)}, f32[4,16,5120]{2,1,0:T(8,128)}) custom-call(s32[2]{0:T(128)} %pad_add_fusion.where_ref, f32[3,1,1,128,5120]{4,3,2,1,0:T(8,128)} %g_ref.5), custom_call_target="tpu_custom_call" | custom-call | bytes 5242880 | tf_op jit(solution)/shard_map/pallas_call | solution.py:40
  6.0 4.7 %shard_map.77 = (f32[4,16,5120]{2,1,0:T(8,128)}, f32[4,16,5120]{2,1,0:T(8,128)}) custom-call(s32[2]{0:T(128)} %pad_add_fusion.where_ref, f32[3,1,1,128,5120]{4,3,2,1,0:T(8,128)} %g_ref.5), custom_call_target="tpu_custom_call" | custom-call | bytes 5242880 | tf_op jit(solution)/shard_map/pallas_call | solution.py:40
  11.2 4.8 %shard_map.78 = (f32[4,16,5120]{2,1,0:T(8,128)}, f32[4,16,5120]{2,1,0:T(8,128)}) custom-call(s32[2]{0:T(128)} %pad_add_fusion.where_ref, f32[3,1,1,128,5120]{4,3,2,1,0:T(8,128)} %g_ref.5), custom_call_target="tpu_custom_call" | custom-call | bytes 5242880 | tf_op jit(solution)/shard_map/pallas_call | solution.py:40
  17.4 19.1 %all-gather = f32[8,1,2]{2,1,0:T(1,128)S(1)} all-gather(f32[1,1,2]{2,1,0:T(1,128)S(1)} %maximum_bitcast_fusion), channel_id=1, replica_groups=mesh['x'=4,'zl'=2,'y'=4,'zh'=4,'core'=2] {'x','zl'}, dimensions={0}, use_global_device_ids=true | all-gather | bytes 72 | tf_op jit(solution)/shard_map/all_gather | solution.py:74
  38.1 1.8 %add.170 = f32[4,16,5120]{2,1,0:T(8,128)S(1)} add(f32[4,16,5120]{2,1,0:T(8,128)} %get-tuple-element.9, f32[4,16,5120]{2,1,0:T(8,128)} %collective-permute-done) | non-fusion elementwise | flops 327680 | bytes 3932160 | tf_op jit(solution)/shard_map/add | solution.py:58
  40.3 1.8 %collective-permute-start.3 = (f32[16,2560]{1,0:T(8,128)S(1)}, f32[16,2560]{1,0:T(8,128)S(1)}, u32[]{:S(2)}, u32[]{:S(2)}) collective-permute-start(f32[16,2560]{1,0:T(8,128)S(1)} %get-tuple-element.36), channel_id=1, source_target_pairs={{0,24},{8,0},{16,8},{24,16},{1,25},{9,1},{17,9},{25,17},{2,26},{10... | collective-permute-start | bytes 491528 | tf_op jit(solution)/shard_map/ppermute | solution.py:22
  42.3 1.5 %collective-permute-start.10 = (f32[16,2560]{1,0:T(8,128)S(1)}, f32[16,2560]{1,0:T(8,128)S(1)}, u32[]{:S(2)}, u32[]{:S(2)}) collective-permute-start(f32[16,2560]{1,0:T(8,128)S(1)} %get-tuple-element.29), channel_id=1, source_target_pairs={{0,8},{8,16},{16,24},{24,0},{1,9},{9,17},{17,25},{25,1},{2,10},{10... | collective-permute-start | bytes 491528 | tf_op jit(solution)/shard_map/ppermute | solution.py:22
  44.7 2.7 %collective-permute-start.19 = (f32[16,2560]{1,0:T(8,128)S(1)}, f32[16,2560]{1,0:T(8,128)S(1)}, u32[]{:S(2)}, u32[]{:S(2)}) collective-permute-start(f32[16,2560]{1,0:T(8,128)S(1)} %get-tuple-element.41), channel_id=1, source_target_pairs={{0,8},{8,16},{16,24},{24,0},{1,9},{9,17},{17,25},{25,1},{2,10},{10... | collective-permute-start | bytes 491528 | tf_op jit(solution)/shard_map/ppermute | solution.py:22
  47.7 1.5 %collective-permute-start.4 = (f32[16,5120]{1,0:T(8,128)S(1)}, f32[16,5120]{1,0:T(8,128)S(1)}, u32[]{:S(2)}, u32[]{:S(2)}) collective-permute-start(f32[16,5120]{1,0:T(8,128)S(1)} %pad_maximum_fusion.1), channel_id=1, source_target_pairs={{0,24},{8,0},{16,8},{24,16},{1,25},{9,1},{17,9},{25,17},{2,26},{10... | collective-permute-start | bytes 983048 | tf_op jit(solution)/shard_map/ppermute | solution.py:22
  49.2 1.4 %collective-permute-done.10 = f32[16,2560]{1,0:T(8,128)S(1)} collective-permute-done((f32[16,2560]{1,0:T(8,128)S(1)}, f32[16,2560]{1,0:T(8,128)S(1)}, u32[]{:S(2)}, u32[]{:S(2)}) %collective-permute-start.10) | collective-permute-done | bytes 163872 | tf_op jit(solution)/shard_map/ppermute | solution.py:22
  54.1 1.7 %collective-permute-start.11 = (f32[16,5120]{1,0:T(8,128)S(1)}, f32[16,5120]{1,0:T(8,128)S(1)}, u32[]{:S(2)}, u32[]{:S(2)}) collective-permute-start(f32[16,5120]{1,0:T(8,128)S(1)} %pad_maximum_fusion.2), channel_id=1, source_target_pairs={{0,8},{8,16},{16,24},{24,0},{1,9},{9,17},{17,25},{25,1},{2,10},{10... | collective-permute-start | bytes 983048 | tf_op jit(solution)/shard_map/ppermute | solution.py:22
  56.3 6.4 %collective-permute-done.4 = f32[16,5120]{1,0:T(8,128)S(1)} collective-permute-done((f32[16,5120]{1,0:T(8,128)S(1)}, f32[16,5120]{1,0:T(8,128)S(1)}, u32[]{:S(2)}, u32[]{:S(2)}) %collective-permute-start.4) | collective-permute-done | bytes 327712 | tf_op jit(solution)/shard_map/ppermute | solution.py:22
  62.9 5.5 %collective-permute-start.7 = (f32[4,5120]{1,0:T(4,128)S(1)}, f32[4,5120]{1,0:T(4,128)S(1)}, u32[]{:S(2)}, u32[]{:S(2)}) collective-permute-start(f32[4,5120]{1,0:T(4,128)S(1)} %get-tuple-element.49), channel_id=1, source_target_pairs={{0,6},{2,0},{4,2},{6,4},{1,7},{3,1},{5,3},{7,5},{8,14},{10,8},{12,... | collective-permute-start | bytes 245768 | tf_op jit(solution)/shard_map/ppermute | solution.py:22
  68.3 1.4 %collective-permute-done.13 = f32[16,5120]{1,0:T(8,128)S(1)} collective-permute-done((f32[16,5120]{1,0:T(8,128)S(1)}, f32[16,5120]{1,0:T(8,128)S(1)}, u32[]{:S(2)}, u32[]{:S(2)}) %collective-permute-start.13) | collective-permute-done | bytes 327712 | tf_op jit(solution)/shard_map/ppermute | solution.py:22
  69.8 6.3 %collective-permute-start.6 = (f32[4,5120]{1,0:T(4,128)S(1)}, f32[4,5120]{1,0:T(4,128)S(1)}, u32[]{:S(2)}, u32[]{:S(2)}) collective-permute-start(f32[4,5120]{1,0:T(4,128)S(1)} %get-tuple-element.50), channel_id=1, source_target_pairs={{0,4},{2,6},{4,0},{6,2},{1,5},{3,7},{5,1},{7,3},{8,12},{10,14},{12... | collective-permute-start | bytes 245768 | tf_op jit(solution)/shard_map/ppermute | solution.py:22
  76.0 1.5 %collective-permute-start.5 = (f32[4,5120]{1,0:T(4,128)S(1)}, f32[4,5120]{1,0:T(4,128)S(1)}, u32[]{:S(2)}, u32[]{:S(2)}) collective-permute-start(f32[4,5120]{1,0:T(4,128)S(1)} %get-tuple-element.48), channel_id=1, source_target_pairs={{0,2},{2,4},{4,6},{6,0},{1,3},{3,5},{5,7},{7,1},{8,10},{10,12},{12... | collective-permute-start | bytes 245768 | tf_op jit(solution)/shard_map/ppermute | solution.py:22
  77.6 2.7 %collective-permute-start.16 = (f32[4,5120]{1,0:T(4,128)S(1)}, f32[4,5120]{1,0:T(4,128)S(1)}, u32[]{:S(2)}, u32[]{:S(2)}) collective-permute-start(f32[4,5120]{1,0:T(4,128)S(1)} %get-tuple-element.46), channel_id=1, source_target_pairs={{0,6},{2,0},{4,2},{6,4},{1,7},{3,1},{5,3},{7,5},{8,14},{10,8},{12,... | collective-permute-start | bytes 245768 | tf_op jit(solution)/shard_map/ppermute | solution.py:22
  81.4 1.6 %collective-permute-start.14 = (f32[4,5120]{1,0:T(4,128)S(1)}, f32[4,5120]{1,0:T(4,128)S(1)}, u32[]{:S(2)}, u32[]{:S(2)}) collective-permute-start(f32[4,5120]{1,0:T(4,128)S(1)} %get-tuple-element.45), channel_id=1, source_target_pairs={{0,2},{2,4},{4,6},{6,0},{1,3},{3,5},{5,7},{7,1},{8,10},{10,12},{12... | collective-permute-start | bytes 245768 | tf_op jit(solution)/shard_map/ppermute | solution.py:22
  83.0 1.4 %collective-permute-done.5 = f32[4,5120]{1,0:T(4,128)S(1)} collective-permute-done((f32[4,5120]{1,0:T(4,128)S(1)}, f32[4,5120]{1,0:T(4,128)S(1)}, u32[]{:S(2)}, u32[]{:S(2)}) %collective-permute-start.5) | collective-permute-done | bytes 81952 | tf_op jit(solution)/shard_map/ppermute | solution.py:22
  84.5 2.1 %collective-permute-start.8 = (f32[1,4,5120]{2,1,0:T(4,128)S(1)}, f32[1,4,5120]{2,1,0:T(4,128)S(1)}, u32[]{:S(2)}, u32[]{:S(2)}) collective-permute-start(f32[1,4,5120]{2,1,0:T(4,128)S(1)} %get-tuple-element.25), channel_id=1, source_target_pairs={{0,32},{32,64},{64,96},{96,128},{128,160},{160,192},{192,224},{224... | collective-permute-start | bytes 245768 | tf_op jit(solution)/shard_map/ppermute | solution.py:22
  87.0 6.1 %collective-permute-start.24 = (f32[4,5120]{1,0:T(4,128)S(1)}, f32[4,5120]{1,0:T(4,128)S(1)}, u32[]{:S(2)}, u32[]{:S(2)}) collective-permute-start(f32[4,5120]{1,0:T(4,128)S(1)} %get-tuple-element.53), channel_id=1, source_target_pairs={{0,4},{2,6},{4,0},{6,2},{1,5},{3,7},{5,1},{7,3},{8,12},{10,14},{12... | collective-permute-start | bytes 245768 | tf_op jit(solution)/shard_map/ppermute | solution.py:22
  93.5 2.7 %collective-permute-done.24 = f32[4,5120]{1,0:T(4,128)S(1)} collective-permute-done((f32[4,5120]{1,0:T(4,128)S(1)}, f32[4,5120]{1,0:T(4,128)S(1)}, u32[]{:S(2)}, u32[]{:S(2)}) %collective-permute-start.24) | collective-permute-done | bytes 81952 | tf_op jit(solution)/shard_map/ppermute | solution.py:22
  96.2 3.5 %collective-permute-done.23 = f32[4,5120]{1,0:T(4,128)S(1)} collective-permute-done((f32[4,5120]{1,0:T(4,128)S(1)}, f32[4,5120]{1,0:T(4,128)S(1)}, u32[]{:S(2)}, u32[]{:S(2)}) %collective-permute-start.23) | collective-permute-done | bytes 81952 | tf_op jit(solution)/shard_map/ppermute | solution.py:22
  101.2 5.3 %collective-permute-done.26 = f32[1,4,5120]{2,1,0:T(4,128)S(1)} collective-permute-done((f32[1,4,5120]{2,1,0:T(4,128)S(1)}, f32[1,4,5120]{2,1,0:T(4,128)S(1)}, u32[]{:S(2)}, u32[]{:S(2)}) %collective-permute-start.26) | collective-permute-done | bytes 81952 | tf_op jit(solution)/shard_map/ppermute | solution.py:22
  (78 shorter events, 13.3 us)
Async XLA Ops:
  6.0 32.1 %collective-permute-start = (f32[4,16,5120]{2,1,0:T(8,128)}, f32[4,16,5120]{2,1,0:T(8,128)}, u32[]{:S(2)}, u32[]{:S(2)}) collective-permute-start(f32[4,16,5120]{2,1,0:T(8,128)} %get-tuple-element.10), channel_id=1, source_target_pairs={{0,1},{1,0},{2,3},{3,2},{4,5},{5,4},{6,7},{7,6},{8,9},{9,8},{10,11... | collective-permute-start | bytes 3932168 | tf_op jit(solution)/shard_map/ppermute | solution.py:22
  10.7 31.4 %collective-permute-start.9 = (f32[4,16,5120]{2,1,0:T(8,128)}, f32[4,16,5120]{2,1,0:T(8,128)S(1)}, u32[]{:S(2)}, u32[]{:S(2)}) collective-permute-start(f32[4,16,5120]{2,1,0:T(8,128)} %get-tuple-element.12), channel_id=1, source_target_pairs={{0,1},{1,0},{2,3},{3,2},{4,5},{5,4},{6,7},{7,6},{8,9},{9,8},{10,11... | collective-permute-start | bytes 3932168 | tf_op jit(solution)/shard_map/ppermute | solution.py:22
  17.4 27.1 %collective-permute-start.18 = (f32[4,16,5120]{2,1,0:T(8,128)}, f32[4,16,5120]{2,1,0:T(8,128)S(1)}, u32[]{:S(2)}, u32[]{:S(2)}) collective-permute-start(f32[4,16,5120]{2,1,0:T(8,128)} %get-tuple-element.14), channel_id=1, source_target_pairs={{0,1},{1,0},{2,3},{3,2},{4,5},{5,4},{6,7},{7,6},{8,9},{9,8},{10,11... | collective-permute-start | bytes 3932168 | tf_op jit(solution)/shard_map/ppermute | solution.py:22
  40.0 7.4 %collective-permute-start.1 = (f32[16,2560]{1,0:T(8,128)S(1)}, f32[16,2560]{1,0:T(8,128)S(1)}, u32[]{:S(2)}, u32[]{:S(2)}) collective-permute-start(f32[16,2560]{1,0:T(8,128)S(1)} %get-tuple-element.35), channel_id=1, source_target_pairs={{0,8},{8,16},{16,24},{24,0},{1,9},{9,17},{17,25},{25,1},{2,10},{10... | collective-permute-start | bytes 491528 | tf_op jit(solution)/shard_map/ppermute | solution.py:22
  40.3 7.4 %collective-permute-start.3 = (f32[16,2560]{1,0:T(8,128)S(1)}, f32[16,2560]{1,0:T(8,128)S(1)}, u32[]{:S(2)}, u32[]{:S(2)}) collective-permute-start(f32[16,2560]{1,0:T(8,128)S(1)} %get-tuple-element.36), channel_id=1, source_target_pairs={{0,24},{8,0},{16,8},{24,16},{1,25},{9,1},{17,9},{25,17},{2,26},{10... | collective-permute-start | bytes 491528 | tf_op jit(solution)/shard_map/ppermute | solution.py:22
  42.3 8.2 %collective-permute-start.10 = (f32[16,2560]{1,0:T(8,128)S(1)}, f32[16,2560]{1,0:T(8,128)S(1)}, u32[]{:S(2)}, u32[]{:S(2)}) collective-permute-start(f32[16,2560]{1,0:T(8,128)S(1)} %get-tuple-element.29), channel_id=1, source_target_pairs={{0,8},{8,16},{16,24},{24,0},{1,9},{9,17},{17,25},{25,1},{2,10},{10... | collective-permute-start | bytes 491528 | tf_op jit(solution)/shard_map/ppermute | solution.py:22
  43.8 8.3 %collective-permute-start.12 = (f32[16,2560]{1,0:T(8,128)S(1)}, f32[16,2560]{1,0:T(8,128)S(1)}, u32[]{:S(2)}, u32[]{:S(2)}) collective-permute-start(f32[16,2560]{1,0:T(8,128)S(1)} %get-tuple-element.30), channel_id=1, source_target_pairs={{0,24},{8,0},{16,8},{24,16},{1,25},{9,1},{17,9},{25,17},{2,26},{10... | collective-permute-start | bytes 491528 | tf_op jit(solution)/shard_map/ppermute | solution.py:22
  44.7 9.4 %collective-permute-start.19 = (f32[16,2560]{1,0:T(8,128)S(1)}, f32[16,2560]{1,0:T(8,128)S(1)}, u32[]{:S(2)}, u32[]{:S(2)}) collective-permute-start(f32[16,2560]{1,0:T(8,128)S(1)} %get-tuple-element.41), channel_id=1, source_target_pairs={{0,8},{8,16},{16,24},{24,0},{1,9},{9,17},{17,25},{25,1},{2,10},{10... | collective-permute-start | bytes 491528 | tf_op jit(solution)/shard_map/ppermute | solution.py:22
  47.4 8.3 %collective-permute-start.21 = (f32[16,2560]{1,0:T(8,128)S(1)}, f32[16,2560]{1,0:T(8,128)S(1)}, u32[]{:S(2)}, u32[]{:S(2)}) collective-permute-start(f32[16,2560]{1,0:T(8,128)S(1)} %get-tuple-element.42), channel_id=1, source_target_pairs={{0,24},{8,0},{16,8},{24,16},{1,25},{9,1},{17,9},{25,17},{2,26},{10... | collective-permute-start | bytes 491528 | tf_op jit(solution)/shard_map/ppermute | solution.py:22
  47.7 15.0 %collective-permute-start.4 = (f32[16,5120]{1,0:T(8,128)S(1)}, f32[16,5120]{1,0:T(8,128)S(1)}, u32[]{:S(2)}, u32[]{:S(2)}) collective-permute-start(f32[16,5120]{1,0:T(8,128)S(1)} %pad_maximum_fusion.1), channel_id=1, source_target_pairs={{0,24},{8,0},{16,8},{24,16},{1,25},{9,1},{17,9},{25,17},{2,26},{10... | collective-permute-start | bytes 983048 | tf_op jit(solution)/shard_map/ppermute | solution.py:22
  50.6 12.1 %collective-permute-start.2 = (f32[16,5120]{1,0:T(8,128)S(1)}, f32[16,5120]{1,0:T(8,128)S(1)}, u32[]{:S(2)}, u32[]{:S(2)}) collective-permute-start(f32[16,5120]{1,0:T(8,128)S(1)} %pad_maximum_fusion), channel_id=1, source_target_pairs={{0,8},{8,16},{16,24},{24,0},{1,9},{9,17},{17,25},{25,1},{2,10},{10... | collective-permute-start | bytes 983048 | tf_op jit(solution)/shard_map/ppermute | solution.py:22
  52.3 17.5 %collective-permute-start.13 = (f32[16,5120]{1,0:T(8,128)S(1)}, f32[16,5120]{1,0:T(8,128)S(1)}, u32[]{:S(2)}, u32[]{:S(2)}) collective-permute-start(f32[16,5120]{1,0:T(8,128)S(1)} %pad_maximum_fusion.3), channel_id=1, source_target_pairs={{0,24},{8,0},{16,8},{24,16},{1,25},{9,1},{17,9},{25,17},{2,26},{10... | collective-permute-start | bytes 983048 | tf_op jit(solution)/shard_map/ppermute | solution.py:22
  54.1 21.9 %collective-permute-start.11 = (f32[16,5120]{1,0:T(8,128)S(1)}, f32[16,5120]{1,0:T(8,128)S(1)}, u32[]{:S(2)}, u32[]{:S(2)}) collective-permute-start(f32[16,5120]{1,0:T(8,128)S(1)} %pad_maximum_fusion.2), channel_id=1, source_target_pairs={{0,8},{8,16},{16,24},{24,0},{1,9},{9,17},{17,25},{25,1},{2,10},{10... | collective-permute-start | bytes 983048 | tf_op jit(solution)/shard_map/ppermute | solution.py:22
  55.8 21.8 %collective-permute-start.22 = (f32[16,5120]{1,0:T(8,128)S(1)}, f32[16,5120]{1,0:T(8,128)S(1)}, u32[]{:S(2)}, u32[]{:S(2)}) collective-permute-start(f32[16,5120]{1,0:T(8,128)S(1)} %pad_maximum_fusion.5), channel_id=1, source_target_pairs={{0,24},{8,0},{16,8},{24,16},{1,25},{9,1},{17,9},{25,17},{2,26},{10... | collective-permute-start | bytes 983048 | tf_op jit(solution)/shard_map/ppermute | solution.py:22
  62.7 17.7 %collective-permute-start.20 = (f32[16,5120]{1,0:T(8,128)S(1)}, f32[16,5120]{1,0:T(8,128)S(1)}, u32[]{:S(2)}, u32[]{:S(2)}) collective-permute-start(f32[16,5120]{1,0:T(8,128)S(1)} %pad_maximum_fusion.4), channel_id=1, source_target_pairs={{0,8},{8,16},{16,24},{24,0},{1,9},{9,17},{17,25},{25,1},{2,10},{10... | collective-permute-start | bytes 983048 | tf_op jit(solution)/shard_map/ppermute | solution.py:22
  62.9 18.5 %collective-permute-start.7 = (f32[4,5120]{1,0:T(4,128)S(1)}, f32[4,5120]{1,0:T(4,128)S(1)}, u32[]{:S(2)}, u32[]{:S(2)}) collective-permute-start(f32[4,5120]{1,0:T(4,128)S(1)} %get-tuple-element.49), channel_id=1, source_target_pairs={{0,6},{2,0},{4,2},{6,4},{1,7},{3,1},{5,3},{7,5},{8,14},{10,8},{12,... | collective-permute-start | bytes 245768 | tf_op jit(solution)/shard_map/ppermute | solution.py:22
  69.8 13.2 %collective-permute-start.6 = (f32[4,5120]{1,0:T(4,128)S(1)}, f32[4,5120]{1,0:T(4,128)S(1)}, u32[]{:S(2)}, u32[]{:S(2)}) collective-permute-start(f32[4,5120]{1,0:T(4,128)S(1)} %get-tuple-element.50), channel_id=1, source_target_pairs={{0,4},{2,6},{4,0},{6,2},{1,5},{3,7},{5,1},{7,3},{8,12},{10,14},{12... | collective-permute-start | bytes 245768 | tf_op jit(solution)/shard_map/ppermute | solution.py:22
  76.0 8.3 %collective-permute-start.5 = (f32[4,5120]{1,0:T(4,128)S(1)}, f32[4,5120]{1,0:T(4,128)S(1)}, u32[]{:S(2)}, u32[]{:S(2)}) collective-permute-start(f32[4,5120]{1,0:T(4,128)S(1)} %get-tuple-element.48), channel_id=1, source_target_pairs={{0,2},{2,4},{4,6},{6,0},{1,3},{3,5},{5,7},{7,1},{8,10},{10,12},{12... | collective-permute-start | bytes 245768 | tf_op jit(solution)/shard_map/ppermute | solution.py:22
  77.6 9.3 %collective-permute-start.16 = (f32[4,5120]{1,0:T(4,128)S(1)}, f32[4,5120]{1,0:T(4,128)S(1)}, u32[]{:S(2)}, u32[]{:S(2)}) collective-permute-start(f32[4,5120]{1,0:T(4,128)S(1)} %get-tuple-element.46), channel_id=1, source_target_pairs={{0,6},{2,0},{4,2},{6,4},{1,7},{3,1},{5,3},{7,5},{8,14},{10,8},{12,... | collective-permute-start | bytes 245768 | tf_op jit(solution)/shard_map/ppermute | solution.py:22
  80.4 12.7 %collective-permute-start.15 = (f32[4,5120]{1,0:T(4,128)S(1)}, f32[4,5120]{1,0:T(4,128)S(1)}, u32[]{:S(2)}, u32[]{:S(2)}) collective-permute-start(f32[4,5120]{1,0:T(4,128)S(1)} %get-tuple-element.47), channel_id=1, source_target_pairs={{0,4},{2,6},{4,0},{6,2},{1,5},{3,7},{5,1},{7,3},{8,12},{10,14},{12... | collective-permute-start | bytes 245768 | tf_op jit(solution)/shard_map/ppermute | solution.py:22
  81.4 11.8 %collective-permute-start.14 = (f32[4,5120]{1,0:T(4,128)S(1)}, f32[4,5120]{1,0:T(4,128)S(1)}, u32[]{:S(2)}, u32[]{:S(2)}) collective-permute-start(f32[4,5120]{1,0:T(4,128)S(1)} %get-tuple-element.45), channel_id=1, source_target_pairs={{0,2},{2,4},{4,6},{6,0},{1,3},{3,5},{5,7},{7,1},{8,10},{10,12},{12... | collective-permute-start | bytes 245768 | tf_op jit(solution)/shard_map/ppermute | solution.py:22
  84.5 8.7 %collective-permute-start.8 = (f32[1,4,5120]{2,1,0:T(4,128)S(1)}, f32[1,4,5120]{2,1,0:T(4,128)S(1)}, u32[]{:S(2)}, u32[]{:S(2)}) collective-permute-start(f32[1,4,5120]{2,1,0:T(4,128)S(1)} %get-tuple-element.25), channel_id=1, source_target_pairs={{0,32},{32,64},{64,96},{96,128},{128,160},{160,192},{192,224},{224... | collective-permute-start | bytes 245768 | tf_op jit(solution)/shard_map/ppermute | solution.py:22
  86.6 6.9 %collective-permute-start.25 = (f32[4,5120]{1,0:T(4,128)S(1)}, f32[4,5120]{1,0:T(4,128)S(1)}, u32[]{:S(2)}, u32[]{:S(2)}) collective-permute-start(f32[4,5120]{1,0:T(4,128)S(1)} %get-tuple-element.52), channel_id=1, source_target_pairs={{0,6},{2,0},{4,2},{6,4},{1,7},{3,1},{5,3},{7,5},{8,14},{10,8},{12,... | collective-permute-start | bytes 245768 | tf_op jit(solution)/shard_map/ppermute | solution.py:22
  87.0 9.2 %collective-permute-start.24 = (f32[4,5120]{1,0:T(4,128)S(1)}, f32[4,5120]{1,0:T(4,128)S(1)}, u32[]{:S(2)}, u32[]{:S(2)}) collective-permute-start(f32[4,5120]{1,0:T(4,128)S(1)} %get-tuple-element.53), channel_id=1, source_target_pairs={{0,4},{2,6},{4,0},{6,2},{1,5},{3,7},{5,1},{7,3},{8,12},{10,14},{12... | collective-permute-start | bytes 245768 | tf_op jit(solution)/shard_map/ppermute | solution.py:22
  (7 other events, 40.0 us)

commit v2 on v1

v2 whole, which is shorter than its diff:
```python
import functools

import jax
import jax.numpy as jnp
from jax import lax
from jax.experimental import pallas as pl
from jax.experimental.pallas import tpu as pltpu
from jax.sharding import Mesh, PartitionSpec as P

STEPS = 3
ROWS = 128
D = 5120
HALF = D // 2
STRIP = 1024
X, ZL, Y, ZH, CORE = 4, 2, 4, 4, 2
GROUP = ("x", "zl")
SHARD = ("y", "zh", "core")

learn_rate = 0.5
momentum_factor = 0.9


def ring(x, axis, by):
    n = lax.axis_size(axis)
    return lax.ppermute(x, axis, [(i, (i + by) % n) for i in range(n)])


def split_kernel(step, g_ref, other_ref, own_ref, block, arrived):
    me, core = lax.axis_index("y"), lax.axis_index("core")
    copies = {}
    for r in (2, 1, 3, 0):
        first_row = pl.multiple_of(32 * lax.rem(me + r, Y), 32)
        copies[r] = pltpu.make_async_copy(
            g_ref.at[step, 0, 0, pl.ds(first_row, 32), :], block.at[r], arrived.at[r]
        )
        copies[r].start()
    row = lax.broadcasted_iota(jnp.int32, (8, STRIP), 0)
    for r in (2, 1, 3, 0):
        copies[r].wait()
        for m in range(2):
            for at in range(0, D, STRIP):
                columns = slice(at, at + STRIP)
                low = block[r, 16 * m : 16 * m + 8, columns]
                high = block[r, 16 * m + 8 : 16 * m + 16, columns]
                first = jnp.where(row < 4, low, pltpu.roll(high, 4, 0))
                second = jnp.where(row < 4, pltpu.roll(low, 4, 0), high)
                own_ref[r, 8 * m : 8 * m + 8, columns] = jnp.where(core == 0, first, second)
                other_ref[r, 8 * m : 8 * m + 8, columns] = jnp.where(core == 0, second, first)


def split_cores(grads, step):
    shape = pltpu.VMEM((Y, 16, D), jnp.float32)
    return pl.pallas_call(
        functools.partial(split_kernel, step),
        out_shape=(shape, shape),
        in_specs=[pl.BlockSpec(memory_space=pltpu.HBM)],
        out_specs=[pl.BlockSpec(memory_space=pltpu.VMEM)] * 2,
        scratch_shapes=[pltpu.VMEM((Y, 32, D), jnp.float32), pltpu.SemaphoreType.DMA((Y,))],
        compiler_params=pltpu.CompilerParams(vmem_limit_bytes=16 << 20),
        cost_estimate=pl.CostEstimate(flops=0, bytes_accessed=2 * ROWS * D * 4, transcendentals=0),
    )(grads)


def shard_mean(grads, step):
    zh = lax.axis_index("zh")
    other, own = split_cores(grads, step)
    part = own + ring(other, "core", 1)
    from_low = ring(part[2, :, :HALF], "y", 1)
    from_high = ring(part[2, :, HALF:], "y", -1)
    up = jnp.concatenate([part[1, :, :HALF] + from_low, part[1, :, HALF:]], axis=1)
    down = jnp.concatenate([part[3, :, :HALF], part[3, :, HALF:] + from_high], axis=1)
    total = part[0] + ring(up, "y", 1) + ring(down, "y", -1)
    rows = [
        lax.dynamic_slice_in_dim(total, 4 * ((zh + k) % ZH), 4, 0) for k in range(ZH)
    ]
    out = rows[0]
    for k in range(1, ZH):
        out = out + ring(rows[k], "zh", k)
    return (out / (Y * ZH * CORE))[None]


def per_device(numerators, push_weight, keep_share, momentum, grads):
    levels = (X * ZL).bit_length() - 1
    means = [shard_mean(grads, step) for step in range(STEPS)]
    weight = jnp.broadcast_to(push_weight[:, None, None], (1, 4, 128))
    values = jnp.concatenate([numerators, weight], axis=2)
    buffer = momentum
    keep_rows = keep_share[:, None, None]
    for step in range(STEPS):
        mean = means[step]
        buffer = momentum_factor * buffer + mean
        moved = learn_rate * (mean + momentum_factor * buffer)
        values = values - jnp.pad(moved, ((0, 0), (0, 0), (0, 128)))
        sent = ring((1.0 - keep_rows) * values, GROUP, 1 << step % levels)
        values = keep_rows * values + sent
    weight = values[:, 0, D]
    displacement = values[:, :, :D] / weight[:, None, None] - numerators / push_weight[:, None, None]
    return (displacement, buffer, weight)


def solution(mesh):
    fine = Mesh(mesh.devices.reshape(X, ZL, Y, ZH, CORE), GROUP + SHARD)
    in_specs = (
        P(GROUP, SHARD, None),
        P(GROUP),
        P(GROUP),
        P(GROUP, SHARD, None),
        P(None, GROUP, SHARD, None, None),
    )
    out_specs = (P(GROUP, SHARD, None), P(GROUP, SHARD, None), P(GROUP))
    return jax.shard_map(
        per_device, mesh=fine, in_specs=in_specs, out_specs=out_specs, check_vma=False
    )
```

time: 108 us -> 91.4 us (0.85)
  blocking collectives: 19.1 us -> 0 us
  Pallas kernels: 14.3 us -> 6.76 us
  waiting for transfers between devices: 24.3 us -> 27.2 us
  starting transfers between devices: 39.8 us -> 42.6 us
  local copies, waits for them, and re-layouts: 1.71 us -> 4.06 us
  other arithmetic: 6.43 us -> 7.57 us
    all_gather x1 -> x0, blocking collectives: 19.1 us -> none  [group_weights(): lax.all_gather(jnp.stack([push_weight, keep_share], axis=1), GROUP, axis=...]
    pallas_call x3, Pallas kernels: 14.3 us -> 6.76 us  [split_cores(): pl.pallas_call(functools.partial(split_kernel, step), out_shape=(shape, s...]
    unnamed x8, local copies, waits for them, and re-layouts: 0.02 us -> 3.24 us
    ppermute x27, waiting for transfers between devices: 24.3 us -> 27.2 us  [ring(): return lax.ppermute(x, axis, [(i, (i + by) % n) for i in range(n)])]
    ppermute x27, starting transfers between devices: 39.8 us -> 42.6 us  [ring(): return lax.ppermute(x, axis, [(i, (i + by) % n) for i in range(n)])]
    add x3, other arithmetic: 2.22 us -> 4.75 us  [shard_mean(): part = own + ring(other, 'core', 1)]
  transfers between devices with their start and end apart: 27 -> 27, of which waited for: 10 -> 7; matrix products, arithmetic and copies ran while one was open for 5% -> 7% of each run, Pallas kernels for 9% -> 5%
where the time goes in v2:
time: 91.4 us; the launch traced here: 90.6 us
  starting transfers between devices  42.6 us (47%)
  waiting for transfers between devices  27.2 us (30%)
  other arithmetic  7.57 us (8%)
  Pallas kernels  6.76 us (7%)
  local copies, waits for them, and re-layouts  4.06 us (4%)
  between operations  2.32 us (3%)
    ppermute x27, starting transfers between devices, ring(): return lax.ppermute(x, axis, [(i, (i + by) % n) for i in range(n)])  42.6 us
    ppermute x27, waiting for transfers between devices, ring(): return lax.ppermute(x, axis, [(i, (i + by) % n) for i in range(n)])  27.2 us
    pallas_call x3, Pallas kernels, split_cores(): pl.pallas_call(functools.partial(split_kernel, step), out_shape=(shape, s...  6.76 us
    add x3, other arithmetic, shard_mean(): part = own + ring(other, 'core', 1)  4.75 us
    unnamed x8, local copies, waits for them, and re-layouts  3.24 us
  transfers between devices with their start and end apart: 27, of which 7 were waited for; matrix products, arithmetic and copies ran while one was open for 7% of the time, Pallas kernels for 5%

profile of v2, /device:TPU:24, one launch (start us, length us, event | category | flops | bytes accessed | tf_op | source)
XLA Modules:
  0.0 90.6 jit_solution(2700725674655750841)
XLA Ops:
  0.6 3.2 %copy-done = f32[3,1,1,128,5120]{4,3,2,1,0:T(8,128)S(1)} copy-done((f32[3,1,1,128,5120]{4,3,2,1,0:T(8,128)S(1)}, f32[3,1,1,128,5120]{4,3,2,1,0:T(8,128)}, u32[]{:S(2)}) %copy-start) | copy-done | bytes 7864344
  3.9 2.3 %shard_map.76 = (f32[4,16,5120]{2,1,0:T(8,128)}, f32[4,16,5120]{2,1,0:T(8,128)S(1)}) custom-call(f32[3,1,1,128,5120]{4,3,2,1,0:T(8,128)S(1)} %copy-done), custom_call_target="tpu_custom_call" | custom-call | bytes 5242880 | tf_op jit(solution)/shard_map/pallas_call | solution.py:53
  6.2 2.3 %shard_map.77 = (f32[4,16,5120]{2,1,0:T(8,128)}, f32[4,16,5120]{2,1,0:T(8,128)S(1)}) custom-call(f32[3,1,1,128,5120]{4,3,2,1,0:T(8,128)S(1)} %copy-done), custom_call_target="tpu_custom_call" | custom-call | bytes 5242880 | tf_op jit(solution)/shard_map/pallas_call | solution.py:53
  9.1 2.2 %shard_map.78 = (f32[4,16,5120]{2,1,0:T(8,128)}, f32[4,16,5120]{2,1,0:T(8,128)S(1)}) custom-call(f32[3,1,1,128,5120]{4,3,2,1,0:T(8,128)S(1)} %copy-done), custom_call_target="tpu_custom_call" | custom-call | bytes 5242880 | tf_op jit(solution)/shard_map/pallas_call | solution.py:53
  12.8 1.8 %add.163 = f32[4,16,5120]{2,1,0:T(8,128)S(1)} add(f32[4,16,5120]{2,1,0:T(8,128)} %copy-done.1, f32[4,16,5120]{2,1,0:T(8,128)} %collective-permute-done) | non-fusion elementwise | flops 327680 | bytes 3932160 | tf_op jit(solution)/shard_map/add | solution.py:67
  14.7 2.0 %collective-permute-start.1 = (f32[16,2560]{1,0:T(8,128)S(1)}, f32[16,2560]{1,0:T(8,128)S(1)}, u32[]{:S(2)}, u32[]{:S(2)}) collective-permute-start(f32[16,2560]{1,0:T(8,128)S(1)} %get-tuple-element.31), channel_id=1, source_target_pairs={{0,8},{8,16},{16,24},{24,0},{1,9},{9,17},{17,25},{25,1},{2,10},{10... | collective-permute-start | bytes 491528 | tf_op jit(solution)/shard_map/ppermute | solution.py:25
  16.8 1.5 %add.185 = f32[4,16,5120]{2,1,0:T(8,128)S(1)} add(f32[4,16,5120]{2,1,0:T(8,128)S(1)} %get-tuple-element.11, f32[4,16,5120]{2,1,0:T(8,128)} %collective-permute-done.9) | non-fusion elementwise | flops 327680 | bytes 3932160 | tf_op jit(solution)/shard_map/add | solution.py:67
  18.3 3.2 %collective-permute-start.10 = (f32[16,2560]{1,0:T(8,128)S(1)}, f32[16,2560]{1,0:T(8,128)S(1)}, u32[]{:S(2)}, u32[]{:S(2)}) collective-permute-start(f32[16,2560]{1,0:T(8,128)S(1)} %get-tuple-element.25), channel_id=1, source_target_pairs={{0,8},{8,16},{16,24},{24,0},{1,9},{9,17},{17,25},{25,1},{2,10},{10... | collective-permute-start | bytes 491528 | tf_op jit(solution)/shard_map/ppermute | solution.py:25
  21.6 1.5 %add.196 = f32[4,16,5120]{2,1,0:T(8,128)S(1)} add(f32[4,16,5120]{2,1,0:T(8,128)S(1)} %get-tuple-element.13, f32[4,16,5120]{2,1,0:T(8,128)} %collective-permute-done.18) | non-fusion elementwise | flops 327680 | bytes 3932160 | tf_op jit(solution)/shard_map/add | solution.py:67
  23.1 3.3 %collective-permute-start.19 = (f32[16,2560]{1,0:T(8,128)S(1)}, f32[16,2560]{1,0:T(8,128)S(1)}, u32[]{:S(2)}, u32[]{:S(2)}) collective-permute-start(f32[16,2560]{1,0:T(8,128)S(1)} %get-tuple-element.37), channel_id=1, source_target_pairs={{0,8},{8,16},{16,24},{24,0},{1,9},{9,17},{17,25},{25,1},{2,10},{10... | collective-permute-start | bytes 491528 | tf_op jit(solution)/shard_map/ppermute | solution.py:25
  26.6 3.3 %collective-permute-start.2 = (f32[16,5120]{1,0:T(8,128)S(1)}, f32[16,5120]{1,0:T(8,128)S(1)}, u32[]{:S(2)}, u32[]{:S(2)}) collective-permute-start(f32[16,5120]{1,0:T(8,128)S(1)} %pad_maximum_fusion), channel_id=1, source_target_pairs={{0,8},{8,16},{16,24},{24,0},{1,9},{9,17},{17,25},{25,1},{2,10},{10... | collective-permute-start | bytes 983048 | tf_op jit(solution)/shard_map/ppermute | solution.py:25
  30.1 3.4 %collective-permute-start.11 = (f32[16,5120]{1,0:T(8,128)S(1)}, f32[16,5120]{1,0:T(8,128)S(1)}, u32[]{:S(2)}, u32[]{:S(2)}) collective-permute-start(f32[16,5120]{1,0:T(8,128)S(1)} %pad_maximum_fusion.2), channel_id=1, source_target_pairs={{0,8},{8,16},{16,24},{24,0},{1,9},{9,17},{17,25},{25,1},{2,10},{10... | collective-permute-start | bytes 983048 | tf_op jit(solution)/shard_map/ppermute | solution.py:25
  35.1 6.6 %collective-permute-done.4 = f32[16,5120]{1,0:T(8,128)S(1)} collective-permute-done((f32[16,5120]{1,0:T(8,128)S(1)}, f32[16,5120]{1,0:T(8,128)S(1)}, u32[]{:S(2)}, u32[]{:S(2)}) %collective-permute-start.4) | collective-permute-done | bytes 327712 | tf_op jit(solution)/shard_map/ppermute | solution.py:25
  41.9 4.6 %collective-permute-start.7 = (f32[4,5120]{1,0:T(4,128)S(1)}, f32[4,5120]{1,0:T(4,128)S(1)}, u32[]{:S(2)}, u32[]{:S(2)}) collective-permute-start(f32[4,5120]{1,0:T(4,128)S(1)} %get-tuple-element.45), channel_id=1, source_target_pairs={{0,6},{2,0},{4,2},{6,4},{1,7},{3,1},{5,3},{7,5},{8,14},{10,8},{12,... | collective-permute-start | bytes 245768 | tf_op jit(solution)/shard_map/ppermute | solution.py:25
  46.5 2.2 %collective-permute-done.13 = f32[16,5120]{1,0:T(8,128)S(1)} collective-permute-done((f32[16,5120]{1,0:T(8,128)S(1)}, f32[16,5120]{1,0:T(8,128)S(1)}, u32[]{:S(2)}, u32[]{:S(2)}) %collective-permute-start.13) | collective-permute-done | bytes 327712 | tf_op jit(solution)/shard_map/ppermute | solution.py:25
  48.8 5.5 %collective-permute-start.6 = (f32[4,5120]{1,0:T(4,128)S(1)}, f32[4,5120]{1,0:T(4,128)S(1)}, u32[]{:S(2)}, u32[]{:S(2)}) collective-permute-start(f32[4,5120]{1,0:T(4,128)S(1)} %get-tuple-element.46), channel_id=1, source_target_pairs={{0,4},{2,6},{4,0},{6,2},{1,5},{3,7},{5,1},{7,3},{8,12},{10,14},{12... | collective-permute-start | bytes 245768 | tf_op jit(solution)/shard_map/ppermute | solution.py:25
  54.2 1.5 %collective-permute-start.5 = (f32[4,5120]{1,0:T(4,128)S(1)}, f32[4,5120]{1,0:T(4,128)S(1)}, u32[]{:S(2)}, u32[]{:S(2)}) collective-permute-start(f32[4,5120]{1,0:T(4,128)S(1)} %get-tuple-element.44), channel_id=1, source_target_pairs={{0,2},{2,4},{4,6},{6,0},{1,3},{3,5},{5,7},{7,1},{8,10},{10,12},{12... | collective-permute-start | bytes 245768 | tf_op jit(solution)/shard_map/ppermute | solution.py:25
  55.9 2.7 %collective-permute-start.16 = (f32[4,5120]{1,0:T(4,128)S(1)}, f32[4,5120]{1,0:T(4,128)S(1)}, u32[]{:S(2)}, u32[]{:S(2)}) collective-permute-start(f32[4,5120]{1,0:T(4,128)S(1)} %get-tuple-element.42), channel_id=1, source_target_pairs={{0,6},{2,0},{4,2},{6,4},{1,7},{3,1},{5,3},{7,5},{8,14},{10,8},{12,... | collective-permute-start | bytes 245768 | tf_op jit(solution)/shard_map/ppermute | solution.py:25
  59.7 2.9 %collective-permute-start.14 = (f32[4,5120]{1,0:T(4,128)S(1)}, f32[4,5120]{1,0:T(4,128)S(1)}, u32[]{:S(2)}, u32[]{:S(2)}) collective-permute-start(f32[4,5120]{1,0:T(4,128)S(1)} %get-tuple-element.41), channel_id=1, source_target_pairs={{0,2},{2,4},{4,6},{6,0},{1,3},{3,5},{5,7},{7,1},{8,10},{10,12},{12... | collective-permute-start | bytes 245768 | tf_op jit(solution)/shard_map/ppermute | solution.py:25
  62.6 1.3 %collective-permute-start.25 = (f32[4,5120]{1,0:T(4,128)S(1)}, f32[4,5120]{1,0:T(4,128)S(1)}, u32[]{:S(2)}, u32[]{:S(2)}) collective-permute-start(f32[4,5120]{1,0:T(4,128)S(1)} %get-tuple-element.48), channel_id=1, source_target_pairs={{0,6},{2,0},{4,2},{6,4},{1,7},{3,1},{5,3},{7,5},{8,14},{10,8},{12,... | collective-permute-start | bytes 245768 | tf_op jit(solution)/shard_map/ppermute | solution.py:25
  63.9 5.0 %collective-permute-start.24 = (f32[4,5120]{1,0:T(4,128)S(1)}, f32[4,5120]{1,0:T(4,128)S(1)}, u32[]{:S(2)}, u32[]{:S(2)}) collective-permute-start(f32[4,5120]{1,0:T(4,128)S(1)} %get-tuple-element.49), channel_id=1, source_target_pairs={{0,4},{2,6},{4,0},{6,2},{1,5},{3,7},{5,1},{7,3},{8,12},{10,14},{12... | collective-permute-start | bytes 245768 | tf_op jit(solution)/shard_map/ppermute | solution.py:25
  70.3 6.5 %collective-permute-done.8 = f32[1,4,5248]{2,1,0:T(4,128)S(1)} collective-permute-done((f32[1,4,5248]{2,1,0:T(4,128)S(1)}, f32[1,4,5248]{2,1,0:T(4,128)S(1)}, u32[]{:S(2)}, u32[]{:S(2)}) %collective-permute-start.8) | collective-permute-done | bytes 84000 | tf_op jit(solution)/shard_map/ppermute | solution.py:25
  77.9 4.7 %collective-permute-done.17 = f32[1,4,5248]{2,1,0:T(4,128)S(1)} collective-permute-done((f32[1,4,5248]{2,1,0:T(4,128)S(1)}, f32[1,4,5248]{2,1,0:T(4,128)S(1)}, u32[]{:S(2)}, u32[]{:S(2)}) %collective-permute-start.17) | collective-permute-done | bytes 84000 | tf_op jit(solution)/shard_map/ppermute | solution.py:25
  83.0 5.7 %collective-permute-done.26 = f32[1,4,5248]{2,1,0:T(4,128)S(1)} collective-permute-done((f32[1,4,5248]{2,1,0:T(4,128)S(1)}, f32[1,4,5248]{2,1,0:T(4,128)S(1)}, u32[]{:S(2)}, u32[]{:S(2)}) %collective-permute-start.26) | collective-permute-done | bytes 84000 | tf_op jit(solution)/shard_map/ppermute | solution.py:25
  (71 shorter events, 8.9 us)
Async XLA Ops:
  8.5 8.3 %collective-permute-start.9 = (f32[4,16,5120]{2,1,0:T(8,128)}, f32[4,16,5120]{2,1,0:T(8,128)}, u32[]{:S(2)}, u32[]{:S(2)}) collective-permute-start(f32[4,16,5120]{2,1,0:T(8,128)} %get-tuple-element.12), channel_id=1, source_target_pairs={{0,1},{1,0},{2,3},{3,2},{4,5},{5,4},{6,7},{7,6},{8,9},{9,8},{10,11... | collective-permute-start | bytes 3932168 | tf_op jit(solution)/shard_map/ppermute | solution.py:25
  11.3 10.2 %collective-permute-start.18 = (f32[4,16,5120]{2,1,0:T(8,128)}, f32[4,16,5120]{2,1,0:T(8,128)}, u32[]{:S(2)}, u32[]{:S(2)}) collective-permute-start(f32[4,16,5120]{2,1,0:T(8,128)} %get-tuple-element.14), channel_id=1, source_target_pairs={{0,1},{1,0},{2,3},{3,2},{4,5},{5,4},{6,7},{7,6},{8,9},{9,8},{10,11... | collective-permute-start | bytes 3932168 | tf_op jit(solution)/shard_map/ppermute | solution.py:25
  14.7 11.7 %collective-permute-start.1 = (f32[16,2560]{1,0:T(8,128)S(1)}, f32[16,2560]{1,0:T(8,128)S(1)}, u32[]{:S(2)}, u32[]{:S(2)}) collective-permute-start(f32[16,2560]{1,0:T(8,128)S(1)} %get-tuple-element.31), channel_id=1, source_target_pairs={{0,8},{8,16},{16,24},{24,0},{1,9},{9,17},{17,25},{25,1},{2,10},{10... | collective-permute-start | bytes 491528 | tf_op jit(solution)/shard_map/ppermute | solution.py:25
  16.7 9.7 %collective-permute-start.3 = (f32[16,2560]{1,0:T(8,128)S(1)}, f32[16,2560]{1,0:T(8,128)S(1)}, u32[]{:S(2)}, u32[]{:S(2)}) collective-permute-start(f32[16,2560]{1,0:T(8,128)S(1)} %get-tuple-element.32), channel_id=1, source_target_pairs={{0,24},{8,0},{16,8},{24,16},{1,25},{9,1},{17,9},{25,17},{2,26},{10... | collective-permute-start | bytes 491528 | tf_op jit(solution)/shard_map/ppermute | solution.py:25
  18.3 8.3 %collective-permute-start.10 = (f32[16,2560]{1,0:T(8,128)S(1)}, f32[16,2560]{1,0:T(8,128)S(1)}, u32[]{:S(2)}, u32[]{:S(2)}) collective-permute-start(f32[16,2560]{1,0:T(8,128)S(1)} %get-tuple-element.25), channel_id=1, source_target_pairs={{0,8},{8,16},{16,24},{24,0},{1,9},{9,17},{17,25},{25,1},{2,10},{10... | collective-permute-start | bytes 491528 | tf_op jit(solution)/shard_map/ppermute | solution.py:25
  21.6 8.4 %collective-permute-start.12 = (f32[16,2560]{1,0:T(8,128)S(1)}, f32[16,2560]{1,0:T(8,128)S(1)}, u32[]{:S(2)}, u32[]{:S(2)}) collective-permute-start(f32[16,2560]{1,0:T(8,128)S(1)} %get-tuple-element.26), channel_id=1, source_target_pairs={{0,24},{8,0},{16,8},{24,16},{1,25},{9,1},{17,9},{25,17},{2,26},{10... | collective-permute-start | bytes 491528 | tf_op jit(solution)/shard_map/ppermute | solution.py:25
  23.1 7.0 %collective-permute-start.19 = (f32[16,2560]{1,0:T(8,128)S(1)}, f32[16,2560]{1,0:T(8,128)S(1)}, u32[]{:S(2)}, u32[]{:S(2)}) collective-permute-start(f32[16,2560]{1,0:T(8,128)S(1)} %get-tuple-element.37), channel_id=1, source_target_pairs={{0,8},{8,16},{16,24},{24,0},{1,9},{9,17},{17,25},{25,1},{2,10},{10... | collective-permute-start | bytes 491528 | tf_op jit(solution)/shard_map/ppermute | solution.py:25
  26.4 8.3 %collective-permute-start.21 = (f32[16,2560]{1,0:T(8,128)S(1)}, f32[16,2560]{1,0:T(8,128)S(1)}, u32[]{:S(2)}, u32[]{:S(2)}) collective-permute-start(f32[16,2560]{1,0:T(8,128)S(1)} %get-tuple-element.38), channel_id=1, source_target_pairs={{0,24},{8,0},{16,8},{24,16},{1,25},{9,1},{17,9},{25,17},{2,26},{10... | collective-permute-start | bytes 491528 | tf_op jit(solution)/shard_map/ppermute | solution.py:25
  26.5 15.3 %collective-permute-start.4 = (f32[16,5120]{1,0:T(8,128)S(1)}, f32[16,5120]{1,0:T(8,128)S(1)}, u32[]{:S(2)}, u32[]{:S(2)}) collective-permute-start(f32[16,5120]{1,0:T(8,128)S(1)} %pad_maximum_fusion.1), channel_id=1, source_target_pairs={{0,24},{8,0},{16,8},{24,16},{1,25},{9,1},{17,9},{25,17},{2,26},{10... | collective-permute-start | bytes 983048 | tf_op jit(solution)/shard_map/ppermute | solution.py:25
  26.6 15.2 %collective-permute-start.2 = (f32[16,5120]{1,0:T(8,128)S(1)}, f32[16,5120]{1,0:T(8,128)S(1)}, u32[]{:S(2)}, u32[]{:S(2)}) collective-permute-start(f32[16,5120]{1,0:T(8,128)S(1)} %pad_maximum_fusion), channel_id=1, source_target_pairs={{0,8},{8,16},{16,24},{24,0},{1,9},{9,17},{17,25},{25,1},{2,10},{10... | collective-permute-start | bytes 983048 | tf_op jit(solution)/shard_map/ppermute | solution.py:25
  30.0 18.8 %collective-permute-start.13 = (f32[16,5120]{1,0:T(8,128)S(1)}, f32[16,5120]{1,0:T(8,128)S(1)}, u32[]{:S(2)}, u32[]{:S(2)}) collective-permute-start(f32[16,5120]{1,0:T(8,128)S(1)} %pad_maximum_fusion.3), channel_id=1, source_target_pairs={{0,24},{8,0},{16,8},{24,16},{1,25},{9,1},{17,9},{25,17},{2,26},{10... | collective-permute-start | bytes 983048 | tf_op jit(solution)/shard_map/ppermute | solution.py:25
  30.1 24.1 %collective-permute-start.11 = (f32[16,5120]{1,0:T(8,128)S(1)}, f32[16,5120]{1,0:T(8,128)S(1)}, u32[]{:S(2)}, u32[]{:S(2)}) collective-permute-start(f32[16,5120]{1,0:T(8,128)S(1)} %pad_maximum_fusion.2), channel_id=1, source_target_pairs={{0,8},{8,16},{16,24},{24,0},{1,9},{9,17},{17,25},{25,1},{2,10},{10... | collective-permute-start | bytes 983048 | tf_op jit(solution)/shard_map/ppermute | solution.py:25
  34.8 21.1 %collective-permute-start.22 = (f32[16,5120]{1,0:T(8,128)S(1)}, f32[16,5120]{1,0:T(8,128)S(1)}, u32[]{:S(2)}, u32[]{:S(2)}) collective-permute-start(f32[16,5120]{1,0:T(8,128)S(1)} %pad_maximum_fusion.5), channel_id=1, source_target_pairs={{0,24},{8,0},{16,8},{24,16},{1,25},{9,1},{17,9},{25,17},{2,26},{10... | collective-permute-start | bytes 983048 | tf_op jit(solution)/shard_map/ppermute | solution.py:25
  41.8 16.9 %collective-permute-start.20 = (f32[16,5120]{1,0:T(8,128)S(1)}, f32[16,5120]{1,0:T(8,128)S(1)}, u32[]{:S(2)}, u32[]{:S(2)}) collective-permute-start(f32[16,5120]{1,0:T(8,128)S(1)} %pad_maximum_fusion.4), channel_id=1, source_target_pairs={{0,8},{8,16},{16,24},{24,0},{1,9},{9,17},{17,25},{25,1},{2,10},{10... | collective-permute-start | bytes 983048 | tf_op jit(solution)/shard_map/ppermute | solution.py:25
  41.9 17.8 %collective-permute-start.7 = (f32[4,5120]{1,0:T(4,128)S(1)}, f32[4,5120]{1,0:T(4,128)S(1)}, u32[]{:S(2)}, u32[]{:S(2)}) collective-permute-start(f32[4,5120]{1,0:T(4,128)S(1)} %get-tuple-element.45), channel_id=1, source_target_pairs={{0,6},{2,0},{4,2},{6,4},{1,7},{3,1},{5,3},{7,5},{8,14},{10,8},{12,... | collective-permute-start | bytes 245768 | tf_op jit(solution)/shard_map/ppermute | solution.py:25
  48.8 13.8 %collective-permute-start.6 = (f32[4,5120]{1,0:T(4,128)S(1)}, f32[4,5120]{1,0:T(4,128)S(1)}, u32[]{:S(2)}, u32[]{:S(2)}) collective-permute-start(f32[4,5120]{1,0:T(4,128)S(1)} %get-tuple-element.46), channel_id=1, source_target_pairs={{0,4},{2,6},{4,0},{6,2},{1,5},{3,7},{5,1},{7,3},{8,12},{10,14},{12... | collective-permute-start | bytes 245768 | tf_op jit(solution)/shard_map/ppermute | solution.py:25
  54.2 9.6 %collective-permute-start.5 = (f32[4,5120]{1,0:T(4,128)S(1)}, f32[4,5120]{1,0:T(4,128)S(1)}, u32[]{:S(2)}, u32[]{:S(2)}) collective-permute-start(f32[4,5120]{1,0:T(4,128)S(1)} %get-tuple-element.44), channel_id=1, source_target_pairs={{0,2},{2,4},{4,6},{6,0},{1,3},{3,5},{5,7},{7,1},{8,10},{10,12},{12... | collective-permute-start | bytes 245768 | tf_op jit(solution)/shard_map/ppermute | solution.py:25
  55.9 13.2 %collective-permute-start.16 = (f32[4,5120]{1,0:T(4,128)S(1)}, f32[4,5120]{1,0:T(4,128)S(1)}, u32[]{:S(2)}, u32[]{:S(2)}) collective-permute-start(f32[4,5120]{1,0:T(4,128)S(1)} %get-tuple-element.42), channel_id=1, source_target_pairs={{0,6},{2,0},{4,2},{6,4},{1,7},{3,1},{5,3},{7,5},{8,14},{10,8},{12,... | collective-permute-start | bytes 245768 | tf_op jit(solution)/shard_map/ppermute | solution.py:25
  58.6 10.5 %collective-permute-start.15 = (f32[4,5120]{1,0:T(4,128)S(1)}, f32[4,5120]{1,0:T(4,128)S(1)}, u32[]{:S(2)}, u32[]{:S(2)}) collective-permute-start(f32[4,5120]{1,0:T(4,128)S(1)} %get-tuple-element.43), channel_id=1, source_target_pairs={{0,4},{2,6},{4,0},{6,2},{1,5},{3,7},{5,1},{7,3},{8,12},{10,14},{12... | collective-permute-start | bytes 245768 | tf_op jit(solution)/shard_map/ppermute | solution.py:25
  59.7 10.6 %collective-permute-start.14 = (f32[4,5120]{1,0:T(4,128)S(1)}, f32[4,5120]{1,0:T(4,128)S(1)}, u32[]{:S(2)}, u32[]{:S(2)}) collective-permute-start(f32[4,5120]{1,0:T(4,128)S(1)} %get-tuple-element.41), channel_id=1, source_target_pairs={{0,2},{2,4},{4,6},{6,0},{1,3},{3,5},{5,7},{7,1},{8,10},{10,12},{12... | collective-permute-start | bytes 245768 | tf_op jit(solution)/shard_map/ppermute | solution.py:25
  62.6 14.4 %collective-permute-start.25 = (f32[4,5120]{1,0:T(4,128)S(1)}, f32[4,5120]{1,0:T(4,128)S(1)}, u32[]{:S(2)}, u32[]{:S(2)}) collective-permute-start(f32[4,5120]{1,0:T(4,128)S(1)} %get-tuple-element.48), channel_id=1, source_target_pairs={{0,6},{2,0},{4,2},{6,4},{1,7},{3,1},{5,3},{7,5},{8,14},{10,8},{12,... | collective-permute-start | bytes 245768 | tf_op jit(solution)/shard_map/ppermute | solution.py:25
  63.9 13.1 %collective-permute-start.24 = (f32[4,5120]{1,0:T(4,128)S(1)}, f32[4,5120]{1,0:T(4,128)S(1)}, u32[]{:S(2)}, u32[]{:S(2)}) collective-permute-start(f32[4,5120]{1,0:T(4,128)S(1)} %get-tuple-element.49), channel_id=1, source_target_pairs={{0,4},{2,6},{4,0},{6,2},{1,5},{3,7},{5,1},{7,3},{8,12},{10,14},{12... | collective-permute-start | bytes 245768 | tf_op jit(solution)/shard_map/ppermute | solution.py:25
  69.0 8.1 %collective-permute-start.23 = (f32[4,5120]{1,0:T(4,128)S(1)}, f32[4,5120]{1,0:T(4,128)S(1)}, u32[]{:S(2)}, u32[]{:S(2)}) collective-permute-start(f32[4,5120]{1,0:T(4,128)S(1)} %get-tuple-element.47), channel_id=1, source_target_pairs={{0,2},{2,4},{4,6},{6,0},{1,3},{3,5},{5,7},{7,1},{8,10},{10,12},{12... | collective-permute-start | bytes 245768 | tf_op jit(solution)/shard_map/ppermute | solution.py:25
  69.1 7.7 %collective-permute-start.8 = (f32[1,4,5248]{2,1,0:T(4,128)S(1)}, f32[1,4,5248]{2,1,0:T(4,128)S(1)}, u32[]{:S(2)}, u32[]{:S(2)}) collective-permute-start(f32[1,4,5248]{2,1,0:T(4,128)S(1)} %broadcast_multiply_fusion.2), channel_id=1, source_target_pairs={{0,32},{32,64},{64,96},{96,128},{128,160},{160,192},{192,224},{224... | collective-permute-start | bytes 251912 | tf_op jit(solution)/shard_map/ppermute | solution.py:25
  (7 other events, 50.4 us)

commit v3 on v2

v3 whole, which is shorter than its diff:
```python
import functools

import jax
import jax.numpy as jnp
from jax import lax
from jax.experimental import pallas as pl
from jax.experimental.pallas import tpu as pltpu
from jax.sharding import Mesh, PartitionSpec as P

STEPS = 3
D = 5120
STRIP = 1024
X, ZL, Y, ZH, CORE = 4, 2, 4, 4, 2
GROUP = ("x", "zl")
SHARD = ("y", "zh", "core")

learn_rate = 0.5
momentum_factor = 0.9


def ring(x, axis, by):
    n = lax.axis_size(axis)
    return lax.ppermute(x, axis, [(i, (i + by) % n) for i in range(n)])


def partner(i, way):
    return i ^ 1 if way == 0 else 3 - i


def swap(x, axis, turn):
    pairs = []
    for y in range(Y):
        for zh in range(ZH):
            for core in range(CORE):
                way = core ^ turn
                to = (partner(y, way), zh) if axis == "y" else (y, partner(zh, way))
                pairs.append(((y * ZH + zh) * CORE + core, (to[0] * ZH + to[1]) * CORE + core))
    return lax.ppermute(x, SHARD, pairs)


def places(i, core):
    first, second = i ^ 1, 3 - i
    return (
        i,
        jnp.where(core == 0, second, first),
        jnp.where(core == 0, first, second),
        i ^ 2,
    )


OTHERS = (0, 2, 1, 3)


def split_kernel(step, g_ref, other_send, own_send, other_keep, own_keep, block, arrived):
    core = lax.axis_index("core")
    y_at = places(lax.axis_index("y"), core)
    z_at = places(lax.axis_index("zh"), core)
    order = (3, 2, 1, 0)
    copies = {}
    for q in order:
        first_row = pl.multiple_of(32 * y_at[q], 32)
        copies[q] = pltpu.make_async_copy(
            g_ref.at[step, 0, 0, pl.ds(first_row, 32), :], block.at[q], arrived.at[q]
        )
        copies[q].start()
    row = lax.broadcasted_iota(jnp.int32, (8, STRIP), 0)
    for q in order:
        copies[q].wait()
        own = (own_keep, own_send)[q // 2]
        other = (other_keep, other_send)[OTHERS[q] // 2]
        for at in range(0, D, STRIP):
            columns = slice(at, at + STRIP)
            top, low = [], []
            for z in range(ZH):
                rows = block[q, pl.ds(pl.multiple_of(8 * z_at[z], 8), 8), columns]
                turned = pltpu.roll(rows, 4, 0)
                top.append(jnp.where(core == 0, rows, turned))
                low.append(jnp.where(core == 0, turned, rows))
            for m in range(2):
                rows = slice(8 * m, 8 * m + 8)
                own[q % 2, rows, columns] = jnp.where(row < 4, top[2 * m], low[2 * m + 1])
                other[OTHERS[q] % 2, rows, columns] = jnp.where(row < 4, low[m], top[m + 2])


def split_cores(grads, step):
    shape = pltpu.VMEM((2, 16, D), jnp.float32)
    return pl.pallas_call(
        functools.partial(split_kernel, step),
        out_shape=(shape,) * 4,
        in_specs=[pl.BlockSpec(memory_space=pltpu.HBM)],
        out_specs=[pl.BlockSpec(memory_space=pltpu.VMEM)] * 4,
        scratch_shapes=[pltpu.VMEM((Y, 32, D), jnp.float32), pltpu.SemaphoreType.DMA((Y,))],
        compiler_params=pltpu.CompilerParams(vmem_limit_bytes=16 << 20),
        cost_estimate=pl.CostEstimate(flops=0, bytes_accessed=8 * 16 * D * 4, transcendentals=0),
    )(pltpu.with_memory_space_constraint(grads, pltpu.HBM))


def shard_mean(grads, step):
    other_send, own_send, other_keep, own_keep = split_cores(grads, step)
    send = own_send + ring(other_send, "core", 1)
    keep = own_keep + ring(other_keep, "core", 1)
    pair = keep + swap(send, "y", 0)
    total = pair[0] + swap(pair[1], "y", 1)
    pair = total[:8] + swap(total[8:], "zh", 0)
    total = pair[:4] + swap(pair[4:], "zh", 1)
    return (total / (Y * ZH * CORE))[None]


def per_device(numerators, push_weight, keep_share, momentum, grads):
    levels = (X * ZL).bit_length() - 1
    means = [shard_mean(grads, step) for step in range(STEPS)]
    weight = jnp.broadcast_to(push_weight[:, None, None], (1, 4, 128))
    values = jnp.concatenate([numerators, weight], axis=2)
    buffer = momentum
    keep_rows = keep_share[:, None, None]
    for step in range(STEPS):
        mean = means[step]
        buffer = momentum_factor * buffer + mean
        moved = learn_rate * (mean + momentum_factor * buffer)
        values = values - jnp.pad(moved, ((0, 0), (0, 0), (0, 128)))
        sent = ring((1.0 - keep_rows) * values, GROUP, 1 << step % levels)
        values = keep_rows * values + sent
    weight = values[:, 0, D]
    displacement = values[:, :, :D] / weight[:, None, None] - numerators / push_weight[:, None, None]
    return (displacement, buffer, weight)


def solution(mesh):
    fine = Mesh(mesh.devices.reshape(X, ZL, Y, ZH, CORE), GROUP + SHARD)
    in_specs = (
        P(GROUP, SHARD, None),
        P(GROUP),
        P(GROUP),
        P(GROUP, SHARD, None),
        P(None, GROUP, SHARD, None, None),
    )
    out_specs = (P(GROUP, SHARD, None), P(GROUP, SHARD, None), P(GROUP))
    return jax.shard_map(
        per_device, mesh=fine, in_specs=in_specs, out_specs=out_specs, check_vma=False
    )
```

time: 91.4 us -> 89.1 us (0.975)
  the two profiles are of different devices: /device:TPU:24 before, /device:TPU:64 now
where the time goes in v3:
time: 89.1 us; the launch traced here: 88.9 us
  waiting for transfers between devices  40.3 us (45%)
  starting transfers between devices  37.4 us (42%)
  Pallas kernels  5.4 us (6%)
  other arithmetic  2.89 us (3%)
  between operations  2.2 us (2%)
    ppermute x12, starting transfers between devices, swap(): return lax.ppermute(x, SHARD, pairs)  34.6 us
    ppermute x12, waiting for transfers between devices, swap(): return lax.ppermute(x, SHARD, pairs)  26.3 us
    ppermute x9, waiting for transfers between devices, ring(): return lax.ppermute(x, axis, [(i, (i + by) % n) for i in range(n)])  14 us
    pallas_call x3, Pallas kernels, split_cores(): pl.pallas_call(functools.partial(split_kernel, step), out_shape=(shape,)...  5.4 us
    ppermute x9, starting transfers between devices, ring(): return lax.ppermute(x, axis, [(i, (i + by) % n) for i in range(n)])  2.87 us
  transfers between devices with their start and end apart: 21, of which 10 were waited for; matrix products, arithmetic and copies ran while one was open for 2% of the time, Pallas kernels for 4%

profile of v3, /device:TPU:64, one launch (start us, length us, event | category | flops | bytes accessed | tf_op | source)
XLA Modules:
  0.0 88.9 jit_solution(18012470869125700343)
XLA Ops:
  0.6 1.8 %shard_map.76 = (f32[2,16,5120]{2,1,0:T(8,128)S(1)}, f32[2,16,5120]{2,1,0:T(8,128)S(1)}, f32[2,16,5120]{2,1,0:T(8,128)S(1)}, f32[2,16,5120]{2,1,0:T(8,128)S(1)}) custom-call(f32[3,1,1,128,5120]{4,3,2,1,0:T(8,128)} %g_ref.5), custom_call_target="tpu_custom_call" | custom-call | bytes 2621440 | tf_op jit(solution)/shard_map/pallas_call | solution.py:87
  2.5 1.8 %shard_map.77 = (f32[2,16,5120]{2,1,0:T(8,128)S(1)}, f32[2,16,5120]{2,1,0:T(8,128)S(1)}, f32[2,16,5120]{2,1,0:T(8,128)S(1)}, f32[2,16,5120]{2,1,0:T(8,128)S(1)}) custom-call(f32[3,1,1,128,5120]{4,3,2,1,0:T(8,128)} %g_ref.5), custom_call_target="tpu_custom_call" | custom-call | bytes 2621440 | tf_op jit(solution)/shard_map/pallas_call | solution.py:87
  4.9 1.8 %shard_map.78 = (f32[2,16,5120]{2,1,0:T(8,128)S(1)}, f32[2,16,5120]{2,1,0:T(8,128)S(1)}, f32[2,16,5120]{2,1,0:T(8,128)S(1)}, f32[2,16,5120]{2,1,0:T(8,128)S(1)}) custom-call(f32[3,1,1,128,5120]{4,3,2,1,0:T(8,128)} %g_ref.5), custom_call_target="tpu_custom_call" | custom-call | bytes 2621440 | tf_op jit(solution)/shard_map/pallas_call | solution.py:87
  7.4 1.7 %collective-permute-start.2 = (f32[2,16,5120]{2,1,0:T(8,128)S(1)}, f32[2,16,5120]{2,1,0:T(8,128)S(1)}, u32[]{:S(2)}, u32[]{:S(2)}) collective-permute-start(f32[2,16,5120]{2,1,0:T(8,128)S(1)} %add.90), channel_id=1, source_target_pairs={{0,8},{1,25},{2,10},{3,27},{4,12},{5,29},{6,14},{7,31},{8,0},{9,17... | collective-permute-start | bytes 1966088 | tf_op jit(solution)/shard_map/ppermute | solution.py:38
  9.1 1.3 %collective-permute-start.7 = (f32[2,16,5120]{2,1,0:T(8,128)S(1)}, f32[2,16,5120]{2,1,0:T(8,128)S(1)}, u32[]{:S(2)}, u32[]{:S(2)}) collective-permute-start(f32[2,16,5120]{2,1,0:T(8,128)S(1)} %get-tuple-element.20), channel_id=1, source_target_pairs={{0,1},{1,0},{2,3},{3,2},{4,5},{5,4},{6,7},{7,6},{8,9},{9,8},{10,11... | collective-permute-start | bytes 1966088 | tf_op jit(solution)/shard_map/ppermute | solution.py:23
  12.1 2.0 %collective-permute-start.16 = (f32[2,16,5120]{2,1,0:T(8,128)S(1)}, f32[2,16,5120]{2,1,0:T(8,128)S(1)}, u32[]{:S(2)}, u32[]{:S(2)}) collective-permute-start(f32[2,16,5120]{2,1,0:T(8,128)S(1)} %add.108), channel_id=1, source_target_pairs={{0,8},{1,25},{2,10},{3,27},{4,12},{5,29},{6,14},{7,31},{8,0},{9,17... | collective-permute-start | bytes 1966088 | tf_op jit(solution)/shard_map/ppermute | solution.py:38
  14.1 4.0 %collective-permute-done.2 = f32[2,16,5120]{2,1,0:T(8,128)S(1)} collective-permute-done((f32[2,16,5120]{2,1,0:T(8,128)S(1)}, f32[2,16,5120]{2,1,0:T(8,128)S(1)}, u32[]{:S(2)}, u32[]{:S(2)}) %collective-permute-start.2) | collective-permute-done | bytes 655392 | tf_op jit(solution)/shard_map/ppermute | solution.py:38
  18.2 3.1 %collective-permute-start.3 = (f32[16,5120]{1,0:T(8,128)S(1)}, f32[16,5120]{1,0:T(8,128)S(1)}, u32[]{:S(2)}, u32[]{:S(2)}) collective-permute-start(f32[16,5120]{1,0:T(8,128)S(1)} %slice_bitcast_fusion.4), channel_id=1, source_target_pairs={{0,24},{1,9},{2,26},{3,11},{4,28},{5,13},{6,30},{7,15},{8,16},{9,1... | collective-permute-start | bytes 983048 | tf_op jit(solution)/shard_map/ppermute | solution.py:38
  21.3 7.3 %collective-permute-done.9 = f32[2,16,5120]{2,1,0:T(8,128)S(1)} collective-permute-done((f32[2,16,5120]{2,1,0:T(8,128)S(1)}, f32[2,16,5120]{2,1,0:T(8,128)S(1)}, u32[]{:S(2)}, u32[]{:S(2)}) %collective-permute-start.9) | collective-permute-done | bytes 655392 | tf_op jit(solution)/shard_map/ppermute | solution.py:38
  28.7 3.1 %collective-permute-start.10 = (f32[16,5120]{1,0:T(8,128)S(1)}, f32[16,5120]{1,0:T(8,128)S(1)}, u32[]{:S(2)}, u32[]{:S(2)}) collective-permute-start(f32[16,5120]{1,0:T(8,128)S(1)} %slice_bitcast_fusion.2), channel_id=1, source_target_pairs={{0,24},{1,9},{2,26},{3,11},{4,28},{5,13},{6,30},{7,15},{8,16},{9,1... | collective-permute-start | bytes 983048 | tf_op jit(solution)/shard_map/ppermute | solution.py:38
  31.8 7.3 %collective-permute-done.16 = f32[2,16,5120]{2,1,0:T(8,128)S(1)} collective-permute-done((f32[2,16,5120]{2,1,0:T(8,128)S(1)}, f32[2,16,5120]{2,1,0:T(8,128)S(1)}, u32[]{:S(2)}, u32[]{:S(2)}) %collective-permute-start.16) | collective-permute-done | bytes 655392 | tf_op jit(solution)/shard_map/ppermute | solution.py:38
  39.3 3.1 %collective-permute-start.17 = (f32[16,5120]{1,0:T(8,128)S(1)}, f32[16,5120]{1,0:T(8,128)S(1)}, u32[]{:S(2)}, u32[]{:S(2)}) collective-permute-start(f32[16,5120]{1,0:T(8,128)S(1)} %slice_bitcast_fusion), channel_id=1, source_target_pairs={{0,24},{1,9},{2,26},{3,11},{4,28},{5,13},{6,30},{7,15},{8,16},{9,1... | collective-permute-start | bytes 983048 | tf_op jit(solution)/shard_map/ppermute | solution.py:38
  42.6 3.0 %collective-permute-start.11 = (f32[8,5120]{1,0:T(8,128)S(1)}, f32[8,5120]{1,0:T(8,128)S(1)}, u32[]{:S(2)}, u32[]{:S(2)}) collective-permute-start(f32[8,5120]{1,0:T(8,128)S(1)} %slice.89), channel_id=1, source_target_pairs={{0,2},{1,7},{2,0},{3,5},{4,6},{5,3},{6,4},{7,1},{8,10},{9,15},{10,... | collective-permute-start | bytes 491528 | tf_op jit(solution)/shard_map/ppermute | solution.py:38
  45.6 2.0 %collective-permute-done.17 = f32[16,5120]{1,0:T(8,128)S(1)} collective-permute-done((f32[16,5120]{1,0:T(8,128)S(1)}, f32[16,5120]{1,0:T(8,128)S(1)}, u32[]{:S(2)}, u32[]{:S(2)}) %collective-permute-start.17) | collective-permute-done | bytes 327712 | tf_op jit(solution)/shard_map/ppermute | solution.py:38
  47.7 1.5 %collective-permute-start.18 = (f32[8,5120]{1,0:T(8,128)S(1)}, f32[8,5120]{1,0:T(8,128)S(1)}, u32[]{:S(2)}, u32[]{:S(2)}) collective-permute-start(f32[8,5120]{1,0:T(8,128)S(1)} %slice.95), channel_id=1, source_target_pairs={{0,2},{1,7},{2,0},{3,5},{4,6},{5,3},{6,4},{7,1},{8,10},{9,15},{10,... | collective-permute-start | bytes 491528 | tf_op jit(solution)/shard_map/ppermute | solution.py:38
  49.2 1.3 %collective-permute-done.4 = f32[8,5120]{1,0:T(8,128)S(1)} collective-permute-done((f32[8,5120]{1,0:T(8,128)S(1)}, f32[8,5120]{1,0:T(8,128)S(1)}, u32[]{:S(2)}, u32[]{:S(2)}) %collective-permute-start.4) | collective-permute-done | bytes 163872 | tf_op jit(solution)/shard_map/ppermute | solution.py:38
  50.5 6.2 %collective-permute-start.5 = (f32[4,5120]{1,0:T(4,128)S(1)}, f32[4,5120]{1,0:T(4,128)S(1)}, u32[]{:S(2)}, u32[]{:S(2)}) collective-permute-start(f32[4,5120]{1,0:T(4,128)S(1)} %slice.85), channel_id=1, source_target_pairs={{0,6},{1,3},{2,4},{3,1},{4,2},{5,7},{6,0},{7,5},{8,14},{9,11},{10,... | collective-permute-start | bytes 245768 | tf_op jit(solution)/shard_map/ppermute | solution.py:38
  56.8 8.6 %collective-permute-start.12 = (f32[4,5120]{1,0:T(4,128)S(1)}, f32[4,5120]{1,0:T(4,128)S(1)}, u32[]{:S(2)}, u32[]{:S(2)}) collective-permute-start(f32[4,5120]{1,0:T(4,128)S(1)} %slice.91), channel_id=1, source_target_pairs={{0,6},{1,3},{2,4},{3,1},{4,2},{5,7},{6,0},{7,5},{8,14},{9,11},{10,... | collective-permute-start | bytes 245768 | tf_op jit(solution)/shard_map/ppermute | solution.py:38
  65.4 2.0 %collective-permute-start.19 = (f32[4,5120]{1,0:T(4,128)S(1)}, f32[4,5120]{1,0:T(4,128)S(1)}, u32[]{:S(2)}, u32[]{:S(2)}) collective-permute-start(f32[4,5120]{1,0:T(4,128)S(1)} %slice.97), channel_id=1, source_target_pairs={{0,6},{1,3},{2,4},{3,1},{4,2},{5,7},{6,0},{7,5},{8,14},{9,11},{10,... | collective-permute-start | bytes 245768 | tf_op jit(solution)/shard_map/ppermute | solution.py:38
  67.8 4.3 %collective-permute-done.19 = f32[4,5120]{1,0:T(4,128)S(1)} collective-permute-done((f32[4,5120]{1,0:T(4,128)S(1)}, f32[4,5120]{1,0:T(4,128)S(1)}, u32[]{:S(2)}, u32[]{:S(2)}) %collective-permute-start.19) | collective-permute-done | bytes 81952 | tf_op jit(solution)/shard_map/ppermute | solution.py:38
  72.8 2.3 %collective-permute-done.6 = f32[1,4,5248]{2,1,0:T(4,128)S(1)} collective-permute-done((f32[1,4,5248]{2,1,0:T(4,128)S(1)}, f32[1,4,5248]{2,1,0:T(4,128)S(1)}, u32[]{:S(2)}, u32[]{:S(2)}) %collective-permute-start.6) | collective-permute-done | bytes 84000 | tf_op jit(solution)/shard_map/ppermute | solution.py:23
  75.3 5.7 %collective-permute-done.13 = f32[1,4,5248]{2,1,0:T(4,128)S(1)} collective-permute-done((f32[1,4,5248]{2,1,0:T(4,128)S(1)}, f32[1,4,5248]{2,1,0:T(4,128)S(1)}, u32[]{:S(2)}, u32[]{:S(2)}) %collective-permute-start.13) | collective-permute-done | bytes 84000 | tf_op jit(solution)/shard_map/ppermute | solution.py:23
  81.1 6.0 %collective-permute-done.20 = f32[1,4,5248]{2,1,0:T(4,128)S(1)} collective-permute-done((f32[1,4,5248]{2,1,0:T(4,128)S(1)}, f32[1,4,5248]{2,1,0:T(4,128)S(1)}, u32[]{:S(2)}, u32[]{:S(2)}) %collective-permute-start.20) | collective-permute-done | bytes 84000 | tf_op jit(solution)/shard_map/ppermute | solution.py:23
  87.6 1.3 %divide_subtract_fusion = f32[1,4,5120]{2,1,0:T(4,128)} fusion(f32[1,4,5120]{2,1,0:T(4,128)S(1)} %copy-done, f32[1,4,5248]{2,1,0:T(4,128)S(1)} %multiply_add_fusion, f32[]{:T(128)} %bitcast.45, f32[]{:T(128)} %bitcast.12), kind=kLoop, calls=%fused_computation.19 | loop fusion | flops 61440 | bytes 245768 | tf_op jit(solution)/shard_map/sub | solution.py:124
  (54 shorter events, 4.3 us)
Async XLA Ops:
  2.4 4.9 %collective-permute-start.1 = (f32[2,16,5120]{2,1,0:T(8,128)S(1)}, f32[2,16,5120]{2,1,0:T(8,128)S(1)}, u32[]{:S(2)}, u32[]{:S(2)}) collective-permute-start(f32[2,16,5120]{2,1,0:T(8,128)S(1)} %get-tuple-element.18), channel_id=1, source_target_pairs={{0,1},{1,0},{2,3},{3,2},{4,5},{5,4},{6,7},{7,6},{8,9},{9,8},{10,11... | collective-permute-start | bytes 1966088 | tf_op jit(solution)/shard_map/ppermute | solution.py:23
  4.4 7.3 %collective-permute-start.8 = (f32[2,16,5120]{2,1,0:T(8,128)S(1)}, f32[2,16,5120]{2,1,0:T(8,128)S(1)}, u32[]{:S(2)}, u32[]{:S(2)}) collective-permute-start(f32[2,16,5120]{2,1,0:T(8,128)S(1)} %get-tuple-element.22), channel_id=1, source_target_pairs={{0,1},{1,0},{2,3},{3,2},{4,5},{5,4},{6,7},{7,6},{8,9},{9,8},{10,11... | collective-permute-start | bytes 1966088 | tf_op jit(solution)/shard_map/ppermute | solution.py:23
  6.7 5.1 %collective-permute-start.15 = (f32[2,16,5120]{2,1,0:T(8,128)S(1)}, f32[2,16,5120]{2,1,0:T(8,128)S(1)}, u32[]{:S(2)}, u32[]{:S(2)}) collective-permute-start(f32[2,16,5120]{2,1,0:T(8,128)S(1)} %get-tuple-element.26), channel_id=1, source_target_pairs={{0,1},{1,0},{2,3},{3,2},{4,5},{5,4},{6,7},{7,6},{8,9},{9,8},{10,11... | collective-permute-start | bytes 1966088 | tf_op jit(solution)/shard_map/ppermute | solution.py:23
  6.8 5.3 %collective-permute-start = (f32[2,16,5120]{2,1,0:T(8,128)S(1)}, f32[2,16,5120]{2,1,0:T(8,128)S(1)}, u32[]{:S(2)}, u32[]{:S(2)}) collective-permute-start(f32[2,16,5120]{2,1,0:T(8,128)S(1)} %get-tuple-element.16), channel_id=1, source_target_pairs={{0,1},{1,0},{2,3},{3,2},{4,5},{5,4},{6,7},{7,6},{8,9},{9,8},{10,11... | collective-permute-start | bytes 1966088 | tf_op jit(solution)/shard_map/ppermute | solution.py:23
  7.4 10.7 %collective-permute-start.2 = (f32[2,16,5120]{2,1,0:T(8,128)S(1)}, f32[2,16,5120]{2,1,0:T(8,128)S(1)}, u32[]{:S(2)}, u32[]{:S(2)}) collective-permute-start(f32[2,16,5120]{2,1,0:T(8,128)S(1)} %add.90), channel_id=1, source_target_pairs={{0,8},{1,25},{2,10},{3,27},{4,12},{5,29},{6,14},{7,31},{8,0},{9,17... | collective-permute-start | bytes 1966088 | tf_op jit(solution)/shard_map/ppermute | solution.py:38
  9.1 12.2 %collective-permute-start.7 = (f32[2,16,5120]{2,1,0:T(8,128)S(1)}, f32[2,16,5120]{2,1,0:T(8,128)S(1)}, u32[]{:S(2)}, u32[]{:S(2)}) collective-permute-start(f32[2,16,5120]{2,1,0:T(8,128)S(1)} %get-tuple-element.20), channel_id=1, source_target_pairs={{0,1},{1,0},{2,3},{3,2},{4,5},{5,4},{6,7},{7,6},{8,9},{9,8},{10,11... | collective-permute-start | bytes 1966088 | tf_op jit(solution)/shard_map/ppermute | solution.py:23
  11.6 20.2 %collective-permute-start.14 = (f32[2,16,5120]{2,1,0:T(8,128)S(1)}, f32[2,16,5120]{2,1,0:T(8,128)S(1)}, u32[]{:S(2)}, u32[]{:S(2)}) collective-permute-start(f32[2,16,5120]{2,1,0:T(8,128)S(1)} %get-tuple-element.24), channel_id=1, source_target_pairs={{0,1},{1,0},{2,3},{3,2},{4,5},{5,4},{6,7},{7,6},{8,9},{9,8},{10,11... | collective-permute-start | bytes 1966088 | tf_op jit(solution)/shard_map/ppermute | solution.py:23
  11.8 16.8 %collective-permute-start.9 = (f32[2,16,5120]{2,1,0:T(8,128)S(1)}, f32[2,16,5120]{2,1,0:T(8,128)S(1)}, u32[]{:S(2)}, u32[]{:S(2)}) collective-permute-start(f32[2,16,5120]{2,1,0:T(8,128)S(1)} %add.99), channel_id=1, source_target_pairs={{0,8},{1,25},{2,10},{3,27},{4,12},{5,29},{6,14},{7,31},{8,0},{9,17... | collective-permute-start | bytes 1966088 | tf_op jit(solution)/shard_map/ppermute | solution.py:38
  12.1 27.0 %collective-permute-start.16 = (f32[2,16,5120]{2,1,0:T(8,128)S(1)}, f32[2,16,5120]{2,1,0:T(8,128)S(1)}, u32[]{:S(2)}, u32[]{:S(2)}) collective-permute-start(f32[2,16,5120]{2,1,0:T(8,128)S(1)} %add.108), channel_id=1, source_target_pairs={{0,8},{1,25},{2,10},{3,27},{4,12},{5,29},{6,14},{7,31},{8,0},{9,17... | collective-permute-start | bytes 1966088 | tf_op jit(solution)/shard_map/ppermute | solution.py:38
  18.1 49.4 %copy-start.1 = (f32[1,4,5120]{2,1,0:T(4,128)S(1)}, f32[1,4,5120]{2,1,0:T(4,128)}, u32[]{:S(2)}) copy-start(f32[1,4,5120]{2,1,0:T(4,128)} %param.8) | copy-start | bytes 245764
  18.1 49.5 %copy-start = (f32[1,4,5120]{2,1,0:T(4,128)S(1)}, f32[1,4,5120]{2,1,0:T(4,128)}, u32[]{:S(2)}) copy-start(f32[1,4,5120]{2,1,0:T(4,128)} %param.5) | copy-start | bytes 245764
  18.2 24.2 %collective-permute-start.3 = (f32[16,5120]{1,0:T(8,128)S(1)}, f32[16,5120]{1,0:T(8,128)S(1)}, u32[]{:S(2)}, u32[]{:S(2)}) collective-permute-start(f32[16,5120]{1,0:T(8,128)S(1)} %slice_bitcast_fusion.4), channel_id=1, source_target_pairs={{0,24},{1,9},{2,26},{3,11},{4,28},{5,13},{6,30},{7,15},{8,16},{9,1... | collective-permute-start | bytes 983048 | tf_op jit(solution)/shard_map/ppermute | solution.py:38
  28.7 13.8 %collective-permute-start.10 = (f32[16,5120]{1,0:T(8,128)S(1)}, f32[16,5120]{1,0:T(8,128)S(1)}, u32[]{:S(2)}, u32[]{:S(2)}) collective-permute-start(f32[16,5120]{1,0:T(8,128)S(1)} %slice_bitcast_fusion.2), channel_id=1, source_target_pairs={{0,24},{1,9},{2,26},{3,11},{4,28},{5,13},{6,30},{7,15},{8,16},{9,1... | collective-permute-start | bytes 983048 | tf_op jit(solution)/shard_map/ppermute | solution.py:38
  39.3 8.4 %collective-permute-start.17 = (f32[16,5120]{1,0:T(8,128)S(1)}, f32[16,5120]{1,0:T(8,128)S(1)}, u32[]{:S(2)}, u32[]{:S(2)}) collective-permute-start(f32[16,5120]{1,0:T(8,128)S(1)} %slice_bitcast_fusion), channel_id=1, source_target_pairs={{0,24},{1,9},{2,26},{3,11},{4,28},{5,13},{6,30},{7,15},{8,16},{9,1... | collective-permute-start | bytes 983048 | tf_op jit(solution)/shard_map/ppermute | solution.py:38
  42.4 8.1 %collective-permute-start.4 = (f32[8,5120]{1,0:T(8,128)S(1)}, f32[8,5120]{1,0:T(8,128)S(1)}, u32[]{:S(2)}, u32[]{:S(2)}) collective-permute-start(f32[8,5120]{1,0:T(8,128)S(1)} %slice.83), channel_id=1, source_target_pairs={{0,2},{1,7},{2,0},{3,5},{4,6},{5,3},{6,4},{7,1},{8,10},{9,15},{10,... | collective-permute-start | bytes 491528 | tf_op jit(solution)/shard_map/ppermute | solution.py:38
  42.6 14.1 %collective-permute-start.11 = (f32[8,5120]{1,0:T(8,128)S(1)}, f32[8,5120]{1,0:T(8,128)S(1)}, u32[]{:S(2)}, u32[]{:S(2)}) collective-permute-start(f32[8,5120]{1,0:T(8,128)S(1)} %slice.89), channel_id=1, source_target_pairs={{0,2},{1,7},{2,0},{3,5},{4,6},{5,3},{6,4},{7,1},{8,10},{9,15},{10,... | collective-permute-start | bytes 491528 | tf_op jit(solution)/shard_map/ppermute | solution.py:38
  47.7 17.7 %collective-permute-start.18 = (f32[8,5120]{1,0:T(8,128)S(1)}, f32[8,5120]{1,0:T(8,128)S(1)}, u32[]{:S(2)}, u32[]{:S(2)}) collective-permute-start(f32[8,5120]{1,0:T(8,128)S(1)} %slice.95), channel_id=1, source_target_pairs={{0,2},{1,7},{2,0},{3,5},{4,6},{5,3},{6,4},{7,1},{8,10},{9,15},{10,... | collective-permute-start | bytes 491528 | tf_op jit(solution)/shard_map/ppermute | solution.py:38
  50.5 17.0 %collective-permute-start.5 = (f32[4,5120]{1,0:T(4,128)S(1)}, f32[4,5120]{1,0:T(4,128)S(1)}, u32[]{:S(2)}, u32[]{:S(2)}) collective-permute-start(f32[4,5120]{1,0:T(4,128)S(1)} %slice.85), channel_id=1, source_target_pairs={{0,6},{1,3},{2,4},{3,1},{4,2},{5,7},{6,0},{7,5},{8,14},{9,11},{10,... | collective-permute-start | bytes 245768 | tf_op jit(solution)/shard_map/ppermute | solution.py:38
  56.8 11.0 %collective-permute-start.12 = (f32[4,5120]{1,0:T(4,128)S(1)}, f32[4,5120]{1,0:T(4,128)S(1)}, u32[]{:S(2)}, u32[]{:S(2)}) collective-permute-start(f32[4,5120]{1,0:T(4,128)S(1)} %slice.91), channel_id=1, source_target_pairs={{0,6},{1,3},{2,4},{3,1},{4,2},{5,7},{6,0},{7,5},{8,14},{9,11},{10,... | collective-permute-start | bytes 245768 | tf_op jit(solution)/shard_map/ppermute | solution.py:38
  65.4 6.6 %collective-permute-start.19 = (f32[4,5120]{1,0:T(4,128)S(1)}, f32[4,5120]{1,0:T(4,128)S(1)}, u32[]{:S(2)}, u32[]{:S(2)}) collective-permute-start(f32[4,5120]{1,0:T(4,128)S(1)} %slice.97), channel_id=1, source_target_pairs={{0,6},{1,3},{2,4},{3,1},{4,2},{5,7},{6,0},{7,5},{8,14},{9,11},{10,... | collective-permute-start | bytes 245768 | tf_op jit(solution)/shard_map/ppermute | solution.py:38
  67.6 7.5 %collective-permute-start.6 = (f32[1,4,5248]{2,1,0:T(4,128)S(1)}, f32[1,4,5248]{2,1,0:T(4,128)S(1)}, u32[]{:S(2)}, u32[]{:S(2)}) collective-permute-start(f32[1,4,5248]{2,1,0:T(4,128)S(1)} %broadcast_multiply_fusion.2), channel_id=1, source_target_pairs={{0,32},{32,64},{64,96},{96,128},{128,160},{160,192},{192,224},{224... | collective-permute-start | bytes 251912 | tf_op jit(solution)/shard_map/ppermute | solution.py:23
  75.2 5.8 %collective-permute-start.13 = (f32[1,4,5248]{2,1,0:T(4,128)S(1)}, f32[1,4,5248]{2,1,0:T(4,128)S(1)}, u32[]{:S(2)}, u32[]{:S(2)}) collective-permute-start(f32[1,4,5248]{2,1,0:T(4,128)S(1)} %get-tuple-element.27), channel_id=1, source_target_pairs={{0,64},{32,96},{64,128},{96,160},{128,192},{160,224},{192,0},{224,... | collective-permute-start | bytes 251912 | tf_op jit(solution)/shard_map/ppermute | solution.py:23
  81.0 6.1 %collective-permute-start.20 = (f32[1,4,5248]{2,1,0:T(4,128)S(1)}, f32[1,4,5248]{2,1,0:T(4,128)S(1)}, u32[]{:S(2)}, u32[]{:S(2)}) collective-permute-start(f32[1,4,5248]{2,1,0:T(4,128)S(1)} %broadcast_multiply_fusion), channel_id=1, source_target_pairs={{0,128},{32,160},{64,192},{96,224},{128,0},{160,32},{192,64},{224,... | collective-permute-start | bytes 251912 | tf_op jit(solution)/shard_map/ppermute | solution.py:23

commit v4 on v3

--- a/solution.py
+++ b/solution.py
@@ -99,11 +99,11 @@
     other_send, own_send, other_keep, own_keep = split_cores(grads, step)
     send = own_send + ring(other_send, "core", 1)
     keep = own_keep + ring(other_keep, "core", 1)
-    pair = keep + swap(send, "y", 0)
-    total = pair[0] + swap(pair[1], "y", 1)
-    pair = total[:8] + swap(total[8:], "zh", 0)
-    total = pair[:4] + swap(pair[4:], "zh", 1)
-    return (total / (Y * ZH * CORE))[None]
+    rows = keep + swap(send, "y", 0)
+    rows = rows[:, :8] + swap(rows[:, 8:], "zh", 0)
+    rows = rows[0] + swap(rows[1], "y", 1)
+    rows = rows[:4] + swap(rows[4:], "zh", 1)
+    return (rows / (Y * ZH * CORE))[None]
 
 
 def per_device(numerators, push_weight, keep_share, momentum, grads):

time: 89.1 us -> 78.6 us (0.88)
  the two profiles are of different devices: /device:TPU:64 before, /device:TPU:24 now
where the time goes in v4:
time: 78.6 us; the launch traced here: 78.4 us
  waiting for transfers between devices  35.1 us (45%)
  starting transfers between devices  32.2 us (41%)
  Pallas kernels  5.4 us (7%)
  other arithmetic  2.89 us (4%)
  between operations  2.17 us (3%)
    ppermute x12, starting transfers between devices, swap(): return lax.ppermute(x, SHARD, pairs)  26.9 us
    ppermute x12, waiting for transfers between devices, swap(): return lax.ppermute(x, SHARD, pairs)  18.5 us
    ppermute x9, waiting for transfers between devices, ring(): return lax.ppermute(x, axis, [(i, (i + by) % n) for i in range(n)])  16.7 us
    pallas_call x3, Pallas kernels, split_cores(): pl.pallas_call(functools.partial(split_kernel, step), out_shape=(shape,)...  5.4 us
    ppermute x9, starting transfers between devices, ring(): return lax.ppermute(x, axis, [(i, (i + by) % n) for i in range(n)])  5.28 us
  transfers between devices with their start and end apart: 21, of which 9 were waited for; matrix products, arithmetic and copies ran while one was open for 2% of the time, Pallas kernels for 5%

profile of v4, /device:TPU:24, one launch (start us, length us, event | category | flops | bytes accessed | tf_op | source)
XLA Modules:
  0.0 78.4 jit_solution(15695748455355907030)
XLA Ops:
  0.6 1.8 %shard_map.76 = (f32[2,16,5120]{2,1,0:T(8,128)S(1)}, f32[2,16,5120]{2,1,0:T(8,128)S(1)}, f32[2,16,5120]{2,1,0:T(8,128)S(1)}, f32[2,16,5120]{2,1,0:T(8,128)S(1)}) custom-call(f32[3,1,1,128,5120]{4,3,2,1,0:T(8,128)} %g_ref.5), custom_call_target="tpu_custom_call" | custom-call | bytes 2621440 | tf_op jit(solution)/shard_map/pallas_call | solution.py:87
  2.5 1.8 %shard_map.77 = (f32[2,16,5120]{2,1,0:T(8,128)S(1)}, f32[2,16,5120]{2,1,0:T(8,128)S(1)}, f32[2,16,5120]{2,1,0:T(8,128)S(1)}, f32[2,16,5120]{2,1,0:T(8,128)S(1)}) custom-call(f32[3,1,1,128,5120]{4,3,2,1,0:T(8,128)} %g_ref.5), custom_call_target="tpu_custom_call" | custom-call | bytes 2621440 | tf_op jit(solution)/shard_map/pallas_call | solution.py:87
  4.9 1.8 %shard_map.78 = (f32[2,16,5120]{2,1,0:T(8,128)S(1)}, f32[2,16,5120]{2,1,0:T(8,128)S(1)}, f32[2,16,5120]{2,1,0:T(8,128)S(1)}, f32[2,16,5120]{2,1,0:T(8,128)S(1)}) custom-call(f32[3,1,1,128,5120]{4,3,2,1,0:T(8,128)} %g_ref.5), custom_call_target="tpu_custom_call" | custom-call | bytes 2621440 | tf_op jit(solution)/shard_map/pallas_call | solution.py:87
  7.4 0.8 %collective-permute-start.2 = (f32[2,16,5120]{2,1,0:T(8,128)S(1)}, f32[2,16,5120]{2,1,0:T(8,128)S(1)}, u32[]{:S(2)}, u32[]{:S(2)}) collective-permute-start(f32[2,16,5120]{2,1,0:T(8,128)S(1)} %add.90), channel_id=1, source_target_pairs={{0,8},{1,25},{2,10},{3,27},{4,12},{5,29},{6,14},{7,31},{8,0},{9,17... | collective-permute-start | bytes 1966088 | tf_op jit(solution)/shard_map/ppermute | solution.py:38
  8.2 1.0 %collective-permute-start.7 = (f32[2,16,5120]{2,1,0:T(8,128)S(1)}, f32[2,16,5120]{2,1,0:T(8,128)S(1)}, u32[]{:S(2)}, u32[]{:S(2)}) collective-permute-start(f32[2,16,5120]{2,1,0:T(8,128)S(1)} %get-tuple-element.20), channel_id=1, source_target_pairs={{0,1},{1,0},{2,3},{3,2},{4,5},{5,4},{6,7},{7,6},{8,9},{9,8},{10,11... | collective-permute-start | bytes 1966088 | tf_op jit(solution)/shard_map/ppermute | solution.py:23
  11.7 1.4 %collective-permute-start.16 = (f32[2,16,5120]{2,1,0:T(8,128)S(1)}, f32[2,16,5120]{2,1,0:T(8,128)S(1)}, u32[]{:S(2)}, u32[]{:S(2)}) collective-permute-start(f32[2,16,5120]{2,1,0:T(8,128)S(1)} %add.108), channel_id=1, source_target_pairs={{0,8},{1,25},{2,10},{3,27},{4,12},{5,29},{6,14},{7,31},{8,0},{9,17... | collective-permute-start | bytes 1966088 | tf_op jit(solution)/shard_map/ppermute | solution.py:38
  13.0 5.0 %collective-permute-done.2 = f32[2,16,5120]{2,1,0:T(8,128)S(1)} collective-permute-done((f32[2,16,5120]{2,1,0:T(8,128)S(1)}, f32[2,16,5120]{2,1,0:T(8,128)S(1)}, u32[]{:S(2)}, u32[]{:S(2)}) %collective-permute-start.2) | collective-permute-done | bytes 655392 | tf_op jit(solution)/shard_map/ppermute | solution.py:38
  18.2 3.4 %collective-permute-start.3 = (f32[2,8,5120]{2,1,0:T(8,128)S(1)}, f32[2,8,5120]{2,1,0:T(8,128)S(1)}, u32[]{:S(2)}, u32[]{:S(2)}) collective-permute-start(f32[2,8,5120]{2,1,0:T(8,128)S(1)} %slice.81), channel_id=1, source_target_pairs={{0,2},{1,7},{2,0},{3,5},{4,6},{5,3},{6,4},{7,1},{8,10},{9,15},{10,... | collective-permute-start | bytes 983048 | tf_op jit(solution)/shard_map/ppermute | solution.py:38
  21.6 3.5 %collective-permute-done.9 = f32[2,16,5120]{2,1,0:T(8,128)S(1)} collective-permute-done((f32[2,16,5120]{2,1,0:T(8,128)S(1)}, f32[2,16,5120]{2,1,0:T(8,128)S(1)}, u32[]{:S(2)}, u32[]{:S(2)}) %collective-permute-start.9) | collective-permute-done | bytes 655392 | tf_op jit(solution)/shard_map/ppermute | solution.py:38
  25.2 3.4 %collective-permute-start.10 = (f32[2,8,5120]{2,1,0:T(8,128)S(1)}, f32[2,8,5120]{2,1,0:T(8,128)S(1)}, u32[]{:S(2)}, u32[]{:S(2)}) collective-permute-start(f32[2,8,5120]{2,1,0:T(8,128)S(1)} %slice.87), channel_id=1, source_target_pairs={{0,2},{1,7},{2,0},{3,5},{4,6},{5,3},{6,4},{7,1},{8,10},{9,15},{10,... | collective-permute-start | bytes 983048 | tf_op jit(solution)/shard_map/ppermute | solution.py:38
  28.6 3.5 %collective-permute-done.16 = f32[2,16,5120]{2,1,0:T(8,128)S(1)} collective-permute-done((f32[2,16,5120]{2,1,0:T(8,128)S(1)}, f32[2,16,5120]{2,1,0:T(8,128)S(1)}, u32[]{:S(2)}, u32[]{:S(2)}) %collective-permute-start.16) | collective-permute-done | bytes 655392 | tf_op jit(solution)/shard_map/ppermute | solution.py:38
  32.2 3.4 %collective-permute-start.17 = (f32[2,8,5120]{2,1,0:T(8,128)S(1)}, f32[2,8,5120]{2,1,0:T(8,128)S(1)}, u32[]{:S(2)}, u32[]{:S(2)}) collective-permute-start(f32[2,8,5120]{2,1,0:T(8,128)S(1)} %slice.93), channel_id=1, source_target_pairs={{0,2},{1,7},{2,0},{3,5},{4,6},{5,3},{6,4},{7,1},{8,10},{9,15},{10,... | collective-permute-start | bytes 983048 | tf_op jit(solution)/shard_map/ppermute | solution.py:38
  36.0 2.2 %collective-permute-done.10 = f32[2,8,5120]{2,1,0:T(8,128)S(1)} collective-permute-done((f32[2,8,5120]{2,1,0:T(8,128)S(1)}, f32[2,8,5120]{2,1,0:T(8,128)S(1)}, u32[]{:S(2)}, u32[]{:S(2)}) %collective-permute-start.10) | collective-permute-done | bytes 327712 | tf_op jit(solution)/shard_map/ppermute | solution.py:38
  38.2 0.9 %collective-permute-start.11 = (f32[8,5120]{1,0:T(8,128)S(1)}, f32[8,5120]{1,0:T(8,128)S(1)}, u32[]{:S(2)}, u32[]{:S(2)}) collective-permute-start(f32[8,5120]{1,0:T(8,128)S(1)} %slice_bitcast_fusion.2), channel_id=1, source_target_pairs={{0,24},{1,9},{2,26},{3,11},{4,28},{5,13},{6,30},{7,15},{8,16},{9,1... | collective-permute-start | bytes 491528 | tf_op jit(solution)/shard_map/ppermute | solution.py:38
  39.1 3.7 %collective-permute-done.17 = f32[2,8,5120]{2,1,0:T(8,128)S(1)} collective-permute-done((f32[2,8,5120]{2,1,0:T(8,128)S(1)}, f32[2,8,5120]{2,1,0:T(8,128)S(1)}, u32[]{:S(2)}, u32[]{:S(2)}) %collective-permute-start.17) | collective-permute-done | bytes 327712 | tf_op jit(solution)/shard_map/ppermute | solution.py:38
  42.9 3.7 %collective-permute-start.18 = (f32[8,5120]{1,0:T(8,128)S(1)}, f32[8,5120]{1,0:T(8,128)S(1)}, u32[]{:S(2)}, u32[]{:S(2)}) collective-permute-start(f32[8,5120]{1,0:T(8,128)S(1)} %slice_bitcast_fusion), channel_id=1, source_target_pairs={{0,24},{1,9},{2,26},{3,11},{4,28},{5,13},{6,30},{7,15},{8,16},{9,1... | collective-permute-start | bytes 491528 | tf_op jit(solution)/shard_map/ppermute | solution.py:38
  46.6 2.6 %collective-permute-start.5 = (f32[4,5120]{1,0:T(4,128)S(1)}, f32[4,5120]{1,0:T(4,128)S(1)}, u32[]{:S(2)}, u32[]{:S(2)}) collective-permute-start(f32[4,5120]{1,0:T(4,128)S(1)} %slice.85), channel_id=1, source_target_pairs={{0,6},{1,3},{2,4},{3,1},{4,2},{5,7},{6,0},{7,5},{8,14},{9,11},{10,... | collective-permute-start | bytes 245768 | tf_op jit(solution)/shard_map/ppermute | solution.py:38
  49.3 1.7 %collective-permute-start.12 = (f32[4,5120]{1,0:T(4,128)S(1)}, f32[4,5120]{1,0:T(4,128)S(1)}, u32[]{:S(2)}, u32[]{:S(2)}) collective-permute-start(f32[4,5120]{1,0:T(4,128)S(1)} %slice.91), channel_id=1, source_target_pairs={{0,6},{1,3},{2,4},{3,1},{4,2},{5,7},{6,0},{7,5},{8,14},{9,11},{10,... | collective-permute-start | bytes 245768 | tf_op jit(solution)/shard_map/ppermute | solution.py:38
  51.0 4.6 %collective-permute-start.19 = (f32[4,5120]{1,0:T(4,128)S(1)}, f32[4,5120]{1,0:T(4,128)S(1)}, u32[]{:S(2)}, u32[]{:S(2)}) collective-permute-start(f32[4,5120]{1,0:T(4,128)S(1)} %slice.97), channel_id=1, source_target_pairs={{0,6},{1,3},{2,4},{3,1},{4,2},{5,7},{6,0},{7,5},{8,14},{9,11},{10,... | collective-permute-start | bytes 245768 | tf_op jit(solution)/shard_map/ppermute | solution.py:38
  55.7 2.7 %collective-permute-start.6 = (f32[1,4,5248]{2,1,0:T(4,128)S(1)}, f32[1,4,5248]{2,1,0:T(4,128)S(1)}, u32[]{:S(2)}, u32[]{:S(2)}) collective-permute-start(f32[1,4,5248]{2,1,0:T(4,128)S(1)} %broadcast_multiply_fusion.2), channel_id=1, source_target_pairs={{0,32},{32,64},{64,96},{96,128},{128,160},{160,192},{192,224},{224... | collective-permute-start | bytes 251912 | tf_op jit(solution)/shard_map/ppermute | solution.py:23
  59.6 4.1 %collective-permute-done.6 = f32[1,4,5248]{2,1,0:T(4,128)S(1)} collective-permute-done((f32[1,4,5248]{2,1,0:T(4,128)S(1)}, f32[1,4,5248]{2,1,0:T(4,128)S(1)}, u32[]{:S(2)}, u32[]{:S(2)}) %collective-permute-start.6) | collective-permute-done | bytes 84000 | tf_op jit(solution)/shard_map/ppermute | solution.py:23
  63.9 6.6 %collective-permute-done.13 = f32[1,4,5248]{2,1,0:T(4,128)S(1)} collective-permute-done((f32[1,4,5248]{2,1,0:T(4,128)S(1)}, f32[1,4,5248]{2,1,0:T(4,128)S(1)}, u32[]{:S(2)}, u32[]{:S(2)}) %collective-permute-start.13) | collective-permute-done | bytes 84000 | tf_op jit(solution)/shard_map/ppermute | solution.py:23
  70.6 6.0 %collective-permute-done.20 = f32[1,4,5248]{2,1,0:T(4,128)S(1)} collective-permute-done((f32[1,4,5248]{2,1,0:T(4,128)S(1)}, f32[1,4,5248]{2,1,0:T(4,128)S(1)}, u32[]{:S(2)}, u32[]{:S(2)}) %collective-permute-start.20) | collective-permute-done | bytes 84000 | tf_op jit(solution)/shard_map/ppermute | solution.py:23
  77.1 1.3 %divide_subtract_fusion = f32[1,4,5120]{2,1,0:T(4,128)} fusion(f32[1,4,5120]{2,1,0:T(4,128)S(1)} %copy-done, f32[1,4,5248]{2,1,0:T(4,128)S(1)} %multiply_add_fusion, f32[]{:T(128)} %bitcast.45, f32[]{:T(128)} %bitcast.12), kind=kLoop, calls=%fused_computation.19 | loop fusion | flops 61440 | bytes 245768 | tf_op jit(solution)/shard_map/sub | solution.py:124
  (54 shorter events, 5.4 us)
Async XLA Ops:
  2.4 4.9 %collective-permute-start.1 = (f32[2,16,5120]{2,1,0:T(8,128)S(1)}, f32[2,16,5120]{2,1,0:T(8,128)S(1)}, u32[]{:S(2)}, u32[]{:S(2)}) collective-permute-start(f32[2,16,5120]{2,1,0:T(8,128)S(1)} %get-tuple-element.18), channel_id=1, source_target_pairs={{0,1},{1,0},{2,3},{3,2},{4,5},{5,4},{6,7},{7,6},{8,9},{9,8},{10,11... | collective-permute-start | bytes 1966088 | tf_op jit(solution)/shard_map/ppermute | solution.py:23
  4.4 6.2 %collective-permute-start.8 = (f32[2,16,5120]{2,1,0:T(8,128)S(1)}, f32[2,16,5120]{2,1,0:T(8,128)S(1)}, u32[]{:S(2)}, u32[]{:S(2)}) collective-permute-start(f32[2,16,5120]{2,1,0:T(8,128)S(1)} %get-tuple-element.22), channel_id=1, source_target_pairs={{0,1},{1,0},{2,3},{3,2},{4,5},{5,4},{6,7},{7,6},{8,9},{9,8},{10,11... | collective-permute-start | bytes 1966088 | tf_op jit(solution)/shard_map/ppermute | solution.py:23
  6.7 4.0 %collective-permute-start.15 = (f32[2,16,5120]{2,1,0:T(8,128)S(1)}, f32[2,16,5120]{2,1,0:T(8,128)S(1)}, u32[]{:S(2)}, u32[]{:S(2)}) collective-permute-start(f32[2,16,5120]{2,1,0:T(8,128)S(1)} %get-tuple-element.26), channel_id=1, source_target_pairs={{0,1},{1,0},{2,3},{3,2},{4,5},{5,4},{6,7},{7,6},{8,9},{9,8},{10,11... | collective-permute-start | bytes 1966088 | tf_op jit(solution)/shard_map/ppermute | solution.py:23
  6.8 4.8 %collective-permute-start = (f32[2,16,5120]{2,1,0:T(8,128)S(1)}, f32[2,16,5120]{2,1,0:T(8,128)S(1)}, u32[]{:S(2)}, u32[]{:S(2)}) collective-permute-start(f32[2,16,5120]{2,1,0:T(8,128)S(1)} %get-tuple-element.16), channel_id=1, source_target_pairs={{0,1},{1,0},{2,3},{3,2},{4,5},{5,4},{6,7},{7,6},{8,9},{9,8},{10,11... | collective-permute-start | bytes 1966088 | tf_op jit(solution)/shard_map/ppermute | solution.py:23
  7.4 10.7 %collective-permute-start.2 = (f32[2,16,5120]{2,1,0:T(8,128)S(1)}, f32[2,16,5120]{2,1,0:T(8,128)S(1)}, u32[]{:S(2)}, u32[]{:S(2)}) collective-permute-start(f32[2,16,5120]{2,1,0:T(8,128)S(1)} %add.90), channel_id=1, source_target_pairs={{0,8},{1,25},{2,10},{3,27},{4,12},{5,29},{6,14},{7,31},{8,0},{9,17... | collective-permute-start | bytes 1966088 | tf_op jit(solution)/shard_map/ppermute | solution.py:38
  8.2 13.3 %collective-permute-start.7 = (f32[2,16,5120]{2,1,0:T(8,128)S(1)}, f32[2,16,5120]{2,1,0:T(8,128)S(1)}, u32[]{:S(2)}, u32[]{:S(2)}) collective-permute-start(f32[2,16,5120]{2,1,0:T(8,128)S(1)} %get-tuple-element.20), channel_id=1, source_target_pairs={{0,1},{1,0},{2,3},{3,2},{4,5},{5,4},{6,7},{7,6},{8,9},{9,8},{10,11... | collective-permute-start | bytes 1966088 | tf_op jit(solution)/shard_map/ppermute | solution.py:23
  10.6 18.0 %collective-permute-start.14 = (f32[2,16,5120]{2,1,0:T(8,128)S(1)}, f32[2,16,5120]{2,1,0:T(8,128)S(1)}, u32[]{:S(2)}, u32[]{:S(2)}) collective-permute-start(f32[2,16,5120]{2,1,0:T(8,128)S(1)} %get-tuple-element.24), channel_id=1, source_target_pairs={{0,1},{1,0},{2,3},{3,2},{4,5},{5,4},{6,7},{7,6},{8,9},{9,8},{10,11... | collective-permute-start | bytes 1966088 | tf_op jit(solution)/shard_map/ppermute | solution.py:23
  10.8 14.3 %collective-permute-start.9 = (f32[2,16,5120]{2,1,0:T(8,128)S(1)}, f32[2,16,5120]{2,1,0:T(8,128)S(1)}, u32[]{:S(2)}, u32[]{:S(2)}) collective-permute-start(f32[2,16,5120]{2,1,0:T(8,128)S(1)} %add.99), channel_id=1, source_target_pairs={{0,8},{1,25},{2,10},{3,27},{4,12},{5,29},{6,14},{7,31},{8,0},{9,17... | collective-permute-start | bytes 1966088 | tf_op jit(solution)/shard_map/ppermute | solution.py:38
  11.7 20.4 %collective-permute-start.16 = (f32[2,16,5120]{2,1,0:T(8,128)S(1)}, f32[2,16,5120]{2,1,0:T(8,128)S(1)}, u32[]{:S(2)}, u32[]{:S(2)}) collective-permute-start(f32[2,16,5120]{2,1,0:T(8,128)S(1)} %add.108), channel_id=1, source_target_pairs={{0,8},{1,25},{2,10},{3,27},{4,12},{5,29},{6,14},{7,31},{8,0},{9,17... | collective-permute-start | bytes 1966088 | tf_op jit(solution)/shard_map/ppermute | solution.py:38
  18.1 37.6 %copy-start.1 = (f32[1,4,5120]{2,1,0:T(4,128)S(1)}, f32[1,4,5120]{2,1,0:T(4,128)}, u32[]{:S(2)}) copy-start(f32[1,4,5120]{2,1,0:T(4,128)} %param.8) | copy-start | bytes 245764
  18.1 37.6 %copy-start = (f32[1,4,5120]{2,1,0:T(4,128)S(1)}, f32[1,4,5120]{2,1,0:T(4,128)}, u32[]{:S(2)}) copy-start(f32[1,4,5120]{2,1,0:T(4,128)} %param.5) | copy-start | bytes 245764
  18.2 17.4 %collective-permute-start.3 = (f32[2,8,5120]{2,1,0:T(8,128)S(1)}, f32[2,8,5120]{2,1,0:T(8,128)S(1)}, u32[]{:S(2)}, u32[]{:S(2)}) collective-permute-start(f32[2,8,5120]{2,1,0:T(8,128)S(1)} %slice.81), channel_id=1, source_target_pairs={{0,2},{1,7},{2,0},{3,5},{4,6},{5,3},{6,4},{7,1},{8,10},{9,15},{10,... | collective-permute-start | bytes 983048 | tf_op jit(solution)/shard_map/ppermute | solution.py:38
  25.2 13.0 %collective-permute-start.10 = (f32[2,8,5120]{2,1,0:T(8,128)S(1)}, f32[2,8,5120]{2,1,0:T(8,128)S(1)}, u32[]{:S(2)}, u32[]{:S(2)}) collective-permute-start(f32[2,8,5120]{2,1,0:T(8,128)S(1)} %slice.87), channel_id=1, source_target_pairs={{0,2},{1,7},{2,0},{3,5},{4,6},{5,3},{6,4},{7,1},{8,10},{9,15},{10,... | collective-permute-start | bytes 983048 | tf_op jit(solution)/shard_map/ppermute | solution.py:38
  32.2 10.6 %collective-permute-start.17 = (f32[2,8,5120]{2,1,0:T(8,128)S(1)}, f32[2,8,5120]{2,1,0:T(8,128)S(1)}, u32[]{:S(2)}, u32[]{:S(2)}) collective-permute-start(f32[2,8,5120]{2,1,0:T(8,128)S(1)} %slice.93), channel_id=1, source_target_pairs={{0,2},{1,7},{2,0},{3,5},{4,6},{5,3},{6,4},{7,1},{8,10},{9,15},{10,... | collective-permute-start | bytes 983048 | tf_op jit(solution)/shard_map/ppermute | solution.py:38
  35.7 10.9 %collective-permute-start.4 = (f32[8,5120]{1,0:T(8,128)S(1)}, f32[8,5120]{1,0:T(8,128)S(1)}, u32[]{:S(2)}, u32[]{:S(2)}) collective-permute-start(f32[8,5120]{1,0:T(8,128)S(1)} %slice_bitcast_fusion.4), channel_id=1, source_target_pairs={{0,24},{1,9},{2,26},{3,11},{4,28},{5,13},{6,30},{7,15},{8,16},{9,1... | collective-permute-start | bytes 491528 | tf_op jit(solution)/shard_map/ppermute | solution.py:38
  38.2 11.0 %collective-permute-start.11 = (f32[8,5120]{1,0:T(8,128)S(1)}, f32[8,5120]{1,0:T(8,128)S(1)}, u32[]{:S(2)}, u32[]{:S(2)}) collective-permute-start(f32[8,5120]{1,0:T(8,128)S(1)} %slice_bitcast_fusion.2), channel_id=1, source_target_pairs={{0,24},{1,9},{2,26},{3,11},{4,28},{5,13},{6,30},{7,15},{8,16},{9,1... | collective-permute-start | bytes 491528 | tf_op jit(solution)/shard_map/ppermute | solution.py:38
  42.9 8.1 %collective-permute-start.18 = (f32[8,5120]{1,0:T(8,128)S(1)}, f32[8,5120]{1,0:T(8,128)S(1)}, u32[]{:S(2)}, u32[]{:S(2)}) collective-permute-start(f32[8,5120]{1,0:T(8,128)S(1)} %slice_bitcast_fusion), channel_id=1, source_target_pairs={{0,24},{1,9},{2,26},{3,11},{4,28},{5,13},{6,30},{7,15},{8,16},{9,1... | collective-permute-start | bytes 491528 | tf_op jit(solution)/shard_map/ppermute | solution.py:38
  46.6 9.0 %collective-permute-start.5 = (f32[4,5120]{1,0:T(4,128)S(1)}, f32[4,5120]{1,0:T(4,128)S(1)}, u32[]{:S(2)}, u32[]{:S(2)}) collective-permute-start(f32[4,5120]{1,0:T(4,128)S(1)} %slice.85), channel_id=1, source_target_pairs={{0,6},{1,3},{2,4},{3,1},{4,2},{5,7},{6,0},{7,5},{8,14},{9,11},{10,... | collective-permute-start | bytes 245768 | tf_op jit(solution)/shard_map/ppermute | solution.py:38
  49.3 9.2 %collective-permute-start.12 = (f32[4,5120]{1,0:T(4,128)S(1)}, f32[4,5120]{1,0:T(4,128)S(1)}, u32[]{:S(2)}, u32[]{:S(2)}) collective-permute-start(f32[4,5120]{1,0:T(4,128)S(1)} %slice.91), channel_id=1, source_target_pairs={{0,6},{1,3},{2,4},{3,1},{4,2},{5,7},{6,0},{7,5},{8,14},{9,11},{10,... | collective-permute-start | bytes 245768 | tf_op jit(solution)/shard_map/ppermute | solution.py:38
  51.0 7.9 %collective-permute-start.19 = (f32[4,5120]{1,0:T(4,128)S(1)}, f32[4,5120]{1,0:T(4,128)S(1)}, u32[]{:S(2)}, u32[]{:S(2)}) collective-permute-start(f32[4,5120]{1,0:T(4,128)S(1)} %slice.97), channel_id=1, source_target_pairs={{0,6},{1,3},{2,4},{3,1},{4,2},{5,7},{6,0},{7,5},{8,14},{9,11},{10,... | collective-permute-start | bytes 245768 | tf_op jit(solution)/shard_map/ppermute | solution.py:38
  55.7 8.0 %collective-permute-start.6 = (f32[1,4,5248]{2,1,0:T(4,128)S(1)}, f32[1,4,5248]{2,1,0:T(4,128)S(1)}, u32[]{:S(2)}, u32[]{:S(2)}) collective-permute-start(f32[1,4,5248]{2,1,0:T(4,128)S(1)} %broadcast_multiply_fusion.2), channel_id=1, source_target_pairs={{0,32},{32,64},{64,96},{96,128},{128,160},{160,192},{192,224},{224... | collective-permute-start | bytes 251912 | tf_op jit(solution)/shard_map/ppermute | solution.py:23
  63.8 6.7 %collective-permute-start.13 = (f32[1,4,5248]{2,1,0:T(4,128)S(1)}, f32[1,4,5248]{2,1,0:T(4,128)S(1)}, u32[]{:S(2)}, u32[]{:S(2)}) collective-permute-start(f32[1,4,5248]{2,1,0:T(4,128)S(1)} %get-tuple-element.27), channel_id=1, source_target_pairs={{0,64},{32,96},{64,128},{96,160},{128,192},{160,224},{192,0},{224,... | collective-permute-start | bytes 251912 | tf_op jit(solution)/shard_map/ppermute | solution.py:23
  70.5 6.1 %collective-permute-start.20 = (f32[1,4,5248]{2,1,0:T(4,128)S(1)}, f32[1,4,5248]{2,1,0:T(4,128)S(1)}, u32[]{:S(2)}, u32[]{:S(2)}) collective-permute-start(f32[1,4,5248]{2,1,0:T(4,128)S(1)} %broadcast_multiply_fusion), channel_id=1, source_target_pairs={{0,128},{32,160},{64,192},{96,224},{128,0},{160,32},{192,64},{224,... | collective-permute-start | bytes 251912 | tf_op jit(solution)/shard_map/ppermute | solution.py:23

commit v5 on v4

--- a/solution.py
+++ b/solution.py
@@ -51,7 +51,8 @@
 OTHERS = (0, 2, 1, 3)
 
 
-def split_kernel(step, g_ref, other_send, own_send, other_keep, own_keep, block, arrived):
+def split_kernel(step, g_ref, *refs):
+    other_send, own_send, other_keep, own_keep, block, arrived = refs[-6:]
     core = lax.axis_index("core")
     y_at = places(lax.axis_index("y"), core)
     z_at = places(lax.axis_index("zh"), core)
@@ -82,46 +83,104 @@
                 other[OTHERS[q] % 2, rows, columns] = jnp.where(row < 4, low[m], top[m + 2])
 
 
-def split_cores(grads, step):
+def split_cores(grads, step, after):
     shape = pltpu.VMEM((2, 16, D), jnp.float32)
     return pl.pallas_call(
         functools.partial(split_kernel, step),
         out_shape=(shape,) * 4,
-        in_specs=[pl.BlockSpec(memory_space=pltpu.HBM)],
+        in_specs=[pl.BlockSpec(memory_space=pltpu.HBM)]
+        + [pl.BlockSpec(memory_space=pl.ANY)] * len(after),
         out_specs=[pl.BlockSpec(memory_space=pltpu.VMEM)] * 4,
         scratch_shapes=[pltpu.VMEM((Y, 32, D), jnp.float32), pltpu.SemaphoreType.DMA((Y,))],
         compiler_params=pltpu.CompilerParams(vmem_limit_bytes=16 << 20),
         cost_estimate=pl.CostEstimate(flops=0, bytes_accessed=8 * 16 * D * 4, transcendentals=0),
-    )(pltpu.with_memory_space_constraint(grads, pltpu.HBM))
-
-
-def shard_mean(grads, step):
-    other_send, own_send, other_keep, own_keep = split_cores(grads, step)
-    send = own_send + ring(other_send, "core", 1)
-    keep = own_keep + ring(other_keep, "core", 1)
-    rows = keep + swap(send, "y", 0)
-    rows = rows[:, :8] + swap(rows[:, 8:], "zh", 0)
-    rows = rows[0] + swap(rows[1], "y", 1)
-    rows = rows[:4] + swap(rows[4:], "zh", 1)
-    return (rows / (Y * ZH * CORE))[None]
+    )(pltpu.with_memory_space_constraint(grads, pltpu.HBM), *after)
 
 
 def per_device(numerators, push_weight, keep_share, momentum, grads):
-    levels = (X * ZL).bit_length() - 1
-    means = [shard_mean(grads, step) for step in range(STEPS)]
+    keep_rows = keep_share[:, None, None]
     weight = jnp.broadcast_to(push_weight[:, None, None], (1, 4, 128))
     values = jnp.concatenate([numerators, weight], axis=2)
+    start = numerators / push_weight[:, None, None]
     buffer = momentum
-    keep_rows = keep_share[:, None, None]
-    for step in range(STEPS):
-        mean = means[step]
-        buffer = momentum_factor * buffer + mean
-        moved = learn_rate * (mean + momentum_factor * buffer)
-        values = values - jnp.pad(moved, ((0, 0), (0, 0), (0, 128)))
-        sent = ring((1.0 - keep_rows) * values, GROUP, 1 << step % levels)
-        values = keep_rows * values + sent
+    other_0, own_0, otherk_0, ownk_0 = split_cores(grads, 0, ())
+    come_C0 = ring(other_0, "core", 1)
+    sent_0 = own_0 + come_C0
+    kept_0 = ownk_0 + ring(otherk_0, "core", 1)
+    other_1, own_1, otherk_1, ownk_1 = split_cores(grads, 1, ())
+    come_C1 = ring(other_1, "core", 1)
+    sent_1 = own_1 + come_C1
+    kept_1 = ownk_1 + ring(otherk_1, "core", 1)
+    other_2, own_2, otherk_2, ownk_2 = split_cores(grads, 2, ())
+    come_C2 = ring(other_2, "core", 1)
+    sent_2 = own_2 + come_C2
+    kept_2 = ownk_2 + ring(otherk_2, "core", 1)
+    ready_Y0 = sent_0
+    come_Y0 = swap(ready_Y0, "y", 0)
+    rows_0 = kept_0 + come_Y0
+    ready_Y1 = sent_1
+    come_Y1 = swap(ready_Y1, "y", 0)
+    rows_1 = kept_1 + come_Y1
+    ready_Y2 = sent_2
+    come_Y2 = swap(ready_Y2, "y", 0)
+    rows_2 = kept_2 + come_Y2
+    ready_Z0 = rows_0[..., 8:, :]
+    come_Z0 = swap(ready_Z0, "zh", 0)
+    rows_0 = rows_0[..., :8, :] + come_Z0
+    ready_Z1 = rows_1[..., 8:, :]
+    come_Z1 = swap(ready_Z1, "zh", 0)
+    rows_1 = rows_1[..., :8, :] + come_Z1
+    ready_YY2 = rows_2[1]
+    come_YY2 = swap(ready_YY2, "y", 1)
+    rows_2 = rows_2[0] + come_YY2
+    ready_YY0 = rows_0[1]
+    come_YY0 = swap(ready_YY0, "y", 1)
+    rows_0 = rows_0[0] + come_YY0
+    ready_YY1 = rows_1[1]
+    come_YY1 = swap(ready_YY1, "y", 1)
+    rows_1 = rows_1[0] + come_YY1
+    ready_Z2 = rows_2[..., 8:, :]
+    come_Z2 = swap(ready_Z2, "zh", 0)
+    rows_2 = rows_2[..., :8, :] + come_Z2
+    ready_ZZ0 = rows_0[..., 4:, :]
+    come_ZZ0 = swap(ready_ZZ0, "zh", 1)
+    rows_0 = rows_0[..., :4, :] + come_ZZ0
+    ready_ZZ1 = rows_1[..., 4:, :]
+    come_ZZ1 = swap(ready_ZZ1, "zh", 1)
+    rows_1 = rows_1[..., :4, :] + come_ZZ1
+    mean = (rows_0 / (Y * ZH * CORE))[None]
+    buffer = momentum_factor * buffer + mean
+    moved = learn_rate * (mean + momentum_factor * buffer)
+    values = values - jnp.pad(moved, ((0, 0), (0, 0), (0, 128)))
+    pushed = (1.0 - keep_rows) * values
+    pushed, buffer, values = lax.optimization_barrier((pushed, buffer, values))
+    ready_M0 = pushed
+    come_M0 = ring(pushed, GROUP, 1)
+    values = keep_rows * values + come_M0
+    mean = (rows_1 / (Y * ZH * CORE))[None]
+    buffer = momentum_factor * buffer + mean
+    moved = learn_rate * (mean + momentum_factor * buffer)
+    values = values - jnp.pad(moved, ((0, 0), (0, 0), (0, 128)))
+    pushed = (1.0 - keep_rows) * values
+    pushed, buffer, values = lax.optimization_barrier((pushed, buffer, values))
+    ready_M1 = pushed
+    come_M1 = ring(pushed, GROUP, 2)
+    values = keep_rows * values + come_M1
+    ready_ZZ2 = rows_2[..., 4:, :]
+    ready_ZZ2, *_ = lax.optimization_barrier((ready_ZZ2, ready_M0))
+    come_ZZ2 = swap(ready_ZZ2, "zh", 1)
+    rows_2 = rows_2[..., :4, :] + come_ZZ2
+    mean = (rows_2 / (Y * ZH * CORE))[None]
+    buffer = momentum_factor * buffer + mean
+    moved = learn_rate * (mean + momentum_factor * buffer)
+    values = values - jnp.pad(moved, ((0, 0), (0, 0), (0, 128)))
+    pushed = (1.0 - keep_rows) * values
+    pushed, buffer, values = lax.optimization_barrier((pushed, buffer, values))
+    ready_M2 = pushed
+    come_M2 = ring(pushed, GROUP, 4)
+    values = keep_rows * values + come_M2
     weight = values[:, 0, D]
-    displacement = values[:, :, :D] / weight[:, None, None] - numerators / push_weight[:, None, None]
+    displacement = values[:, :, :D] / values[:, :, D : D + 1] - start
     return (displacement, buffer, weight)
 
 

time: 78.6 us -> 73 us (0.929)
  waiting for transfers between devices: 35.1 us -> 25 us
  starting transfers between devices: 32.2 us -> 36.6 us
    ppermute x9, waiting for transfers between devices: 16.7 us -> 6.05 us  [ring(): return lax.ppermute(x, axis, [(i, (i + by) % n) for i in range(n)])]
    ppermute x9, starting transfers between devices: 5.28 us -> 8.54 us  [ring(): return lax.ppermute(x, axis, [(i, (i + by) % n) for i in range(n)])]
    ppermute x12, starting transfers between devices: 26.9 us -> 28.1 us  [swap(): return lax.ppermute(x, SHARD, pairs)]
where the time goes in v5:
time: 73 us; the launch traced here: 72.3 us
  starting transfers between devices  36.6 us (50%)
  waiting for transfers between devices  25 us (34%)
  Pallas kernels  5.4 us (7%)
  other arithmetic  2.36 us (3%)
  between operations  2.17 us (3%)
  local copies, waits for them, and re-layouts  0.8 us (1%)
    ppermute x12, starting transfers between devices, swap(): return lax.ppermute(x, SHARD, pairs)  28.1 us
    ppermute x12, waiting for transfers between devices, swap(): return lax.ppermute(x, SHARD, pairs)  18.9 us
    ppermute x9, starting transfers between devices, ring(): return lax.ppermute(x, axis, [(i, (i + by) % n) for i in range(n)])  8.54 us
    ppermute x9, waiting for transfers between devices, ring(): return lax.ppermute(x, axis, [(i, (i + by) % n) for i in range(n)])  6.05 us
    pallas_call x3, Pallas kernels, split_cores(): pl.pallas_call(functools.partial(split_kernel, step), out_shape=(shape,)...  5.4 us
  transfers between devices with their start and end apart: 21, of which 9 were waited for; matrix products, arithmetic and copies ran while one was open for 2% of the time, Pallas kernels for 5%

profile of v5, /device:TPU:24, one launch (start us, length us, event | category | flops | bytes accessed | tf_op | source)
XLA Modules:
  0.0 72.3 jit_solution(9324081716027540934)
XLA Ops:
  0.6 1.8 %shard_map.76 = (f32[2,16,5120]{2,1,0:T(8,128)S(1)}, f32[2,16,5120]{2,1,0:T(8,128)S(1)}, f32[2,16,5120]{2,1,0:T(8,128)S(1)}, f32[2,16,5120]{2,1,0:T(8,128)S(1)}) custom-call(f32[3,1,1,128,5120]{4,3,2,1,0:T(8,128)} %g_ref.5), custom_call_target="tpu_custom_call" | custom-call | bytes 2621440 | tf_op jit(solution)/shard_map/pallas_call | solution.py:88
  2.5 1.8 %shard_map.77 = (f32[2,16,5120]{2,1,0:T(8,128)S(1)}, f32[2,16,5120]{2,1,0:T(8,128)S(1)}, f32[2,16,5120]{2,1,0:T(8,128)S(1)}, f32[2,16,5120]{2,1,0:T(8,128)S(1)}) custom-call(f32[3,1,1,128,5120]{4,3,2,1,0:T(8,128)} %g_ref.5), custom_call_target="tpu_custom_call" | custom-call | bytes 2621440 | tf_op jit(solution)/shard_map/pallas_call | solution.py:88
  4.9 1.8 %shard_map.78 = (f32[2,16,5120]{2,1,0:T(8,128)S(1)}, f32[2,16,5120]{2,1,0:T(8,128)S(1)}, f32[2,16,5120]{2,1,0:T(8,128)S(1)}, f32[2,16,5120]{2,1,0:T(8,128)S(1)}) custom-call(f32[3,1,1,128,5120]{4,3,2,1,0:T(8,128)} %g_ref.5), custom_call_target="tpu_custom_call" | custom-call | bytes 2621440 | tf_op jit(solution)/shard_map/pallas_call | solution.py:88
  8.2 1.0 %collective-permute-start.7 = (f32[2,16,5120]{2,1,0:T(8,128)S(1)}, f32[2,16,5120]{2,1,0:T(8,128)S(1)}, u32[]{:S(2)}, u32[]{:S(2)}) collective-permute-start(f32[2,16,5120]{2,1,0:T(8,128)S(1)} %get-tuple-element.32), channel_id=1, source_target_pairs={{0,1},{1,0},{2,3},{3,2},{4,5},{5,4},{6,7},{7,6},{8,9},{9,8},{10,11... | collective-permute-start | bytes 1966088 | tf_op jit(solution)/shard_map/ppermute | solution.py:23
  11.7 1.4 %collective-permute-start.16 = (f32[2,16,5120]{2,1,0:T(8,128)S(1)}, f32[2,16,5120]{2,1,0:T(8,128)S(1)}, u32[]{:S(2)}, u32[]{:S(2)}) collective-permute-start(f32[2,16,5120]{2,1,0:T(8,128)S(1)} %add.108), channel_id=1, source_target_pairs={{0,8},{1,25},{2,10},{3,27},{4,12},{5,29},{6,14},{7,31},{8,0},{9,17... | collective-permute-start | bytes 1966088 | tf_op jit(solution)/shard_map/ppermute | solution.py:38
  13.0 5.0 %collective-permute-done.2 = f32[2,16,5120]{2,1,0:T(8,128)S(1)} collective-permute-done((f32[2,16,5120]{2,1,0:T(8,128)S(1)}, f32[2,16,5120]{2,1,0:T(8,128)S(1)}, u32[]{:S(2)}, u32[]{:S(2)}) %collective-permute-start.2) | collective-permute-done | bytes 655392 | tf_op jit(solution)/shard_map/ppermute | solution.py:38
  18.2 3.4 %collective-permute-start.3 = (f32[2,8,5120]{2,1,0:T(8,128)S(1)}, f32[2,8,5120]{2,1,0:T(8,128)S(1)}, u32[]{:S(2)}, u32[]{:S(2)}) collective-permute-start(f32[2,8,5120]{2,1,0:T(8,128)S(1)} %slice.85), channel_id=1, source_target_pairs={{0,2},{1,7},{2,0},{3,5},{4,6},{5,3},{6,4},{7,1},{8,10},{9,15},{10,... | collective-permute-start | bytes 983048 | tf_op jit(solution)/shard_map/ppermute | solution.py:38
  21.6 3.5 %collective-permute-done.9 = f32[2,16,5120]{2,1,0:T(8,128)S(1)} collective-permute-done((f32[2,16,5120]{2,1,0:T(8,128)S(1)}, f32[2,16,5120]{2,1,0:T(8,128)S(1)}, u32[]{:S(2)}, u32[]{:S(2)}) %collective-permute-start.9) | collective-permute-done | bytes 655392 | tf_op jit(solution)/shard_map/ppermute | solution.py:38
  25.2 3.4 %collective-permute-start.10 = (f32[2,8,5120]{2,1,0:T(8,128)S(1)}, f32[2,8,5120]{2,1,0:T(8,128)S(1)}, u32[]{:S(2)}, u32[]{:S(2)}) collective-permute-start(f32[2,8,5120]{2,1,0:T(8,128)S(1)} %slice.91), channel_id=1, source_target_pairs={{0,2},{1,7},{2,0},{3,5},{4,6},{5,3},{6,4},{7,1},{8,10},{9,15},{10,... | collective-permute-start | bytes 983048 | tf_op jit(solution)/shard_map/ppermute | solution.py:38
  28.6 3.5 %collective-permute-done.16 = f32[2,16,5120]{2,1,0:T(8,128)S(1)} collective-permute-done((f32[2,16,5120]{2,1,0:T(8,128)S(1)}, f32[2,16,5120]{2,1,0:T(8,128)S(1)}, u32[]{:S(2)}, u32[]{:S(2)}) %collective-permute-start.16) | collective-permute-done | bytes 655392 | tf_op jit(solution)/shard_map/ppermute | solution.py:38
  32.2 2.0 %collective-permute-start.17 = (f32[16,5120]{1,0:T(8,128)S(1)}, f32[16,5120]{1,0:T(8,128)S(1)}, u32[]{:S(2)}, u32[]{:S(2)}) collective-permute-start(f32[16,5120]{1,0:T(8,128)S(1)} %slice_bitcast_fusion), channel_id=1, source_target_pairs={{0,24},{1,9},{2,26},{3,11},{4,28},{5,13},{6,30},{7,15},{8,16},{9,1... | collective-permute-start | bytes 983048 | tf_op jit(solution)/shard_map/ppermute | solution.py:38
  34.3 1.4 %collective-permute-start.4 = (f32[8,5120]{1,0:T(8,128)S(1)}, f32[8,5120]{1,0:T(8,128)S(1)}, u32[]{:S(2)}, u32[]{:S(2)}) collective-permute-start(f32[8,5120]{1,0:T(8,128)S(1)} %slice_bitcast_fusion.4), channel_id=1, source_target_pairs={{0,24},{1,9},{2,26},{3,11},{4,28},{5,13},{6,30},{7,15},{8,16},{9,1... | collective-permute-start | bytes 491528 | tf_op jit(solution)/shard_map/ppermute | solution.py:38
  35.7 2.5 %collective-permute-done.10 = f32[2,8,5120]{2,1,0:T(8,128)S(1)} collective-permute-done((f32[2,8,5120]{2,1,0:T(8,128)S(1)}, f32[2,8,5120]{2,1,0:T(8,128)S(1)}, u32[]{:S(2)}, u32[]{:S(2)}) %collective-permute-start.10) | collective-permute-done | bytes 327712 | tf_op jit(solution)/shard_map/ppermute | solution.py:38
  38.6 2.0 %collective-permute-done.17 = f32[16,5120]{1,0:T(8,128)S(1)} collective-permute-done((f32[16,5120]{1,0:T(8,128)S(1)}, f32[16,5120]{1,0:T(8,128)S(1)}, u32[]{:S(2)}, u32[]{:S(2)}) %collective-permute-start.17) | collective-permute-done | bytes 327712 | tf_op jit(solution)/shard_map/ppermute | solution.py:38
  40.7 3.4 %collective-permute-start.18 = (f32[8,5120]{1,0:T(8,128)S(1)}, f32[8,5120]{1,0:T(8,128)S(1)}, u32[]{:S(2)}, u32[]{:S(2)}) collective-permute-start(f32[8,5120]{1,0:T(8,128)S(1)} %slice.99), channel_id=1, source_target_pairs={{0,2},{1,7},{2,0},{3,5},{4,6},{5,3},{6,4},{7,1},{8,10},{9,15},{10,... | collective-permute-start | bytes 491528 | tf_op jit(solution)/shard_map/ppermute | solution.py:38
  44.1 4.7 %collective-permute-start.5 = (f32[4,5120]{1,0:T(4,128)S(1)}, f32[4,5120]{1,0:T(4,128)S(1)}, u32[]{:S(2)}, u32[]{:S(2)}) collective-permute-start(f32[4,5120]{1,0:T(4,128)S(1)} %slice.89), channel_id=1, source_target_pairs={{0,6},{1,3},{2,4},{3,1},{4,2},{5,7},{6,0},{7,5},{8,14},{9,11},{10,... | collective-permute-start | bytes 245768 | tf_op jit(solution)/shard_map/ppermute | solution.py:38
  48.9 1.7 %collective-permute-start.12 = (f32[4,5120]{1,0:T(4,128)S(1)}, f32[4,5120]{1,0:T(4,128)S(1)}, u32[]{:S(2)}, u32[]{:S(2)}) collective-permute-start(f32[4,5120]{1,0:T(4,128)S(1)} %slice.95), channel_id=1, source_target_pairs={{0,6},{1,3},{2,4},{3,1},{4,2},{5,7},{6,0},{7,5},{8,14},{9,11},{10,... | collective-permute-start | bytes 245768 | tf_op jit(solution)/shard_map/ppermute | solution.py:38
  51.5 2.7 %collective-permute-start.6 = (f32[1,4,5248]{2,1,0:T(4,128)S(1)}, f32[1,4,5248]{2,1,0:T(4,128)S(1)}, u32[]{:S(2)}, u32[]{:S(2)}) collective-permute-start(f32[1,4,5248]{2,1,0:T(4,128)S(1)} %get-tuple-element.30), channel_id=1, source_target_pairs={{0,32},{32,64},{64,96},{96,128},{128,160},{160,192},{192,224},{224... | collective-permute-start | bytes 251912 | tf_op jit(solution)/shard_map/ppermute | solution.py:23
  54.2 4.8 %collective-permute-start.19 = (f32[4,5120]{1,0:T(4,128)S(1)}, f32[4,5120]{1,0:T(4,128)S(1)}, u32[]{:S(2)}, u32[]{:S(2)}) collective-permute-start(f32[4,5120]{1,0:T(4,128)S(1)} %slice.101), channel_id=1, source_target_pairs={{0,6},{1,3},{2,4},{3,1},{4,2},{5,7},{6,0},{7,5},{8,14},{9,11},{10,... | collective-permute-start | bytes 245768 | tf_op jit(solution)/shard_map/ppermute | solution.py:38
  59.1 1.6 %collective-permute-start.13 = (f32[1,4,5248]{2,1,0:T(4,128)S(1)}, f32[1,4,5248]{2,1,0:T(4,128)S(1)}, u32[]{:S(2)}, u32[]{:S(2)}) collective-permute-start(f32[1,4,5248]{2,1,0:T(4,128)S(1)} %get-tuple-element.37), channel_id=1, source_target_pairs={{0,64},{32,96},{64,128},{96,160},{128,192},{160,224},{192,0},{224,... | collective-permute-start | bytes 251912 | tf_op jit(solution)/shard_map/ppermute | solution.py:23
  60.7 1.6 %collective-permute-done.19 = f32[4,5120]{1,0:T(4,128)S(1)} collective-permute-done((f32[4,5120]{1,0:T(4,128)S(1)}, f32[4,5120]{1,0:T(4,128)S(1)}, u32[]{:S(2)}, u32[]{:S(2)}) %collective-permute-start.19) | collective-permute-done | bytes 81952 | tf_op jit(solution)/shard_map/ppermute | solution.py:38
  63.0 1.9 %collective-permute-done.13 = f32[1,4,5248]{2,1,0:T(4,128)S(1)} collective-permute-done((f32[1,4,5248]{2,1,0:T(4,128)S(1)}, f32[1,4,5248]{2,1,0:T(4,128)S(1)}, u32[]{:S(2)}, u32[]{:S(2)}) %collective-permute-start.13) | collective-permute-done | bytes 84000 | tf_op jit(solution)/shard_map/ppermute | solution.py:23
  64.9 1.9 %collective-permute-start.20 = (f32[1,4,5248]{2,1,0:T(4,128)S(1)}, f32[1,4,5248]{2,1,0:T(4,128)S(1)}, u32[]{:S(2)}, u32[]{:S(2)}) collective-permute-start(f32[1,4,5248]{2,1,0:T(4,128)S(1)} %get-tuple-element.45), channel_id=1, source_target_pairs={{0,128},{32,160},{64,192},{96,224},{128,0},{160,32},{192,64},{224,... | collective-permute-start | bytes 251912 | tf_op jit(solution)/shard_map/ppermute | solution.py:23
  66.8 4.2 %collective-permute-done.20 = f32[1,4,5248]{2,1,0:T(4,128)S(1)} collective-permute-done((f32[1,4,5248]{2,1,0:T(4,128)S(1)}, f32[1,4,5248]{2,1,0:T(4,128)S(1)}, u32[]{:S(2)}, u32[]{:S(2)}) %collective-permute-start.20) | collective-permute-done | bytes 84000 | tf_op jit(solution)/shard_map/ppermute | solution.py:23
  (56 shorter events, 7.4 us)
Async XLA Ops:
  2.4 4.9 %collective-permute-start.1 = (f32[2,16,5120]{2,1,0:T(8,128)S(1)}, f32[2,16,5120]{2,1,0:T(8,128)S(1)}, u32[]{:S(2)}, u32[]{:S(2)}) collective-permute-start(f32[2,16,5120]{2,1,0:T(8,128)S(1)} %get-tuple-element.28), channel_id=1, source_target_pairs={{0,1},{1,0},{2,3},{3,2},{4,5},{5,4},{6,7},{7,6},{8,9},{9,8},{10,11... | collective-permute-start | bytes 1966088 | tf_op jit(solution)/shard_map/ppermute | solution.py:23
  4.4 6.2 %collective-permute-start.8 = (f32[2,16,5120]{2,1,0:T(8,128)S(1)}, f32[2,16,5120]{2,1,0:T(8,128)S(1)}, u32[]{:S(2)}, u32[]{:S(2)}) collective-permute-start(f32[2,16,5120]{2,1,0:T(8,128)S(1)} %get-tuple-element.34), channel_id=1, source_target_pairs={{0,1},{1,0},{2,3},{3,2},{4,5},{5,4},{6,7},{7,6},{8,9},{9,8},{10,11... | collective-permute-start | bytes 1966088 | tf_op jit(solution)/shard_map/ppermute | solution.py:23
  6.7 4.0 %collective-permute-start.15 = (f32[2,16,5120]{2,1,0:T(8,128)S(1)}, f32[2,16,5120]{2,1,0:T(8,128)S(1)}, u32[]{:S(2)}, u32[]{:S(2)}) collective-permute-start(f32[2,16,5120]{2,1,0:T(8,128)S(1)} %get-tuple-element.41), channel_id=1, source_target_pairs={{0,1},{1,0},{2,3},{3,2},{4,5},{5,4},{6,7},{7,6},{8,9},{9,8},{10,11... | collective-permute-start | bytes 1966088 | tf_op jit(solution)/shard_map/ppermute | solution.py:23
  6.8 4.8 %collective-permute-start = (f32[2,16,5120]{2,1,0:T(8,128)S(1)}, f32[2,16,5120]{2,1,0:T(8,128)S(1)}, u32[]{:S(2)}, u32[]{:S(2)}) collective-permute-start(f32[2,16,5120]{2,1,0:T(8,128)S(1)} %get-tuple-element.26), channel_id=1, source_target_pairs={{0,1},{1,0},{2,3},{3,2},{4,5},{5,4},{6,7},{7,6},{8,9},{9,8},{10,11... | collective-permute-start | bytes 1966088 | tf_op jit(solution)/shard_map/ppermute | solution.py:23
  7.4 10.7 %collective-permute-start.2 = (f32[2,16,5120]{2,1,0:T(8,128)S(1)}, f32[2,16,5120]{2,1,0:T(8,128)S(1)}, u32[]{:S(2)}, u32[]{:S(2)}) collective-permute-start(f32[2,16,5120]{2,1,0:T(8,128)S(1)} %add.90), channel_id=1, source_target_pairs={{0,8},{1,25},{2,10},{3,27},{4,12},{5,29},{6,14},{7,31},{8,0},{9,17... | collective-permute-start | bytes 1966088 | tf_op jit(solution)/shard_map/ppermute | solution.py:38
  8.2 13.3 %collective-permute-start.7 = (f32[2,16,5120]{2,1,0:T(8,128)S(1)}, f32[2,16,5120]{2,1,0:T(8,128)S(1)}, u32[]{:S(2)}, u32[]{:S(2)}) collective-permute-start(f32[2,16,5120]{2,1,0:T(8,128)S(1)} %get-tuple-element.32), channel_id=1, source_target_pairs={{0,1},{1,0},{2,3},{3,2},{4,5},{5,4},{6,7},{7,6},{8,9},{9,8},{10,11... | collective-permute-start | bytes 1966088 | tf_op jit(solution)/shard_map/ppermute | solution.py:23
  10.6 18.0 %collective-permute-start.14 = (f32[2,16,5120]{2,1,0:T(8,128)S(1)}, f32[2,16,5120]{2,1,0:T(8,128)S(1)}, u32[]{:S(2)}, u32[]{:S(2)}) collective-permute-start(f32[2,16,5120]{2,1,0:T(8,128)S(1)} %get-tuple-element.39), channel_id=1, source_target_pairs={{0,1},{1,0},{2,3},{3,2},{4,5},{5,4},{6,7},{7,6},{8,9},{9,8},{10,11... | collective-permute-start | bytes 1966088 | tf_op jit(solution)/shard_map/ppermute | solution.py:23
  10.8 14.3 %collective-permute-start.9 = (f32[2,16,5120]{2,1,0:T(8,128)S(1)}, f32[2,16,5120]{2,1,0:T(8,128)S(1)}, u32[]{:S(2)}, u32[]{:S(2)}) collective-permute-start(f32[2,16,5120]{2,1,0:T(8,128)S(1)} %add.99), channel_id=1, source_target_pairs={{0,8},{1,25},{2,10},{3,27},{4,12},{5,29},{6,14},{7,31},{8,0},{9,17... | collective-permute-start | bytes 1966088 | tf_op jit(solution)/shard_map/ppermute | solution.py:38
  11.7 20.4 %collective-permute-start.16 = (f32[2,16,5120]{2,1,0:T(8,128)S(1)}, f32[2,16,5120]{2,1,0:T(8,128)S(1)}, u32[]{:S(2)}, u32[]{:S(2)}) collective-permute-start(f32[2,16,5120]{2,1,0:T(8,128)S(1)} %add.108), channel_id=1, source_target_pairs={{0,8},{1,25},{2,10},{3,27},{4,12},{5,29},{6,14},{7,31},{8,0},{9,17... | collective-permute-start | bytes 1966088 | tf_op jit(solution)/shard_map/ppermute | solution.py:38
  18.1 33.3 %copy-start.1 = (f32[1,4,5120]{2,1,0:T(4,128)S(1)}, f32[1,4,5120]{2,1,0:T(4,128)}, u32[]{:S(2)}) copy-start(f32[1,4,5120]{2,1,0:T(4,128)} %param.8) | copy-start | bytes 245764
  18.1 33.4 %copy-start = (f32[1,4,5120]{2,1,0:T(4,128)S(1)}, f32[1,4,5120]{2,1,0:T(4,128)}, u32[]{:S(2)}) copy-start(f32[1,4,5120]{2,1,0:T(4,128)} %param.5) | copy-start | bytes 245764
  18.2 16.1 %collective-permute-start.3 = (f32[2,8,5120]{2,1,0:T(8,128)S(1)}, f32[2,8,5120]{2,1,0:T(8,128)S(1)}, u32[]{:S(2)}, u32[]{:S(2)}) collective-permute-start(f32[2,8,5120]{2,1,0:T(8,128)S(1)} %slice.85), channel_id=1, source_target_pairs={{0,2},{1,7},{2,0},{3,5},{4,6},{5,3},{6,4},{7,1},{8,10},{9,15},{10,... | collective-permute-start | bytes 983048 | tf_op jit(solution)/shard_map/ppermute | solution.py:38
  25.2 13.0 %collective-permute-start.10 = (f32[2,8,5120]{2,1,0:T(8,128)S(1)}, f32[2,8,5120]{2,1,0:T(8,128)S(1)}, u32[]{:S(2)}, u32[]{:S(2)}) collective-permute-start(f32[2,8,5120]{2,1,0:T(8,128)S(1)} %slice.91), channel_id=1, source_target_pairs={{0,2},{1,7},{2,0},{3,5},{4,6},{5,3},{6,4},{7,1},{8,10},{9,15},{10,... | collective-permute-start | bytes 983048 | tf_op jit(solution)/shard_map/ppermute | solution.py:38
  32.2 8.4 %collective-permute-start.17 = (f32[16,5120]{1,0:T(8,128)S(1)}, f32[16,5120]{1,0:T(8,128)S(1)}, u32[]{:S(2)}, u32[]{:S(2)}) collective-permute-start(f32[16,5120]{1,0:T(8,128)S(1)} %slice_bitcast_fusion), channel_id=1, source_target_pairs={{0,24},{1,9},{2,26},{3,11},{4,28},{5,13},{6,30},{7,15},{8,16},{9,1... | collective-permute-start | bytes 983048 | tf_op jit(solution)/shard_map/ppermute | solution.py:38
  34.3 9.7 %collective-permute-start.4 = (f32[8,5120]{1,0:T(8,128)S(1)}, f32[8,5120]{1,0:T(8,128)S(1)}, u32[]{:S(2)}, u32[]{:S(2)}) collective-permute-start(f32[8,5120]{1,0:T(8,128)S(1)} %slice_bitcast_fusion.4), channel_id=1, source_target_pairs={{0,24},{1,9},{2,26},{3,11},{4,28},{5,13},{6,30},{7,15},{8,16},{9,1... | collective-permute-start | bytes 491528 | tf_op jit(solution)/shard_map/ppermute | solution.py:38
  38.2 10.6 %collective-permute-start.11 = (f32[8,5120]{1,0:T(8,128)S(1)}, f32[8,5120]{1,0:T(8,128)S(1)}, u32[]{:S(2)}, u32[]{:S(2)}) collective-permute-start(f32[8,5120]{1,0:T(8,128)S(1)} %slice_bitcast_fusion.2), channel_id=1, source_target_pairs={{0,24},{1,9},{2,26},{3,11},{4,28},{5,13},{6,30},{7,15},{8,16},{9,1... | collective-permute-start | bytes 491528 | tf_op jit(solution)/shard_map/ppermute | solution.py:38
  40.7 9.9 %collective-permute-start.18 = (f32[8,5120]{1,0:T(8,128)S(1)}, f32[8,5120]{1,0:T(8,128)S(1)}, u32[]{:S(2)}, u32[]{:S(2)}) collective-permute-start(f32[8,5120]{1,0:T(8,128)S(1)} %slice.99), channel_id=1, source_target_pairs={{0,2},{1,7},{2,0},{3,5},{4,6},{5,3},{6,4},{7,1},{8,10},{9,15},{10,... | collective-permute-start | bytes 491528 | tf_op jit(solution)/shard_map/ppermute | solution.py:38
  44.1 7.3 %collective-permute-start.5 = (f32[4,5120]{1,0:T(4,128)S(1)}, f32[4,5120]{1,0:T(4,128)S(1)}, u32[]{:S(2)}, u32[]{:S(2)}) collective-permute-start(f32[4,5120]{1,0:T(4,128)S(1)} %slice.89), channel_id=1, source_target_pairs={{0,6},{1,3},{2,4},{3,1},{4,2},{5,7},{6,0},{7,5},{8,14},{9,11},{10,... | collective-permute-start | bytes 245768 | tf_op jit(solution)/shard_map/ppermute | solution.py:38
  48.9 10.1 %collective-permute-start.12 = (f32[4,5120]{1,0:T(4,128)S(1)}, f32[4,5120]{1,0:T(4,128)S(1)}, u32[]{:S(2)}, u32[]{:S(2)}) collective-permute-start(f32[4,5120]{1,0:T(4,128)S(1)} %slice.95), channel_id=1, source_target_pairs={{0,6},{1,3},{2,4},{3,1},{4,2},{5,7},{6,0},{7,5},{8,14},{9,11},{10,... | collective-permute-start | bytes 245768 | tf_op jit(solution)/shard_map/ppermute | solution.py:38
  51.5 7.5 %collective-permute-start.6 = (f32[1,4,5248]{2,1,0:T(4,128)S(1)}, f32[1,4,5248]{2,1,0:T(4,128)S(1)}, u32[]{:S(2)}, u32[]{:S(2)}) collective-permute-start(f32[1,4,5248]{2,1,0:T(4,128)S(1)} %get-tuple-element.30), channel_id=1, source_target_pairs={{0,32},{32,64},{64,96},{96,128},{128,160},{160,192},{192,224},{224... | collective-permute-start | bytes 251912 | tf_op jit(solution)/shard_map/ppermute | solution.py:23
  54.2 8.1 %collective-permute-start.19 = (f32[4,5120]{1,0:T(4,128)S(1)}, f32[4,5120]{1,0:T(4,128)S(1)}, u32[]{:S(2)}, u32[]{:S(2)}) collective-permute-start(f32[4,5120]{1,0:T(4,128)S(1)} %slice.101), channel_id=1, source_target_pairs={{0,6},{1,3},{2,4},{3,1},{4,2},{5,7},{6,0},{7,5},{8,14},{9,11},{10,... | collective-permute-start | bytes 245768 | tf_op jit(solution)/shard_map/ppermute | solution.py:38
  59.1 5.8 %collective-permute-start.13 = (f32[1,4,5248]{2,1,0:T(4,128)S(1)}, f32[1,4,5248]{2,1,0:T(4,128)S(1)}, u32[]{:S(2)}, u32[]{:S(2)}) collective-permute-start(f32[1,4,5248]{2,1,0:T(4,128)S(1)} %get-tuple-element.37), channel_id=1, source_target_pairs={{0,64},{32,96},{64,128},{96,160},{128,192},{160,224},{192,0},{224,... | collective-permute-start | bytes 251912 | tf_op jit(solution)/shard_map/ppermute | solution.py:23
  64.9 6.1 %collective-permute-start.20 = (f32[1,4,5248]{2,1,0:T(4,128)S(1)}, f32[1,4,5248]{2,1,0:T(4,128)S(1)}, u32[]{:S(2)}, u32[]{:S(2)}) collective-permute-start(f32[1,4,5248]{2,1,0:T(4,128)S(1)} %get-tuple-element.45), channel_id=1, source_target_pairs={{0,128},{32,160},{64,192},{96,224},{128,0},{160,32},{192,64},{224,... | collective-permute-start | bytes 251912 | tf_op jit(solution)/shard_map/ppermute | solution.py:23

commit v6 on v5

--- a/solution.py
+++ b/solution.py
@@ -51,29 +51,30 @@
 OTHERS = (0, 2, 1, 3)
 
 
-def split_kernel(step, g_ref, *refs):
-    other_send, own_send, other_keep, own_keep, block, arrived = refs[-6:]
+def split_kernel(steps, g_ref, *refs):
+    block, arrived = refs[-2:]
     core = lax.axis_index("core")
     y_at = places(lax.axis_index("y"), core)
     z_at = places(lax.axis_index("zh"), core)
-    order = (3, 2, 1, 0)
+    order = [(n, q) for n in range(len(steps)) for q in (3, 2, 1, 0)]
     copies = {}
-    for q in order:
+    for n, q in order:
         first_row = pl.multiple_of(32 * y_at[q], 32)
-        copies[q] = pltpu.make_async_copy(
-            g_ref.at[step, 0, 0, pl.ds(first_row, 32), :], block.at[q], arrived.at[q]
+        copies[n, q] = pltpu.make_async_copy(
+            g_ref.at[steps[n], 0, 0, pl.ds(first_row, 32), :], block.at[n, q], arrived.at[n, q]
         )
-        copies[q].start()
+        copies[n, q].start()
     row = lax.broadcasted_iota(jnp.int32, (8, STRIP), 0)
-    for q in order:
-        copies[q].wait()
+    for n, q in order:
+        copies[n, q].wait()
+        other_send, own_send, other_keep, own_keep = refs[4 * n : 4 * n + 4]
         own = (own_keep, own_send)[q // 2]
         other = (other_keep, other_send)[OTHERS[q] // 2]
         for at in range(0, D, STRIP):
             columns = slice(at, at + STRIP)
             top, low = [], []
             for z in range(ZH):
-                rows = block[q, pl.ds(pl.multiple_of(8 * z_at[z], 8), 8), columns]
+                rows = block[n, q, pl.ds(pl.multiple_of(8 * z_at[z], 8), 8), columns]
                 turned = pltpu.roll(rows, 4, 0)
                 top.append(jnp.where(core == 0, rows, turned))
                 low.append(jnp.where(core == 0, turned, rows))
@@ -83,18 +84,22 @@
                 other[OTHERS[q] % 2, rows, columns] = jnp.where(row < 4, low[m], top[m + 2])
 
 
-def split_cores(grads, step, after):
-    shape = pltpu.VMEM((2, 16, D), jnp.float32)
+def split_cores(grads, steps):
+    count = len(steps)
     return pl.pallas_call(
-        functools.partial(split_kernel, step),
-        out_shape=(shape,) * 4,
-        in_specs=[pl.BlockSpec(memory_space=pltpu.HBM)]
-        + [pl.BlockSpec(memory_space=pl.ANY)] * len(after),
-        out_specs=[pl.BlockSpec(memory_space=pltpu.VMEM)] * 4,
-        scratch_shapes=[pltpu.VMEM((Y, 32, D), jnp.float32), pltpu.SemaphoreType.DMA((Y,))],
-        compiler_params=pltpu.CompilerParams(vmem_limit_bytes=16 << 20),
-        cost_estimate=pl.CostEstimate(flops=0, bytes_accessed=8 * 16 * D * 4, transcendentals=0),
-    )(pltpu.with_memory_space_constraint(grads, pltpu.HBM), *after)
+        functools.partial(split_kernel, steps),
+        out_shape=(pltpu.VMEM((2, 16, D), jnp.float32),) * (4 * count),
+        in_specs=[pl.BlockSpec(memory_space=pltpu.HBM)],
+        out_specs=[pl.BlockSpec(memory_space=pltpu.VMEM)] * (4 * count),
+        scratch_shapes=[
+            pltpu.VMEM((count, Y, 32, D), jnp.float32),
+            pltpu.SemaphoreType.DMA((count, Y)),
+        ],
+        compiler_params=pltpu.CompilerParams(vmem_limit_bytes=24 << 20),
+        cost_estimate=pl.CostEstimate(
+            flops=0, bytes_accessed=8 * count * 16 * D * 4, transcendentals=0
+        ),
+    )(pltpu.with_memory_space_constraint(grads, pltpu.HBM))
 
 
 def per_device(numerators, push_weight, keep_share, momentum, grads):
@@ -103,15 +108,16 @@
     values = jnp.concatenate([numerators, weight], axis=2)
     start = numerators / push_weight[:, None, None]
     buffer = momentum
-    other_0, own_0, otherk_0, ownk_0 = split_cores(grads, 0, ())
+    other_0, own_0, otherk_0, ownk_0 = split_cores(grads, (0,))
     come_C0 = ring(other_0, "core", 1)
     sent_0 = own_0 + come_C0
     kept_0 = ownk_0 + ring(otherk_0, "core", 1)
-    other_1, own_1, otherk_1, ownk_1 = split_cores(grads, 1, ())
+    later = split_cores(grads, (1, 2))
+    other_1, own_1, otherk_1, ownk_1 = later[:4]
     come_C1 = ring(other_1, "core", 1)
     sent_1 = own_1 + come_C1
     kept_1 = ownk_1 + ring(otherk_1, "core", 1)
-    other_2, own_2, otherk_2, ownk_2 = split_cores(grads, 2, ())
+    other_2, own_2, otherk_2, ownk_2 = later[4:]
     come_C2 = ring(other_2, "core", 1)
     sent_2 = own_2 + come_C2
     kept_2 = ownk_2 + ring(otherk_2, "core", 1)
@@ -122,6 +128,7 @@
     come_Y1 = swap(ready_Y1, "y", 0)
     rows_1 = kept_1 + come_Y1
     ready_Y2 = sent_2
+    ready_Y2, _ = lax.optimization_barrier((ready_Y2, ready_Y0))
     come_Y2 = swap(ready_Y2, "y", 0)
     rows_2 = kept_2 + come_Y2
     ready_Z0 = rows_0[..., 8:, :]

time: 73 us -> 71.9 us (0.985)
  Pallas kernels: 5.4 us -> 4.44 us
    pallas_call x3 -> x2, Pallas kernels: 5.4 us -> 4.44 us  [split_cores(): pl.pallas_call(functools.partial(split_kernel, steps), out_shape=(pltpu.V...]
  transfers between devices with their start and end apart: 21 -> 21, of which waited for: 9 -> 9; matrix products, arithmetic and copies ran while one was open for 2% -> 2% of each run, Pallas kernels for 5% -> 4%
where the time goes in v6:
time: 71.9 us; the launch traced here: 71.3 us
  starting transfers between devices  36.5 us (51%)
  waiting for transfers between devices  25 us (35%)
  Pallas kernels  4.44 us (6%)
  other arithmetic  2.36 us (3%)
  between operations  2.16 us (3%)
  local copies, waits for them, and re-layouts  0.8 us (1%)
    ppermute x12, starting transfers between devices, swap(): return lax.ppermute(x, SHARD, pairs)  28.1 us
    ppermute x12, waiting for transfers between devices, swap(): return lax.ppermute(x, SHARD, pairs)  18.9 us
    ppermute x9, starting transfers between devices, ring(): return lax.ppermute(x, axis, [(i, (i + by) % n) for i in range(n)])  8.45 us
    ppermute x9, waiting for transfers between devices, ring(): return lax.ppermute(x, axis, [(i, (i + by) % n) for i in range(n)])  6.05 us
    pallas_call x2, Pallas kernels, split_cores(): pl.pallas_call(functools.partial(split_kernel, steps), out_shape=(pltpu.V...  4.44 us
  transfers between devices with their start and end apart: 21, of which 9 were waited for; matrix products, arithmetic and copies ran while one was open for 2% of the time, Pallas kernels for 4%

profile of v6, /device:TPU:24, one launch (start us, length us, event | category | flops | bytes accessed | tf_op | source)
XLA Modules:
  0.0 71.3 jit_solution(18402359326962894559)
XLA Ops:
  0.6 1.8 %shard_map.76 = (f32[2,16,5120]{2,1,0:T(8,128)S(1)}, f32[2,16,5120]{2,1,0:T(8,128)S(1)}, f32[2,16,5120]{2,1,0:T(8,128)S(1)}, f32[2,16,5120]{2,1,0:T(8,128)S(1)}) custom-call(f32[3,1,1,128,5120]{4,3,2,1,0:T(8,128)} %g_ref.3), custom_call_target="tpu_custom_call" | custom-call | bytes 2621440 | tf_op jit(solution)/shard_map/pallas_call | solution.py:89
  2.5 2.6 %shard_map.77 = (f32[2,16,5120]{2,1,0:T(8,128)S(1)}, f32[2,16,5120]{2,1,0:T(8,128)S(1)}, f32[2,16,5120]{2,1,0:T(8,128)S(1)}, f32[2,16,5120]{2,1,0:T(8,128)S(1)},...) custom-call(f32[3,1,1,128,5120]{4,3,2,1,0:T(8,128)} %g_ref.3), custom_call_target="tpu_custom_call" | custom-call | bytes 5242880 | tf_op jit(solution)/shard_map/pallas_call | solution.py:89
  6.3 0.8 %collective-permute-start.2 = (f32[2,16,5120]{2,1,0:T(8,128)S(1)}, f32[2,16,5120]{2,1,0:T(8,128)S(1)}, u32[]{:S(2)}, u32[]{:S(2)}) collective-permute-start(f32[2,16,5120]{2,1,0:T(8,128)S(1)} %add.90), channel_id=1, source_target_pairs={{0,8},{1,25},{2,10},{3,27},{4,12},{5,29},{6,14},{7,31},{8,0},{9,17... | collective-permute-start | bytes 1966088 | tf_op jit(solution)/shard_map/ppermute | solution.py:38
  7.2 1.0 %collective-permute-start.7 = (f32[2,16,5120]{2,1,0:T(8,128)S(1)}, f32[2,16,5120]{2,1,0:T(8,128)S(1)}, u32[]{:S(2)}, u32[]{:S(2)}) collective-permute-start(f32[2,16,5120]{2,1,0:T(8,128)S(1)} %get-tuple-element.33), channel_id=1, source_target_pairs={{0,1},{1,0},{2,3},{3,2},{4,5},{5,4},{6,7},{7,6},{8,9},{9,8},{10,11... | collective-permute-start | bytes 1966088 | tf_op jit(solution)/shard_map/ppermute | solution.py:23
  10.6 1.4 %collective-permute-start.16 = (f32[2,16,5120]{2,1,0:T(8,128)S(1)}, f32[2,16,5120]{2,1,0:T(8,128)S(1)}, u32[]{:S(2)}, u32[]{:S(2)}) collective-permute-start(f32[2,16,5120]{2,1,0:T(8,128)S(1)} %add.108), channel_id=1, source_target_pairs={{0,8},{1,25},{2,10},{3,27},{4,12},{5,29},{6,14},{7,31},{8,0},{9,17... | collective-permute-start | bytes 1966088 | tf_op jit(solution)/shard_map/ppermute | solution.py:38
  12.0 5.0 %collective-permute-done.2 = f32[2,16,5120]{2,1,0:T(8,128)S(1)} collective-permute-done((f32[2,16,5120]{2,1,0:T(8,128)S(1)}, f32[2,16,5120]{2,1,0:T(8,128)S(1)}, u32[]{:S(2)}, u32[]{:S(2)}) %collective-permute-start.2) | collective-permute-done | bytes 655392 | tf_op jit(solution)/shard_map/ppermute | solution.py:38
  17.1 3.4 %collective-permute-start.3 = (f32[2,8,5120]{2,1,0:T(8,128)S(1)}, f32[2,8,5120]{2,1,0:T(8,128)S(1)}, u32[]{:S(2)}, u32[]{:S(2)}) collective-permute-start(f32[2,8,5120]{2,1,0:T(8,128)S(1)} %slice.85), channel_id=1, source_target_pairs={{0,2},{1,7},{2,0},{3,5},{4,6},{5,3},{6,4},{7,1},{8,10},{9,15},{10,... | collective-permute-start | bytes 983048 | tf_op jit(solution)/shard_map/ppermute | solution.py:38
  20.5 3.5 %collective-permute-done.9 = f32[2,16,5120]{2,1,0:T(8,128)S(1)} collective-permute-done((f32[2,16,5120]{2,1,0:T(8,128)S(1)}, f32[2,16,5120]{2,1,0:T(8,128)S(1)}, u32[]{:S(2)}, u32[]{:S(2)}) %collective-permute-start.9) | collective-permute-done | bytes 655392 | tf_op jit(solution)/shard_map/ppermute | solution.py:38
  24.2 3.4 %collective-permute-start.10 = (f32[2,8,5120]{2,1,0:T(8,128)S(1)}, f32[2,8,5120]{2,1,0:T(8,128)S(1)}, u32[]{:S(2)}, u32[]{:S(2)}) collective-permute-start(f32[2,8,5120]{2,1,0:T(8,128)S(1)} %slice.91), channel_id=1, source_target_pairs={{0,2},{1,7},{2,0},{3,5},{4,6},{5,3},{6,4},{7,1},{8,10},{9,15},{10,... | collective-permute-start | bytes 983048 | tf_op jit(solution)/shard_map/ppermute | solution.py:38
  27.5 3.5 %collective-permute-done.16 = f32[2,16,5120]{2,1,0:T(8,128)S(1)} collective-permute-done((f32[2,16,5120]{2,1,0:T(8,128)S(1)}, f32[2,16,5120]{2,1,0:T(8,128)S(1)}, u32[]{:S(2)}, u32[]{:S(2)}) %collective-permute-start.16) | collective-permute-done | bytes 655392 | tf_op jit(solution)/shard_map/ppermute | solution.py:38
  31.2 2.0 %collective-permute-start.17 = (f32[16,5120]{1,0:T(8,128)S(1)}, f32[16,5120]{1,0:T(8,128)S(1)}, u32[]{:S(2)}, u32[]{:S(2)}) collective-permute-start(f32[16,5120]{1,0:T(8,128)S(1)} %slice_bitcast_fusion), channel_id=1, source_target_pairs={{0,24},{1,9},{2,26},{3,11},{4,28},{5,13},{6,30},{7,15},{8,16},{9,1... | collective-permute-start | bytes 983048 | tf_op jit(solution)/shard_map/ppermute | solution.py:38
  33.3 1.4 %collective-permute-start.4 = (f32[8,5120]{1,0:T(8,128)S(1)}, f32[8,5120]{1,0:T(8,128)S(1)}, u32[]{:S(2)}, u32[]{:S(2)}) collective-permute-start(f32[8,5120]{1,0:T(8,128)S(1)} %slice_bitcast_fusion.4), channel_id=1, source_target_pairs={{0,24},{1,9},{2,26},{3,11},{4,28},{5,13},{6,30},{7,15},{8,16},{9,1... | collective-permute-start | bytes 491528 | tf_op jit(solution)/shard_map/ppermute | solution.py:38
  34.7 2.5 %collective-permute-done.10 = f32[2,8,5120]{2,1,0:T(8,128)S(1)} collective-permute-done((f32[2,8,5120]{2,1,0:T(8,128)S(1)}, f32[2,8,5120]{2,1,0:T(8,128)S(1)}, u32[]{:S(2)}, u32[]{:S(2)}) %collective-permute-start.10) | collective-permute-done | bytes 327712 | tf_op jit(solution)/shard_map/ppermute | solution.py:38
  37.6 2.0 %collective-permute-done.17 = f32[16,5120]{1,0:T(8,128)S(1)} collective-permute-done((f32[16,5120]{1,0:T(8,128)S(1)}, f32[16,5120]{1,0:T(8,128)S(1)}, u32[]{:S(2)}, u32[]{:S(2)}) %collective-permute-start.17) | collective-permute-done | bytes 327712 | tf_op jit(solution)/shard_map/ppermute | solution.py:38
  39.6 3.4 %collective-permute-start.18 = (f32[8,5120]{1,0:T(8,128)S(1)}, f32[8,5120]{1,0:T(8,128)S(1)}, u32[]{:S(2)}, u32[]{:S(2)}) collective-permute-start(f32[8,5120]{1,0:T(8,128)S(1)} %slice.99), channel_id=1, source_target_pairs={{0,2},{1,7},{2,0},{3,5},{4,6},{5,3},{6,4},{7,1},{8,10},{9,15},{10,... | collective-permute-start | bytes 491528 | tf_op jit(solution)/shard_map/ppermute | solution.py:38
  43.0 4.7 %collective-permute-start.5 = (f32[4,5120]{1,0:T(4,128)S(1)}, f32[4,5120]{1,0:T(4,128)S(1)}, u32[]{:S(2)}, u32[]{:S(2)}) collective-permute-start(f32[4,5120]{1,0:T(4,128)S(1)} %slice.89), channel_id=1, source_target_pairs={{0,6},{1,3},{2,4},{3,1},{4,2},{5,7},{6,0},{7,5},{8,14},{9,11},{10,... | collective-permute-start | bytes 245768 | tf_op jit(solution)/shard_map/ppermute | solution.py:38
  47.8 1.7 %collective-permute-start.12 = (f32[4,5120]{1,0:T(4,128)S(1)}, f32[4,5120]{1,0:T(4,128)S(1)}, u32[]{:S(2)}, u32[]{:S(2)}) collective-permute-start(f32[4,5120]{1,0:T(4,128)S(1)} %slice.95), channel_id=1, source_target_pairs={{0,6},{1,3},{2,4},{3,1},{4,2},{5,7},{6,0},{7,5},{8,14},{9,11},{10,... | collective-permute-start | bytes 245768 | tf_op jit(solution)/shard_map/ppermute | solution.py:38
  50.5 2.7 %collective-permute-start.6 = (f32[1,4,5248]{2,1,0:T(4,128)S(1)}, f32[1,4,5248]{2,1,0:T(4,128)S(1)}, u32[]{:S(2)}, u32[]{:S(2)}) collective-permute-start(f32[1,4,5248]{2,1,0:T(4,128)S(1)} %get-tuple-element.31), channel_id=1, source_target_pairs={{0,32},{32,64},{64,96},{96,128},{128,160},{160,192},{192,224},{224... | collective-permute-start | bytes 251912 | tf_op jit(solution)/shard_map/ppermute | solution.py:23
  53.1 4.8 %collective-permute-start.19 = (f32[4,5120]{1,0:T(4,128)S(1)}, f32[4,5120]{1,0:T(4,128)S(1)}, u32[]{:S(2)}, u32[]{:S(2)}) collective-permute-start(f32[4,5120]{1,0:T(4,128)S(1)} %slice.101), channel_id=1, source_target_pairs={{0,6},{1,3},{2,4},{3,1},{4,2},{5,7},{6,0},{7,5},{8,14},{9,11},{10,... | collective-permute-start | bytes 245768 | tf_op jit(solution)/shard_map/ppermute | solution.py:38
  58.0 1.6 %collective-permute-start.13 = (f32[1,4,5248]{2,1,0:T(4,128)S(1)}, f32[1,4,5248]{2,1,0:T(4,128)S(1)}, u32[]{:S(2)}, u32[]{:S(2)}) collective-permute-start(f32[1,4,5248]{2,1,0:T(4,128)S(1)} %get-tuple-element.38), channel_id=1, source_target_pairs={{0,64},{32,96},{64,128},{96,160},{128,192},{160,224},{192,0},{224,... | collective-permute-start | bytes 251912 | tf_op jit(solution)/shard_map/ppermute | solution.py:23
  59.6 1.6 %collective-permute-done.19 = f32[4,5120]{1,0:T(4,128)S(1)} collective-permute-done((f32[4,5120]{1,0:T(4,128)S(1)}, f32[4,5120]{1,0:T(4,128)S(1)}, u32[]{:S(2)}, u32[]{:S(2)}) %collective-permute-start.19) | collective-permute-done | bytes 81952 | tf_op jit(solution)/shard_map/ppermute | solution.py:38
  61.9 1.9 %collective-permute-done.13 = f32[1,4,5248]{2,1,0:T(4,128)S(1)} collective-permute-done((f32[1,4,5248]{2,1,0:T(4,128)S(1)}, f32[1,4,5248]{2,1,0:T(4,128)S(1)}, u32[]{:S(2)}, u32[]{:S(2)}) %collective-permute-start.13) | collective-permute-done | bytes 84000 | tf_op jit(solution)/shard_map/ppermute | solution.py:23
  63.8 1.9 %collective-permute-start.20 = (f32[1,4,5248]{2,1,0:T(4,128)S(1)}, f32[1,4,5248]{2,1,0:T(4,128)S(1)}, u32[]{:S(2)}, u32[]{:S(2)}) collective-permute-start(f32[1,4,5248]{2,1,0:T(4,128)S(1)} %get-tuple-element.47), channel_id=1, source_target_pairs={{0,128},{32,160},{64,192},{96,224},{128,0},{160,32},{192,64},{224,... | collective-permute-start | bytes 251912 | tf_op jit(solution)/shard_map/ppermute | solution.py:23
  65.7 4.2 %collective-permute-done.20 = f32[1,4,5248]{2,1,0:T(4,128)S(1)} collective-permute-done((f32[1,4,5248]{2,1,0:T(4,128)S(1)}, f32[1,4,5248]{2,1,0:T(4,128)S(1)}, u32[]{:S(2)}, u32[]{:S(2)}) %collective-permute-start.20) | collective-permute-done | bytes 84000 | tf_op jit(solution)/shard_map/ppermute | solution.py:23
  (55 shorter events, 6.4 us)
Async XLA Ops:
  2.4 3.8 %collective-permute-start.1 = (f32[2,16,5120]{2,1,0:T(8,128)S(1)}, f32[2,16,5120]{2,1,0:T(8,128)S(1)}, u32[]{:S(2)}, u32[]{:S(2)}) collective-permute-start(f32[2,16,5120]{2,1,0:T(8,128)S(1)} %get-tuple-element.29), channel_id=1, source_target_pairs={{0,1},{1,0},{2,3},{3,2},{4,5},{5,4},{6,7},{7,6},{8,9},{9,8},{10,11... | collective-permute-start | bytes 1966088 | tf_op jit(solution)/shard_map/ppermute | solution.py:23
  5.2 4.3 %collective-permute-start.8 = (f32[2,16,5120]{2,1,0:T(8,128)S(1)}, f32[2,16,5120]{2,1,0:T(8,128)S(1)}, u32[]{:S(2)}, u32[]{:S(2)}) collective-permute-start(f32[2,16,5120]{2,1,0:T(8,128)S(1)} %get-tuple-element.35), channel_id=1, source_target_pairs={{0,1},{1,0},{2,3},{3,2},{4,5},{5,4},{6,7},{7,6},{8,9},{9,8},{10,11... | collective-permute-start | bytes 1966088 | tf_op jit(solution)/shard_map/ppermute | solution.py:23
  5.7 3.9 %collective-permute-start.15 = (f32[2,16,5120]{2,1,0:T(8,128)S(1)}, f32[2,16,5120]{2,1,0:T(8,128)S(1)}, u32[]{:S(2)}, u32[]{:S(2)}) collective-permute-start(f32[2,16,5120]{2,1,0:T(8,128)S(1)} %get-tuple-element.42), channel_id=1, source_target_pairs={{0,1},{1,0},{2,3},{3,2},{4,5},{5,4},{6,7},{7,6},{8,9},{9,8},{10,11... | collective-permute-start | bytes 1966088 | tf_op jit(solution)/shard_map/ppermute | solution.py:23
  5.8 4.7 %collective-permute-start = (f32[2,16,5120]{2,1,0:T(8,128)S(1)}, f32[2,16,5120]{2,1,0:T(8,128)S(1)}, u32[]{:S(2)}, u32[]{:S(2)}) collective-permute-start(f32[2,16,5120]{2,1,0:T(8,128)S(1)} %get-tuple-element.27), channel_id=1, source_target_pairs={{0,1},{1,0},{2,3},{3,2},{4,5},{5,4},{6,7},{7,6},{8,9},{9,8},{10,11... | collective-permute-start | bytes 1966088 | tf_op jit(solution)/shard_map/ppermute | solution.py:23
  6.3 10.7 %collective-permute-start.2 = (f32[2,16,5120]{2,1,0:T(8,128)S(1)}, f32[2,16,5120]{2,1,0:T(8,128)S(1)}, u32[]{:S(2)}, u32[]{:S(2)}) collective-permute-start(f32[2,16,5120]{2,1,0:T(8,128)S(1)} %add.90), channel_id=1, source_target_pairs={{0,8},{1,25},{2,10},{3,27},{4,12},{5,29},{6,14},{7,31},{8,0},{9,17... | collective-permute-start | bytes 1966088 | tf_op jit(solution)/shard_map/ppermute | solution.py:38
  7.2 13.3 %collective-permute-start.7 = (f32[2,16,5120]{2,1,0:T(8,128)S(1)}, f32[2,16,5120]{2,1,0:T(8,128)S(1)}, u32[]{:S(2)}, u32[]{:S(2)}) collective-permute-start(f32[2,16,5120]{2,1,0:T(8,128)S(1)} %get-tuple-element.33), channel_id=1, source_target_pairs={{0,1},{1,0},{2,3},{3,2},{4,5},{5,4},{6,7},{7,6},{8,9},{9,8},{10,11... | collective-permute-start | bytes 1966088 | tf_op jit(solution)/shard_map/ppermute | solution.py:23
  9.5 18.0 %collective-permute-start.14 = (f32[2,16,5120]{2,1,0:T(8,128)S(1)}, f32[2,16,5120]{2,1,0:T(8,128)S(1)}, u32[]{:S(2)}, u32[]{:S(2)}) collective-permute-start(f32[2,16,5120]{2,1,0:T(8,128)S(1)} %get-tuple-element.40), channel_id=1, source_target_pairs={{0,1},{1,0},{2,3},{3,2},{4,5},{5,4},{6,7},{7,6},{8,9},{9,8},{10,11... | collective-permute-start | bytes 1966088 | tf_op jit(solution)/shard_map/ppermute | solution.py:23
  9.7 14.3 %collective-permute-start.9 = (f32[2,16,5120]{2,1,0:T(8,128)S(1)}, f32[2,16,5120]{2,1,0:T(8,128)S(1)}, u32[]{:S(2)}, u32[]{:S(2)}) collective-permute-start(f32[2,16,5120]{2,1,0:T(8,128)S(1)} %add.99), channel_id=1, source_target_pairs={{0,8},{1,25},{2,10},{3,27},{4,12},{5,29},{6,14},{7,31},{8,0},{9,17... | collective-permute-start | bytes 1966088 | tf_op jit(solution)/shard_map/ppermute | solution.py:38
  10.6 20.4 %collective-permute-start.16 = (f32[2,16,5120]{2,1,0:T(8,128)S(1)}, f32[2,16,5120]{2,1,0:T(8,128)S(1)}, u32[]{:S(2)}, u32[]{:S(2)}) collective-permute-start(f32[2,16,5120]{2,1,0:T(8,128)S(1)} %add.108), channel_id=1, source_target_pairs={{0,8},{1,25},{2,10},{3,27},{4,12},{5,29},{6,14},{7,31},{8,0},{9,17... | collective-permute-start | bytes 1966088 | tf_op jit(solution)/shard_map/ppermute | solution.py:38
  17.0 33.3 %copy-start.1 = (f32[1,4,5120]{2,1,0:T(4,128)S(1)}, f32[1,4,5120]{2,1,0:T(4,128)}, u32[]{:S(2)}) copy-start(f32[1,4,5120]{2,1,0:T(4,128)} %param.8) | copy-start | bytes 245764
  17.0 33.4 %copy-start = (f32[1,4,5120]{2,1,0:T(4,128)S(1)}, f32[1,4,5120]{2,1,0:T(4,128)}, u32[]{:S(2)}) copy-start(f32[1,4,5120]{2,1,0:T(4,128)} %param.5) | copy-start | bytes 245764
  17.1 16.1 %collective-permute-start.3 = (f32[2,8,5120]{2,1,0:T(8,128)S(1)}, f32[2,8,5120]{2,1,0:T(8,128)S(1)}, u32[]{:S(2)}, u32[]{:S(2)}) collective-permute-start(f32[2,8,5120]{2,1,0:T(8,128)S(1)} %slice.85), channel_id=1, source_target_pairs={{0,2},{1,7},{2,0},{3,5},{4,6},{5,3},{6,4},{7,1},{8,10},{9,15},{10,... | collective-permute-start | bytes 983048 | tf_op jit(solution)/shard_map/ppermute | solution.py:38
  24.2 13.0 %collective-permute-start.10 = (f32[2,8,5120]{2,1,0:T(8,128)S(1)}, f32[2,8,5120]{2,1,0:T(8,128)S(1)}, u32[]{:S(2)}, u32[]{:S(2)}) collective-permute-start(f32[2,8,5120]{2,1,0:T(8,128)S(1)} %slice.91), channel_id=1, source_target_pairs={{0,2},{1,7},{2,0},{3,5},{4,6},{5,3},{6,4},{7,1},{8,10},{9,15},{10,... | collective-permute-start | bytes 983048 | tf_op jit(solution)/shard_map/ppermute | solution.py:38
  31.2 8.4 %collective-permute-start.17 = (f32[16,5120]{1,0:T(8,128)S(1)}, f32[16,5120]{1,0:T(8,128)S(1)}, u32[]{:S(2)}, u32[]{:S(2)}) collective-permute-start(f32[16,5120]{1,0:T(8,128)S(1)} %slice_bitcast_fusion), channel_id=1, source_target_pairs={{0,24},{1,9},{2,26},{3,11},{4,28},{5,13},{6,30},{7,15},{8,16},{9,1... | collective-permute-start | bytes 983048 | tf_op jit(solution)/shard_map/ppermute | solution.py:38
  33.3 9.7 %collective-permute-start.4 = (f32[8,5120]{1,0:T(8,128)S(1)}, f32[8,5120]{1,0:T(8,128)S(1)}, u32[]{:S(2)}, u32[]{:S(2)}) collective-permute-start(f32[8,5120]{1,0:T(8,128)S(1)} %slice_bitcast_fusion.4), channel_id=1, source_target_pairs={{0,24},{1,9},{2,26},{3,11},{4,28},{5,13},{6,30},{7,15},{8,16},{9,1... | collective-permute-start | bytes 491528 | tf_op jit(solution)/shard_map/ppermute | solution.py:38
  37.2 10.6 %collective-permute-start.11 = (f32[8,5120]{1,0:T(8,128)S(1)}, f32[8,5120]{1,0:T(8,128)S(1)}, u32[]{:S(2)}, u32[]{:S(2)}) collective-permute-start(f32[8,5120]{1,0:T(8,128)S(1)} %slice_bitcast_fusion.2), channel_id=1, source_target_pairs={{0,24},{1,9},{2,26},{3,11},{4,28},{5,13},{6,30},{7,15},{8,16},{9,1... | collective-permute-start | bytes 491528 | tf_op jit(solution)/shard_map/ppermute | solution.py:38
  39.6 9.9 %collective-permute-start.18 = (f32[8,5120]{1,0:T(8,128)S(1)}, f32[8,5120]{1,0:T(8,128)S(1)}, u32[]{:S(2)}, u32[]{:S(2)}) collective-permute-start(f32[8,5120]{1,0:T(8,128)S(1)} %slice.99), channel_id=1, source_target_pairs={{0,2},{1,7},{2,0},{3,5},{4,6},{5,3},{6,4},{7,1},{8,10},{9,15},{10,... | collective-permute-start | bytes 491528 | tf_op jit(solution)/shard_map/ppermute | solution.py:38
  43.0 7.3 %collective-permute-start.5 = (f32[4,5120]{1,0:T(4,128)S(1)}, f32[4,5120]{1,0:T(4,128)S(1)}, u32[]{:S(2)}, u32[]{:S(2)}) collective-permute-start(f32[4,5120]{1,0:T(4,128)S(1)} %slice.89), channel_id=1, source_target_pairs={{0,6},{1,3},{2,4},{3,1},{4,2},{5,7},{6,0},{7,5},{8,14},{9,11},{10,... | collective-permute-start | bytes 245768 | tf_op jit(solution)/shard_map/ppermute | solution.py:38
  47.8 10.1 %collective-permute-start.12 = (f32[4,5120]{1,0:T(4,128)S(1)}, f32[4,5120]{1,0:T(4,128)S(1)}, u32[]{:S(2)}, u32[]{:S(2)}) collective-permute-start(f32[4,5120]{1,0:T(4,128)S(1)} %slice.95), channel_id=1, source_target_pairs={{0,6},{1,3},{2,4},{3,1},{4,2},{5,7},{6,0},{7,5},{8,14},{9,11},{10,... | collective-permute-start | bytes 245768 | tf_op jit(solution)/shard_map/ppermute | solution.py:38
  50.5 7.5 %collective-permute-start.6 = (f32[1,4,5248]{2,1,0:T(4,128)S(1)}, f32[1,4,5248]{2,1,0:T(4,128)S(1)}, u32[]{:S(2)}, u32[]{:S(2)}) collective-permute-start(f32[1,4,5248]{2,1,0:T(4,128)S(1)} %get-tuple-element.31), channel_id=1, source_target_pairs={{0,32},{32,64},{64,96},{96,128},{128,160},{160,192},{192,224},{224... | collective-permute-start | bytes 251912 | tf_op jit(solution)/shard_map/ppermute | solution.py:23
  53.1 8.1 %collective-permute-start.19 = (f32[4,5120]{1,0:T(4,128)S(1)}, f32[4,5120]{1,0:T(4,128)S(1)}, u32[]{:S(2)}, u32[]{:S(2)}) collective-permute-start(f32[4,5120]{1,0:T(4,128)S(1)} %slice.101), channel_id=1, source_target_pairs={{0,6},{1,3},{2,4},{3,1},{4,2},{5,7},{6,0},{7,5},{8,14},{9,11},{10,... | collective-permute-start | bytes 245768 | tf_op jit(solution)/shard_map/ppermute | solution.py:38
  58.0 5.8 %collective-permute-start.13 = (f32[1,4,5248]{2,1,0:T(4,128)S(1)}, f32[1,4,5248]{2,1,0:T(4,128)S(1)}, u32[]{:S(2)}, u32[]{:S(2)}) collective-permute-start(f32[1,4,5248]{2,1,0:T(4,128)S(1)} %get-tuple-element.38), channel_id=1, source_target_pairs={{0,64},{32,96},{64,128},{96,160},{128,192},{160,224},{192,0},{224,... | collective-permute-start | bytes 251912 | tf_op jit(solution)/shard_map/ppermute | solution.py:23
  63.8 6.1 %collective-permute-start.20 = (f32[1,4,5248]{2,1,0:T(4,128)S(1)}, f32[1,4,5248]{2,1,0:T(4,128)S(1)}, u32[]{:S(2)}, u32[]{:S(2)}) collective-permute-start(f32[1,4,5248]{2,1,0:T(4,128)S(1)} %get-tuple-element.47), channel_id=1, source_target_pairs={{0,128},{32,160},{64,192},{96,224},{128,0},{160,32},{192,64},{224,... | collective-permute-start | bytes 251912 | tf_op jit(solution)/shard_map/ppermute | solution.py:23

commit v7 on v6

--- a/solution.py
+++ b/solution.py
@@ -128,7 +128,7 @@
     come_Y1 = swap(ready_Y1, "y", 0)
     rows_1 = kept_1 + come_Y1
     ready_Y2 = sent_2
-    ready_Y2, _ = lax.optimization_barrier((ready_Y2, ready_Y0))
+    ready_Y2, *_ = lax.optimization_barrier((ready_Y2, ready_Y0))
     come_Y2 = swap(ready_Y2, "y", 0)
     rows_2 = kept_2 + come_Y2
     ready_Z0 = rows_0[..., 8:, :]
@@ -147,6 +147,7 @@
     come_YY1 = swap(ready_YY1, "y", 1)
     rows_1 = rows_1[0] + come_YY1
     ready_Z2 = rows_2[..., 8:, :]
+    ready_Z2, *_ = lax.optimization_barrier((ready_Z2, ready_YY1))
     come_Z2 = swap(ready_Z2, "zh", 0)
     rows_2 = rows_2[..., :8, :] + come_Z2
     ready_ZZ0 = rows_0[..., 4:, :]

time: 71.9 us -> 71.9 us (level)
  no operation moved by 1% of the time
where the time goes in v7:
time: 71.9 us; the launch traced here: 71.3 us
  starting transfers between devices  36.5 us (51%)
  waiting for transfers between devices  25 us (35%)
  Pallas kernels  4.44 us (6%)
  other arithmetic  2.36 us (3%)
  between operations  2.16 us (3%)
  local copies, waits for them, and re-layouts  0.8 us (1%)
    ppermute x12, starting transfers between devices, swap(): return lax.ppermute(x, SHARD, pairs)  28.1 us
    ppermute x12, waiting for transfers between devices, swap(): return lax.ppermute(x, SHARD, pairs)  18.9 us
    ppermute x9, starting transfers between devices, ring(): return lax.ppermute(x, axis, [(i, (i + by) % n) for i in range(n)])  8.45 us
    ppermute x9, waiting for transfers between devices, ring(): return lax.ppermute(x, axis, [(i, (i + by) % n) for i in range(n)])  6.05 us
    pallas_call x2, Pallas kernels, split_cores(): pl.pallas_call(functools.partial(split_kernel, steps), out_shape=(pltpu.V...  4.44 us
  transfers between devices with their start and end apart: 21, of which 9 were waited for; matrix products, arithmetic and copies ran while one was open for 2% of the time, Pallas kernels for 4%

profile of v7, /device:TPU:24, one launch (start us, length us, event | category | flops | bytes accessed | tf_op | source)
XLA Modules:
  0.0 71.3 jit_solution(18402359326962894559)
XLA Ops:
  0.6 1.8 %shard_map.76 = (f32[2,16,5120]{2,1,0:T(8,128)S(1)}, f32[2,16,5120]{2,1,0:T(8,128)S(1)}, f32[2,16,5120]{2,1,0:T(8,128)S(1)}, f32[2,16,5120]{2,1,0:T(8,128)S(1)}) custom-call(f32[3,1,1,128,5120]{4,3,2,1,0:T(8,128)} %g_ref.3), custom_call_target="tpu_custom_call" | custom-call | bytes 2621440 | tf_op jit(solution)/shard_map/pallas_call | solution.py:89
  2.5 2.6 %shard_map.77 = (f32[2,16,5120]{2,1,0:T(8,128)S(1)}, f32[2,16,5120]{2,1,0:T(8,128)S(1)}, f32[2,16,5120]{2,1,0:T(8,128)S(1)}, f32[2,16,5120]{2,1,0:T(8,128)S(1)},...) custom-call(f32[3,1,1,128,5120]{4,3,2,1,0:T(8,128)} %g_ref.3), custom_call_target="tpu_custom_call" | custom-call | bytes 5242880 | tf_op jit(solution)/shard_map/pallas_call | solution.py:89
  6.3 0.8 %collective-permute-start.2 = (f32[2,16,5120]{2,1,0:T(8,128)S(1)}, f32[2,16,5120]{2,1,0:T(8,128)S(1)}, u32[]{:S(2)}, u32[]{:S(2)}) collective-permute-start(f32[2,16,5120]{2,1,0:T(8,128)S(1)} %add.90), channel_id=1, source_target_pairs={{0,8},{1,25},{2,10},{3,27},{4,12},{5,29},{6,14},{7,31},{8,0},{9,17... | collective-permute-start | bytes 1966088 | tf_op jit(solution)/shard_map/ppermute | solution.py:38
  7.2 1.0 %collective-permute-start.7 = (f32[2,16,5120]{2,1,0:T(8,128)S(1)}, f32[2,16,5120]{2,1,0:T(8,128)S(1)}, u32[]{:S(2)}, u32[]{:S(2)}) collective-permute-start(f32[2,16,5120]{2,1,0:T(8,128)S(1)} %get-tuple-element.34), channel_id=1, source_target_pairs={{0,1},{1,0},{2,3},{3,2},{4,5},{5,4},{6,7},{7,6},{8,9},{9,8},{10,11... | collective-permute-start | bytes 1966088 | tf_op jit(solution)/shard_map/ppermute | solution.py:23
  10.6 1.4 %collective-permute-start.16 = (f32[2,16,5120]{2,1,0:T(8,128)S(1)}, f32[2,16,5120]{2,1,0:T(8,128)S(1)}, u32[]{:S(2)}, u32[]{:S(2)}) collective-permute-start(f32[2,16,5120]{2,1,0:T(8,128)S(1)} %add.108), channel_id=1, source_target_pairs={{0,8},{1,25},{2,10},{3,27},{4,12},{5,29},{6,14},{7,31},{8,0},{9,17... | collective-permute-start | bytes 1966088 | tf_op jit(solution)/shard_map/ppermute | solution.py:38
  12.0 5.0 %collective-permute-done.2 = f32[2,16,5120]{2,1,0:T(8,128)S(1)} collective-permute-done((f32[2,16,5120]{2,1,0:T(8,128)S(1)}, f32[2,16,5120]{2,1,0:T(8,128)S(1)}, u32[]{:S(2)}, u32[]{:S(2)}) %collective-permute-start.2) | collective-permute-done | bytes 655392 | tf_op jit(solution)/shard_map/ppermute | solution.py:38
  17.1 3.4 %collective-permute-start.3 = (f32[2,8,5120]{2,1,0:T(8,128)S(1)}, f32[2,8,5120]{2,1,0:T(8,128)S(1)}, u32[]{:S(2)}, u32[]{:S(2)}) collective-permute-start(f32[2,8,5120]{2,1,0:T(8,128)S(1)} %slice.85), channel_id=1, source_target_pairs={{0,2},{1,7},{2,0},{3,5},{4,6},{5,3},{6,4},{7,1},{8,10},{9,15},{10,... | collective-permute-start | bytes 983048 | tf_op jit(solution)/shard_map/ppermute | solution.py:38
  20.5 3.5 %collective-permute-done.9 = f32[2,16,5120]{2,1,0:T(8,128)S(1)} collective-permute-done((f32[2,16,5120]{2,1,0:T(8,128)S(1)}, f32[2,16,5120]{2,1,0:T(8,128)S(1)}, u32[]{:S(2)}, u32[]{:S(2)}) %collective-permute-start.9) | collective-permute-done | bytes 655392 | tf_op jit(solution)/shard_map/ppermute | solution.py:38
  24.2 3.4 %collective-permute-start.10 = (f32[2,8,5120]{2,1,0:T(8,128)S(1)}, f32[2,8,5120]{2,1,0:T(8,128)S(1)}, u32[]{:S(2)}, u32[]{:S(2)}) collective-permute-start(f32[2,8,5120]{2,1,0:T(8,128)S(1)} %slice.91), channel_id=1, source_target_pairs={{0,2},{1,7},{2,0},{3,5},{4,6},{5,3},{6,4},{7,1},{8,10},{9,15},{10,... | collective-permute-start | bytes 983048 | tf_op jit(solution)/shard_map/ppermute | solution.py:38
  27.5 3.5 %collective-permute-done.16 = f32[2,16,5120]{2,1,0:T(8,128)S(1)} collective-permute-done((f32[2,16,5120]{2,1,0:T(8,128)S(1)}, f32[2,16,5120]{2,1,0:T(8,128)S(1)}, u32[]{:S(2)}, u32[]{:S(2)}) %collective-permute-start.16) | collective-permute-done | bytes 655392 | tf_op jit(solution)/shard_map/ppermute | solution.py:38
  31.2 2.0 %collective-permute-start.17 = (f32[16,5120]{1,0:T(8,128)S(1)}, f32[16,5120]{1,0:T(8,128)S(1)}, u32[]{:S(2)}, u32[]{:S(2)}) collective-permute-start(f32[16,5120]{1,0:T(8,128)S(1)} %slice_bitcast_fusion), channel_id=1, source_target_pairs={{0,24},{1,9},{2,26},{3,11},{4,28},{5,13},{6,30},{7,15},{8,16},{9,1... | collective-permute-start | bytes 983048 | tf_op jit(solution)/shard_map/ppermute | solution.py:38
  33.3 1.4 %collective-permute-start.4 = (f32[8,5120]{1,0:T(8,128)S(1)}, f32[8,5120]{1,0:T(8,128)S(1)}, u32[]{:S(2)}, u32[]{:S(2)}) collective-permute-start(f32[8,5120]{1,0:T(8,128)S(1)} %slice_bitcast_fusion.4), channel_id=1, source_target_pairs={{0,24},{1,9},{2,26},{3,11},{4,28},{5,13},{6,30},{7,15},{8,16},{9,1... | collective-permute-start | bytes 491528 | tf_op jit(solution)/shard_map/ppermute | solution.py:38
  34.7 2.5 %collective-permute-done.10 = f32[2,8,5120]{2,1,0:T(8,128)S(1)} collective-permute-done((f32[2,8,5120]{2,1,0:T(8,128)S(1)}, f32[2,8,5120]{2,1,0:T(8,128)S(1)}, u32[]{:S(2)}, u32[]{:S(2)}) %collective-permute-start.10) | collective-permute-done | bytes 327712 | tf_op jit(solution)/shard_map/ppermute | solution.py:38
  37.6 2.0 %collective-permute-done.17 = f32[16,5120]{1,0:T(8,128)S(1)} collective-permute-done((f32[16,5120]{1,0:T(8,128)S(1)}, f32[16,5120]{1,0:T(8,128)S(1)}, u32[]{:S(2)}, u32[]{:S(2)}) %collective-permute-start.17) | collective-permute-done | bytes 327712 | tf_op jit(solution)/shard_map/ppermute | solution.py:38
  39.6 3.4 %collective-permute-start.18 = (f32[8,5120]{1,0:T(8,128)S(1)}, f32[8,5120]{1,0:T(8,128)S(1)}, u32[]{:S(2)}, u32[]{:S(2)}) collective-permute-start(f32[8,5120]{1,0:T(8,128)S(1)} %slice.99), channel_id=1, source_target_pairs={{0,2},{1,7},{2,0},{3,5},{4,6},{5,3},{6,4},{7,1},{8,10},{9,15},{10,... | collective-permute-start | bytes 491528 | tf_op jit(solution)/shard_map/ppermute | solution.py:38
  43.0 4.7 %collective-permute-start.5 = (f32[4,5120]{1,0:T(4,128)S(1)}, f32[4,5120]{1,0:T(4,128)S(1)}, u32[]{:S(2)}, u32[]{:S(2)}) collective-permute-start(f32[4,5120]{1,0:T(4,128)S(1)} %slice.89), channel_id=1, source_target_pairs={{0,6},{1,3},{2,4},{3,1},{4,2},{5,7},{6,0},{7,5},{8,14},{9,11},{10,... | collective-permute-start | bytes 245768 | tf_op jit(solution)/shard_map/ppermute | solution.py:38
  47.8 1.7 %collective-permute-start.12 = (f32[4,5120]{1,0:T(4,128)S(1)}, f32[4,5120]{1,0:T(4,128)S(1)}, u32[]{:S(2)}, u32[]{:S(2)}) collective-permute-start(f32[4,5120]{1,0:T(4,128)S(1)} %slice.95), channel_id=1, source_target_pairs={{0,6},{1,3},{2,4},{3,1},{4,2},{5,7},{6,0},{7,5},{8,14},{9,11},{10,... | collective-permute-start | bytes 245768 | tf_op jit(solution)/shard_map/ppermute | solution.py:38
  50.5 2.7 %collective-permute-start.6 = (f32[1,4,5248]{2,1,0:T(4,128)S(1)}, f32[1,4,5248]{2,1,0:T(4,128)S(1)}, u32[]{:S(2)}, u32[]{:S(2)}) collective-permute-start(f32[1,4,5248]{2,1,0:T(4,128)S(1)} %get-tuple-element.32), channel_id=1, source_target_pairs={{0,32},{32,64},{64,96},{96,128},{128,160},{160,192},{192,224},{224... | collective-permute-start | bytes 251912 | tf_op jit(solution)/shard_map/ppermute | solution.py:23
  53.1 4.8 %collective-permute-start.19 = (f32[4,5120]{1,0:T(4,128)S(1)}, f32[4,5120]{1,0:T(4,128)S(1)}, u32[]{:S(2)}, u32[]{:S(2)}) collective-permute-start(f32[4,5120]{1,0:T(4,128)S(1)} %slice.101), channel_id=1, source_target_pairs={{0,6},{1,3},{2,4},{3,1},{4,2},{5,7},{6,0},{7,5},{8,14},{9,11},{10,... | collective-permute-start | bytes 245768 | tf_op jit(solution)/shard_map/ppermute | solution.py:38
  58.0 1.6 %collective-permute-start.13 = (f32[1,4,5248]{2,1,0:T(4,128)S(1)}, f32[1,4,5248]{2,1,0:T(4,128)S(1)}, u32[]{:S(2)}, u32[]{:S(2)}) collective-permute-start(f32[1,4,5248]{2,1,0:T(4,128)S(1)} %get-tuple-element.39), channel_id=1, source_target_pairs={{0,64},{32,96},{64,128},{96,160},{128,192},{160,224},{192,0},{224,... | collective-permute-start | bytes 251912 | tf_op jit(solution)/shard_map/ppermute | solution.py:23
  59.6 1.6 %collective-permute-done.19 = f32[4,5120]{1,0:T(4,128)S(1)} collective-permute-done((f32[4,5120]{1,0:T(4,128)S(1)}, f32[4,5120]{1,0:T(4,128)S(1)}, u32[]{:S(2)}, u32[]{:S(2)}) %collective-permute-start.19) | collective-permute-done | bytes 81952 | tf_op jit(solution)/shard_map/ppermute | solution.py:38
  61.9 1.9 %collective-permute-done.13 = f32[1,4,5248]{2,1,0:T(4,128)S(1)} collective-permute-done((f32[1,4,5248]{2,1,0:T(4,128)S(1)}, f32[1,4,5248]{2,1,0:T(4,128)S(1)}, u32[]{:S(2)}, u32[]{:S(2)}) %collective-permute-start.13) | collective-permute-done | bytes 84000 | tf_op jit(solution)/shard_map/ppermute | solution.py:23
  63.8 1.9 %collective-permute-start.20 = (f32[1,4,5248]{2,1,0:T(4,128)S(1)}, f32[1,4,5248]{2,1,0:T(4,128)S(1)}, u32[]{:S(2)}, u32[]{:S(2)}) collective-permute-start(f32[1,4,5248]{2,1,0:T(4,128)S(1)} %get-tuple-element.49), channel_id=1, source_target_pairs={{0,128},{32,160},{64,192},{96,224},{128,0},{160,32},{192,64},{224,... | collective-permute-start | bytes 251912 | tf_op jit(solution)/shard_map/ppermute | solution.py:23
  65.7 4.2 %collective-permute-done.20 = f32[1,4,5248]{2,1,0:T(4,128)S(1)} collective-permute-done((f32[1,4,5248]{2,1,0:T(4,128)S(1)}, f32[1,4,5248]{2,1,0:T(4,128)S(1)}, u32[]{:S(2)}, u32[]{:S(2)}) %collective-permute-start.20) | collective-permute-done | bytes 84000 | tf_op jit(solution)/shard_map/ppermute | solution.py:23
  (55 shorter events, 6.4 us)
Async XLA Ops:
  2.4 3.8 %collective-permute-start.1 = (f32[2,16,5120]{2,1,0:T(8,128)S(1)}, f32[2,16,5120]{2,1,0:T(8,128)S(1)}, u32[]{:S(2)}, u32[]{:S(2)}) collective-permute-start(f32[2,16,5120]{2,1,0:T(8,128)S(1)} %get-tuple-element.30), channel_id=1, source_target_pairs={{0,1},{1,0},{2,3},{3,2},{4,5},{5,4},{6,7},{7,6},{8,9},{9,8},{10,11... | collective-permute-start | bytes 1966088 | tf_op jit(solution)/shard_map/ppermute | solution.py:23
  5.2 4.3 %collective-permute-start.8 = (f32[2,16,5120]{2,1,0:T(8,128)S(1)}, f32[2,16,5120]{2,1,0:T(8,128)S(1)}, u32[]{:S(2)}, u32[]{:S(2)}) collective-permute-start(f32[2,16,5120]{2,1,0:T(8,128)S(1)} %get-tuple-element.36), channel_id=1, source_target_pairs={{0,1},{1,0},{2,3},{3,2},{4,5},{5,4},{6,7},{7,6},{8,9},{9,8},{10,11... | collective-permute-start | bytes 1966088 | tf_op jit(solution)/shard_map/ppermute | solution.py:23
  5.7 3.9 %collective-permute-start.15 = (f32[2,16,5120]{2,1,0:T(8,128)S(1)}, f32[2,16,5120]{2,1,0:T(8,128)S(1)}, u32[]{:S(2)}, u32[]{:S(2)}) collective-permute-start(f32[2,16,5120]{2,1,0:T(8,128)S(1)} %get-tuple-element.43), channel_id=1, source_target_pairs={{0,1},{1,0},{2,3},{3,2},{4,5},{5,4},{6,7},{7,6},{8,9},{9,8},{10,11... | collective-permute-start | bytes 1966088 | tf_op jit(solution)/shard_map/ppermute | solution.py:23
  5.8 4.7 %collective-permute-start = (f32[2,16,5120]{2,1,0:T(8,128)S(1)}, f32[2,16,5120]{2,1,0:T(8,128)S(1)}, u32[]{:S(2)}, u32[]{:S(2)}) collective-permute-start(f32[2,16,5120]{2,1,0:T(8,128)S(1)} %get-tuple-element.28), channel_id=1, source_target_pairs={{0,1},{1,0},{2,3},{3,2},{4,5},{5,4},{6,7},{7,6},{8,9},{9,8},{10,11... | collective-permute-start | bytes 1966088 | tf_op jit(solution)/shard_map/ppermute | solution.py:23
  6.3 10.7 %collective-permute-start.2 = (f32[2,16,5120]{2,1,0:T(8,128)S(1)}, f32[2,16,5120]{2,1,0:T(8,128)S(1)}, u32[]{:S(2)}, u32[]{:S(2)}) collective-permute-start(f32[2,16,5120]{2,1,0:T(8,128)S(1)} %add.90), channel_id=1, source_target_pairs={{0,8},{1,25},{2,10},{3,27},{4,12},{5,29},{6,14},{7,31},{8,0},{9,17... | collective-permute-start | bytes 1966088 | tf_op jit(solution)/shard_map/ppermute | solution.py:38
  7.2 13.3 %collective-permute-start.7 = (f32[2,16,5120]{2,1,0:T(8,128)S(1)}, f32[2,16,5120]{2,1,0:T(8,128)S(1)}, u32[]{:S(2)}, u32[]{:S(2)}) collective-permute-start(f32[2,16,5120]{2,1,0:T(8,128)S(1)} %get-tuple-element.34), channel_id=1, source_target_pairs={{0,1},{1,0},{2,3},{3,2},{4,5},{5,4},{6,7},{7,6},{8,9},{9,8},{10,11... | collective-permute-start | bytes 1966088 | tf_op jit(solution)/shard_map/ppermute | solution.py:23
  9.5 18.0 %collective-permute-start.14 = (f32[2,16,5120]{2,1,0:T(8,128)S(1)}, f32[2,16,5120]{2,1,0:T(8,128)S(1)}, u32[]{:S(2)}, u32[]{:S(2)}) collective-permute-start(f32[2,16,5120]{2,1,0:T(8,128)S(1)} %get-tuple-element.41), channel_id=1, source_target_pairs={{0,1},{1,0},{2,3},{3,2},{4,5},{5,4},{6,7},{7,6},{8,9},{9,8},{10,11... | collective-permute-start | bytes 1966088 | tf_op jit(solution)/shard_map/ppermute | solution.py:23
  9.7 14.3 %collective-permute-start.9 = (f32[2,16,5120]{2,1,0:T(8,128)S(1)}, f32[2,16,5120]{2,1,0:T(8,128)S(1)}, u32[]{:S(2)}, u32[]{:S(2)}) collective-permute-start(f32[2,16,5120]{2,1,0:T(8,128)S(1)} %add.99), channel_id=1, source_target_pairs={{0,8},{1,25},{2,10},{3,27},{4,12},{5,29},{6,14},{7,31},{8,0},{9,17... | collective-permute-start | bytes 1966088 | tf_op jit(solution)/shard_map/ppermute | solution.py:38
  10.6 20.4 %collective-permute-start.16 = (f32[2,16,5120]{2,1,0:T(8,128)S(1)}, f32[2,16,5120]{2,1,0:T(8,128)S(1)}, u32[]{:S(2)}, u32[]{:S(2)}) collective-permute-start(f32[2,16,5120]{2,1,0:T(8,128)S(1)} %add.108), channel_id=1, source_target_pairs={{0,8},{1,25},{2,10},{3,27},{4,12},{5,29},{6,14},{7,31},{8,0},{9,17... | collective-permute-start | bytes 1966088 | tf_op jit(solution)/shard_map/ppermute | solution.py:38
  17.0 33.3 %copy-start.1 = (f32[1,4,5120]{2,1,0:T(4,128)S(1)}, f32[1,4,5120]{2,1,0:T(4,128)}, u32[]{:S(2)}) copy-start(f32[1,4,5120]{2,1,0:T(4,128)} %param.8) | copy-start | bytes 245764
  17.0 33.4 %copy-start = (f32[1,4,5120]{2,1,0:T(4,128)S(1)}, f32[1,4,5120]{2,1,0:T(4,128)}, u32[]{:S(2)}) copy-start(f32[1,4,5120]{2,1,0:T(4,128)} %param.5) | copy-start | bytes 245764
  17.1 16.1 %collective-permute-start.3 = (f32[2,8,5120]{2,1,0:T(8,128)S(1)}, f32[2,8,5120]{2,1,0:T(8,128)S(1)}, u32[]{:S(2)}, u32[]{:S(2)}) collective-permute-start(f32[2,8,5120]{2,1,0:T(8,128)S(1)} %slice.85), channel_id=1, source_target_pairs={{0,2},{1,7},{2,0},{3,5},{4,6},{5,3},{6,4},{7,1},{8,10},{9,15},{10,... | collective-permute-start | bytes 983048 | tf_op jit(solution)/shard_map/ppermute | solution.py:38
  24.2 13.0 %collective-permute-start.10 = (f32[2,8,5120]{2,1,0:T(8,128)S(1)}, f32[2,8,5120]{2,1,0:T(8,128)S(1)}, u32[]{:S(2)}, u32[]{:S(2)}) collective-permute-start(f32[2,8,5120]{2,1,0:T(8,128)S(1)} %slice.91), channel_id=1, source_target_pairs={{0,2},{1,7},{2,0},{3,5},{4,6},{5,3},{6,4},{7,1},{8,10},{9,15},{10,... | collective-permute-start | bytes 983048 | tf_op jit(solution)/shard_map/ppermute | solution.py:38
  31.2 8.4 %collective-permute-start.17 = (f32[16,5120]{1,0:T(8,128)S(1)}, f32[16,5120]{1,0:T(8,128)S(1)}, u32[]{:S(2)}, u32[]{:S(2)}) collective-permute-start(f32[16,5120]{1,0:T(8,128)S(1)} %slice_bitcast_fusion), channel_id=1, source_target_pairs={{0,24},{1,9},{2,26},{3,11},{4,28},{5,13},{6,30},{7,15},{8,16},{9,1... | collective-permute-start | bytes 983048 | tf_op jit(solution)/shard_map/ppermute | solution.py:38
  33.3 9.7 %collective-permute-start.4 = (f32[8,5120]{1,0:T(8,128)S(1)}, f32[8,5120]{1,0:T(8,128)S(1)}, u32[]{:S(2)}, u32[]{:S(2)}) collective-permute-start(f32[8,5120]{1,0:T(8,128)S(1)} %slice_bitcast_fusion.4), channel_id=1, source_target_pairs={{0,24},{1,9},{2,26},{3,11},{4,28},{5,13},{6,30},{7,15},{8,16},{9,1... | collective-permute-start | bytes 491528 | tf_op jit(solution)/shard_map/ppermute | solution.py:38
  37.2 10.6 %collective-permute-start.11 = (f32[8,5120]{1,0:T(8,128)S(1)}, f32[8,5120]{1,0:T(8,128)S(1)}, u32[]{:S(2)}, u32[]{:S(2)}) collective-permute-start(f32[8,5120]{1,0:T(8,128)S(1)} %slice_bitcast_fusion.2), channel_id=1, source_target_pairs={{0,24},{1,9},{2,26},{3,11},{4,28},{5,13},{6,30},{7,15},{8,16},{9,1... | collective-permute-start | bytes 491528 | tf_op jit(solution)/shard_map/ppermute | solution.py:38
  39.6 9.9 %collective-permute-start.18 = (f32[8,5120]{1,0:T(8,128)S(1)}, f32[8,5120]{1,0:T(8,128)S(1)}, u32[]{:S(2)}, u32[]{:S(2)}) collective-permute-start(f32[8,5120]{1,0:T(8,128)S(1)} %slice.99), channel_id=1, source_target_pairs={{0,2},{1,7},{2,0},{3,5},{4,6},{5,3},{6,4},{7,1},{8,10},{9,15},{10,... | collective-permute-start | bytes 491528 | tf_op jit(solution)/shard_map/ppermute | solution.py:38
  43.0 7.3 %collective-permute-start.5 = (f32[4,5120]{1,0:T(4,128)S(1)}, f32[4,5120]{1,0:T(4,128)S(1)}, u32[]{:S(2)}, u32[]{:S(2)}) collective-permute-start(f32[4,5120]{1,0:T(4,128)S(1)} %slice.89), channel_id=1, source_target_pairs={{0,6},{1,3},{2,4},{3,1},{4,2},{5,7},{6,0},{7,5},{8,14},{9,11},{10,... | collective-permute-start | bytes 245768 | tf_op jit(solution)/shard_map/ppermute | solution.py:38
  47.8 10.1 %collective-permute-start.12 = (f32[4,5120]{1,0:T(4,128)S(1)}, f32[4,5120]{1,0:T(4,128)S(1)}, u32[]{:S(2)}, u32[]{:S(2)}) collective-permute-start(f32[4,5120]{1,0:T(4,128)S(1)} %slice.95), channel_id=1, source_target_pairs={{0,6},{1,3},{2,4},{3,1},{4,2},{5,7},{6,0},{7,5},{8,14},{9,11},{10,... | collective-permute-start | bytes 245768 | tf_op jit(solution)/shard_map/ppermute | solution.py:38
  50.5 7.5 %collective-permute-start.6 = (f32[1,4,5248]{2,1,0:T(4,128)S(1)}, f32[1,4,5248]{2,1,0:T(4,128)S(1)}, u32[]{:S(2)}, u32[]{:S(2)}) collective-permute-start(f32[1,4,5248]{2,1,0:T(4,128)S(1)} %get-tuple-element.32), channel_id=1, source_target_pairs={{0,32},{32,64},{64,96},{96,128},{128,160},{160,192},{192,224},{224... | collective-permute-start | bytes 251912 | tf_op jit(solution)/shard_map/ppermute | solution.py:23
  53.1 8.1 %collective-permute-start.19 = (f32[4,5120]{1,0:T(4,128)S(1)}, f32[4,5120]{1,0:T(4,128)S(1)}, u32[]{:S(2)}, u32[]{:S(2)}) collective-permute-start(f32[4,5120]{1,0:T(4,128)S(1)} %slice.101), channel_id=1, source_target_pairs={{0,6},{1,3},{2,4},{3,1},{4,2},{5,7},{6,0},{7,5},{8,14},{9,11},{10,... | collective-permute-start | bytes 245768 | tf_op jit(solution)/shard_map/ppermute | solution.py:38
  58.0 5.8 %collective-permute-start.13 = (f32[1,4,5248]{2,1,0:T(4,128)S(1)}, f32[1,4,5248]{2,1,0:T(4,128)S(1)}, u32[]{:S(2)}, u32[]{:S(2)}) collective-permute-start(f32[1,4,5248]{2,1,0:T(4,128)S(1)} %get-tuple-element.39), channel_id=1, source_target_pairs={{0,64},{32,96},{64,128},{96,160},{128,192},{160,224},{192,0},{224,... | collective-permute-start | bytes 251912 | tf_op jit(solution)/shard_map/ppermute | solution.py:23
  63.8 6.1 %collective-permute-start.20 = (f32[1,4,5248]{2,1,0:T(4,128)S(1)}, f32[1,4,5248]{2,1,0:T(4,128)S(1)}, u32[]{:S(2)}, u32[]{:S(2)}) collective-permute-start(f32[1,4,5248]{2,1,0:T(4,128)S(1)} %get-tuple-element.49), channel_id=1, source_target_pairs={{0,128},{32,160},{64,192},{96,224},{128,0},{160,32},{192,64},{224,... | collective-permute-start | bytes 251912 | tf_op jit(solution)/shard_map/ppermute | solution.py:23

commit v8 on v6

--- a/solution.py
+++ b/solution.py
@@ -9,7 +9,7 @@
 
 STEPS = 3
 D = 5120
-STRIP = 1024
+STRIP = 256
 X, ZL, Y, ZH, CORE = 4, 2, 4, 4, 2
 GROUP = ("x", "zl")
 SHARD = ("y", "zh", "core")

time: 71.9 us -> 71.9 us (level)
  no operation moved by 1% of the time
where the time goes in v8:
time: 71.9 us; the launch traced here: 71.3 us
  starting transfers between devices  36.5 us (51%)
  waiting for transfers between devices  25 us (35%)
  Pallas kernels  4.44 us (6%)
  other arithmetic  2.36 us (3%)
  between operations  2.16 us (3%)
  local copies, waits for them, and re-layouts  0.8 us (1%)
    ppermute x12, starting transfers between devices, swap(): return lax.ppermute(x, SHARD, pairs)  28.1 us
    ppermute x12, waiting for transfers between devices, swap(): return lax.ppermute(x, SHARD, pairs)  18.9 us
    ppermute x9, starting transfers between devices, ring(): return lax.ppermute(x, axis, [(i, (i + by) % n) for i in range(n)])  8.45 us
    ppermute x9, waiting for transfers between devices, ring(): return lax.ppermute(x, axis, [(i, (i + by) % n) for i in range(n)])  6.05 us
    pallas_call x2, Pallas kernels, split_cores(): pl.pallas_call(functools.partial(split_kernel, steps), out_shape=(pltpu.V...  4.44 us
  transfers between devices with their start and end apart: 21, of which 9 were waited for; matrix products, arithmetic and copies ran while one was open for 2% of the time, Pallas kernels for 4%

profile of v8, /device:TPU:24, one launch (start us, length us, event | category | flops | bytes accessed | tf_op | source)
XLA Modules:
  0.0 71.3 jit_solution(9746899392820480130)
XLA Ops:
  0.6 1.8 %shard_map.76 = (f32[2,16,5120]{2,1,0:T(8,128)S(1)}, f32[2,16,5120]{2,1,0:T(8,128)S(1)}, f32[2,16,5120]{2,1,0:T(8,128)S(1)}, f32[2,16,5120]{2,1,0:T(8,128)S(1)}) custom-call(f32[3,1,1,128,5120]{4,3,2,1,0:T(8,128)} %g_ref.3), custom_call_target="tpu_custom_call" | custom-call | bytes 2621440 | tf_op jit(solution)/shard_map/pallas_call | solution.py:89
  2.5 2.6 %shard_map.77 = (f32[2,16,5120]{2,1,0:T(8,128)S(1)}, f32[2,16,5120]{2,1,0:T(8,128)S(1)}, f32[2,16,5120]{2,1,0:T(8,128)S(1)}, f32[2,16,5120]{2,1,0:T(8,128)S(1)},...) custom-call(f32[3,1,1,128,5120]{4,3,2,1,0:T(8,128)} %g_ref.3), custom_call_target="tpu_custom_call" | custom-call | bytes 5242880 | tf_op jit(solution)/shard_map/pallas_call | solution.py:89
  6.3 0.8 %collective-permute-start.2 = (f32[2,16,5120]{2,1,0:T(8,128)S(1)}, f32[2,16,5120]{2,1,0:T(8,128)S(1)}, u32[]{:S(2)}, u32[]{:S(2)}) collective-permute-start(f32[2,16,5120]{2,1,0:T(8,128)S(1)} %add.90), channel_id=1, source_target_pairs={{0,8},{1,25},{2,10},{3,27},{4,12},{5,29},{6,14},{7,31},{8,0},{9,17... | collective-permute-start | bytes 1966088 | tf_op jit(solution)/shard_map/ppermute | solution.py:38
  7.2 1.0 %collective-permute-start.7 = (f32[2,16,5120]{2,1,0:T(8,128)S(1)}, f32[2,16,5120]{2,1,0:T(8,128)S(1)}, u32[]{:S(2)}, u32[]{:S(2)}) collective-permute-start(f32[2,16,5120]{2,1,0:T(8,128)S(1)} %get-tuple-element.33), channel_id=1, source_target_pairs={{0,1},{1,0},{2,3},{3,2},{4,5},{5,4},{6,7},{7,6},{8,9},{9,8},{10,11... | collective-permute-start | bytes 1966088 | tf_op jit(solution)/shard_map/ppermute | solution.py:23
  10.6 1.4 %collective-permute-start.16 = (f32[2,16,5120]{2,1,0:T(8,128)S(1)}, f32[2,16,5120]{2,1,0:T(8,128)S(1)}, u32[]{:S(2)}, u32[]{:S(2)}) collective-permute-start(f32[2,16,5120]{2,1,0:T(8,128)S(1)} %add.108), channel_id=1, source_target_pairs={{0,8},{1,25},{2,10},{3,27},{4,12},{5,29},{6,14},{7,31},{8,0},{9,17... | collective-permute-start | bytes 1966088 | tf_op jit(solution)/shard_map/ppermute | solution.py:38
  12.0 5.0 %collective-permute-done.2 = f32[2,16,5120]{2,1,0:T(8,128)S(1)} collective-permute-done((f32[2,16,5120]{2,1,0:T(8,128)S(1)}, f32[2,16,5120]{2,1,0:T(8,128)S(1)}, u32[]{:S(2)}, u32[]{:S(2)}) %collective-permute-start.2) | collective-permute-done | bytes 655392 | tf_op jit(solution)/shard_map/ppermute | solution.py:38
  17.1 3.4 %collective-permute-start.3 = (f32[2,8,5120]{2,1,0:T(8,128)S(1)}, f32[2,8,5120]{2,1,0:T(8,128)S(1)}, u32[]{:S(2)}, u32[]{:S(2)}) collective-permute-start(f32[2,8,5120]{2,1,0:T(8,128)S(1)} %slice.85), channel_id=1, source_target_pairs={{0,2},{1,7},{2,0},{3,5},{4,6},{5,3},{6,4},{7,1},{8,10},{9,15},{10,... | collective-permute-start | bytes 983048 | tf_op jit(solution)/shard_map/ppermute | solution.py:38
  20.5 3.5 %collective-permute-done.9 = f32[2,16,5120]{2,1,0:T(8,128)S(1)} collective-permute-done((f32[2,16,5120]{2,1,0:T(8,128)S(1)}, f32[2,16,5120]{2,1,0:T(8,128)S(1)}, u32[]{:S(2)}, u32[]{:S(2)}) %collective-permute-start.9) | collective-permute-done | bytes 655392 | tf_op jit(solution)/shard_map/ppermute | solution.py:38
  24.2 3.4 %collective-permute-start.10 = (f32[2,8,5120]{2,1,0:T(8,128)S(1)}, f32[2,8,5120]{2,1,0:T(8,128)S(1)}, u32[]{:S(2)}, u32[]{:S(2)}) collective-permute-start(f32[2,8,5120]{2,1,0:T(8,128)S(1)} %slice.91), channel_id=1, source_target_pairs={{0,2},{1,7},{2,0},{3,5},{4,6},{5,3},{6,4},{7,1},{8,10},{9,15},{10,... | collective-permute-start | bytes 983048 | tf_op jit(solution)/shard_map/ppermute | solution.py:38
  27.5 3.5 %collective-permute-done.16 = f32[2,16,5120]{2,1,0:T(8,128)S(1)} collective-permute-done((f32[2,16,5120]{2,1,0:T(8,128)S(1)}, f32[2,16,5120]{2,1,0:T(8,128)S(1)}, u32[]{:S(2)}, u32[]{:S(2)}) %collective-permute-start.16) | collective-permute-done | bytes 655392 | tf_op jit(solution)/shard_map/ppermute | solution.py:38
  31.2 2.0 %collective-permute-start.17 = (f32[16,5120]{1,0:T(8,128)S(1)}, f32[16,5120]{1,0:T(8,128)S(1)}, u32[]{:S(2)}, u32[]{:S(2)}) collective-permute-start(f32[16,5120]{1,0:T(8,128)S(1)} %slice_bitcast_fusion), channel_id=1, source_target_pairs={{0,24},{1,9},{2,26},{3,11},{4,28},{5,13},{6,30},{7,15},{8,16},{9,1... | collective-permute-start | bytes 983048 | tf_op jit(solution)/shard_map/ppermute | solution.py:38
  33.3 1.4 %collective-permute-start.4 = (f32[8,5120]{1,0:T(8,128)S(1)}, f32[8,5120]{1,0:T(8,128)S(1)}, u32[]{:S(2)}, u32[]{:S(2)}) collective-permute-start(f32[8,5120]{1,0:T(8,128)S(1)} %slice_bitcast_fusion.4), channel_id=1, source_target_pairs={{0,24},{1,9},{2,26},{3,11},{4,28},{5,13},{6,30},{7,15},{8,16},{9,1... | collective-permute-start | bytes 491528 | tf_op jit(solution)/shard_map/ppermute | solution.py:38
  34.7 2.5 %collective-permute-done.10 = f32[2,8,5120]{2,1,0:T(8,128)S(1)} collective-permute-done((f32[2,8,5120]{2,1,0:T(8,128)S(1)}, f32[2,8,5120]{2,1,0:T(8,128)S(1)}, u32[]{:S(2)}, u32[]{:S(2)}) %collective-permute-start.10) | collective-permute-done | bytes 327712 | tf_op jit(solution)/shard_map/ppermute | solution.py:38
  37.6 2.0 %collective-permute-done.17 = f32[16,5120]{1,0:T(8,128)S(1)} collective-permute-done((f32[16,5120]{1,0:T(8,128)S(1)}, f32[16,5120]{1,0:T(8,128)S(1)}, u32[]{:S(2)}, u32[]{:S(2)}) %collective-permute-start.17) | collective-permute-done | bytes 327712 | tf_op jit(solution)/shard_map/ppermute | solution.py:38
  39.6 3.4 %collective-permute-start.18 = (f32[8,5120]{1,0:T(8,128)S(1)}, f32[8,5120]{1,0:T(8,128)S(1)}, u32[]{:S(2)}, u32[]{:S(2)}) collective-permute-start(f32[8,5120]{1,0:T(8,128)S(1)} %slice.99), channel_id=1, source_target_pairs={{0,2},{1,7},{2,0},{3,5},{4,6},{5,3},{6,4},{7,1},{8,10},{9,15},{10,... | collective-permute-start | bytes 491528 | tf_op jit(solution)/shard_map/ppermute | solution.py:38
  43.0 4.7 %collective-permute-start.5 = (f32[4,5120]{1,0:T(4,128)S(1)}, f32[4,5120]{1,0:T(4,128)S(1)}, u32[]{:S(2)}, u32[]{:S(2)}) collective-permute-start(f32[4,5120]{1,0:T(4,128)S(1)} %slice.89), channel_id=1, source_target_pairs={{0,6},{1,3},{2,4},{3,1},{4,2},{5,7},{6,0},{7,5},{8,14},{9,11},{10,... | collective-permute-start | bytes 245768 | tf_op jit(solution)/shard_map/ppermute | solution.py:38
  47.8 1.7 %collective-permute-start.12 = (f32[4,5120]{1,0:T(4,128)S(1)}, f32[4,5120]{1,0:T(4,128)S(1)}, u32[]{:S(2)}, u32[]{:S(2)}) collective-permute-start(f32[4,5120]{1,0:T(4,128)S(1)} %slice.95), channel_id=1, source_target_pairs={{0,6},{1,3},{2,4},{3,1},{4,2},{5,7},{6,0},{7,5},{8,14},{9,11},{10,... | collective-permute-start | bytes 245768 | tf_op jit(solution)/shard_map/ppermute | solution.py:38
  50.5 2.7 %collective-permute-start.6 = (f32[1,4,5248]{2,1,0:T(4,128)S(1)}, f32[1,4,5248]{2,1,0:T(4,128)S(1)}, u32[]{:S(2)}, u32[]{:S(2)}) collective-permute-start(f32[1,4,5248]{2,1,0:T(4,128)S(1)} %get-tuple-element.31), channel_id=1, source_target_pairs={{0,32},{32,64},{64,96},{96,128},{128,160},{160,192},{192,224},{224... | collective-permute-start | bytes 251912 | tf_op jit(solution)/shard_map/ppermute | solution.py:23
  53.1 4.8 %collective-permute-start.19 = (f32[4,5120]{1,0:T(4,128)S(1)}, f32[4,5120]{1,0:T(4,128)S(1)}, u32[]{:S(2)}, u32[]{:S(2)}) collective-permute-start(f32[4,5120]{1,0:T(4,128)S(1)} %slice.101), channel_id=1, source_target_pairs={{0,6},{1,3},{2,4},{3,1},{4,2},{5,7},{6,0},{7,5},{8,14},{9,11},{10,... | collective-permute-start | bytes 245768 | tf_op jit(solution)/shard_map/ppermute | solution.py:38
  58.0 1.6 %collective-permute-start.13 = (f32[1,4,5248]{2,1,0:T(4,128)S(1)}, f32[1,4,5248]{2,1,0:T(4,128)S(1)}, u32[]{:S(2)}, u32[]{:S(2)}) collective-permute-start(f32[1,4,5248]{2,1,0:T(4,128)S(1)} %get-tuple-element.38), channel_id=1, source_target_pairs={{0,64},{32,96},{64,128},{96,160},{128,192},{160,224},{192,0},{224,... | collective-permute-start | bytes 251912 | tf_op jit(solution)/shard_map/ppermute | solution.py:23
  59.6 1.6 %collective-permute-done.19 = f32[4,5120]{1,0:T(4,128)S(1)} collective-permute-done((f32[4,5120]{1,0:T(4,128)S(1)}, f32[4,5120]{1,0:T(4,128)S(1)}, u32[]{:S(2)}, u32[]{:S(2)}) %collective-permute-start.19) | collective-permute-done | bytes 81952 | tf_op jit(solution)/shard_map/ppermute | solution.py:38
  61.9 1.9 %collective-permute-done.13 = f32[1,4,5248]{2,1,0:T(4,128)S(1)} collective-permute-done((f32[1,4,5248]{2,1,0:T(4,128)S(1)}, f32[1,4,5248]{2,1,0:T(4,128)S(1)}, u32[]{:S(2)}, u32[]{:S(2)}) %collective-permute-start.13) | collective-permute-done | bytes 84000 | tf_op jit(solution)/shard_map/ppermute | solution.py:23
  63.8 1.9 %collective-permute-start.20 = (f32[1,4,5248]{2,1,0:T(4,128)S(1)}, f32[1,4,5248]{2,1,0:T(4,128)S(1)}, u32[]{:S(2)}, u32[]{:S(2)}) collective-permute-start(f32[1,4,5248]{2,1,0:T(4,128)S(1)} %get-tuple-element.47), channel_id=1, source_target_pairs={{0,128},{32,160},{64,192},{96,224},{128,0},{160,32},{192,64},{224,... | collective-permute-start | bytes 251912 | tf_op jit(solution)/shard_map/ppermute | solution.py:23
  65.7 4.2 %collective-permute-done.20 = f32[1,4,5248]{2,1,0:T(4,128)S(1)} collective-permute-done((f32[1,4,5248]{2,1,0:T(4,128)S(1)}, f32[1,4,5248]{2,1,0:T(4,128)S(1)}, u32[]{:S(2)}, u32[]{:S(2)}) %collective-permute-start.20) | collective-permute-done | bytes 84000 | tf_op jit(solution)/shard_map/ppermute | solution.py:23
  (55 shorter events, 6.4 us)
Async XLA Ops:
  2.4 3.8 %collective-permute-start.1 = (f32[2,16,5120]{2,1,0:T(8,128)S(1)}, f32[2,16,5120]{2,1,0:T(8,128)S(1)}, u32[]{:S(2)}, u32[]{:S(2)}) collective-permute-start(f32[2,16,5120]{2,1,0:T(8,128)S(1)} %get-tuple-element.29), channel_id=1, source_target_pairs={{0,1},{1,0},{2,3},{3,2},{4,5},{5,4},{6,7},{7,6},{8,9},{9,8},{10,11... | collective-permute-start | bytes 1966088 | tf_op jit(solution)/shard_map/ppermute | solution.py:23
  5.2 4.3 %collective-permute-start.8 = (f32[2,16,5120]{2,1,0:T(8,128)S(1)}, f32[2,16,5120]{2,1,0:T(8,128)S(1)}, u32[]{:S(2)}, u32[]{:S(2)}) collective-permute-start(f32[2,16,5120]{2,1,0:T(8,128)S(1)} %get-tuple-element.35), channel_id=1, source_target_pairs={{0,1},{1,0},{2,3},{3,2},{4,5},{5,4},{6,7},{7,6},{8,9},{9,8},{10,11... | collective-permute-start | bytes 1966088 | tf_op jit(solution)/shard_map/ppermute | solution.py:23
  5.7 3.9 %collective-permute-start.15 = (f32[2,16,5120]{2,1,0:T(8,128)S(1)}, f32[2,16,5120]{2,1,0:T(8,128)S(1)}, u32[]{:S(2)}, u32[]{:S(2)}) collective-permute-start(f32[2,16,5120]{2,1,0:T(8,128)S(1)} %get-tuple-element.42), channel_id=1, source_target_pairs={{0,1},{1,0},{2,3},{3,2},{4,5},{5,4},{6,7},{7,6},{8,9},{9,8},{10,11... | collective-permute-start | bytes 1966088 | tf_op jit(solution)/shard_map/ppermute | solution.py:23
  5.8 4.7 %collective-permute-start = (f32[2,16,5120]{2,1,0:T(8,128)S(1)}, f32[2,16,5120]{2,1,0:T(8,128)S(1)}, u32[]{:S(2)}, u32[]{:S(2)}) collective-permute-start(f32[2,16,5120]{2,1,0:T(8,128)S(1)} %get-tuple-element.27), channel_id=1, source_target_pairs={{0,1},{1,0},{2,3},{3,2},{4,5},{5,4},{6,7},{7,6},{8,9},{9,8},{10,11... | collective-permute-start | bytes 1966088 | tf_op jit(solution)/shard_map/ppermute | solution.py:23
  6.3 10.7 %collective-permute-start.2 = (f32[2,16,5120]{2,1,0:T(8,128)S(1)}, f32[2,16,5120]{2,1,0:T(8,128)S(1)}, u32[]{:S(2)}, u32[]{:S(2)}) collective-permute-start(f32[2,16,5120]{2,1,0:T(8,128)S(1)} %add.90), channel_id=1, source_target_pairs={{0,8},{1,25},{2,10},{3,27},{4,12},{5,29},{6,14},{7,31},{8,0},{9,17... | collective-permute-start | bytes 1966088 | tf_op jit(solution)/shard_map/ppermute | solution.py:38
  7.2 13.3 %collective-permute-start.7 = (f32[2,16,5120]{2,1,0:T(8,128)S(1)}, f32[2,16,5120]{2,1,0:T(8,128)S(1)}, u32[]{:S(2)}, u32[]{:S(2)}) collective-permute-start(f32[2,16,5120]{2,1,0:T(8,128)S(1)} %get-tuple-element.33), channel_id=1, source_target_pairs={{0,1},{1,0},{2,3},{3,2},{4,5},{5,4},{6,7},{7,6},{8,9},{9,8},{10,11... | collective-permute-start | bytes 1966088 | tf_op jit(solution)/shard_map/ppermute | solution.py:23
  9.5 18.0 %collective-permute-start.14 = (f32[2,16,5120]{2,1,0:T(8,128)S(1)}, f32[2,16,5120]{2,1,0:T(8,128)S(1)}, u32[]{:S(2)}, u32[]{:S(2)}) collective-permute-start(f32[2,16,5120]{2,1,0:T(8,128)S(1)} %get-tuple-element.40), channel_id=1, source_target_pairs={{0,1},{1,0},{2,3},{3,2},{4,5},{5,4},{6,7},{7,6},{8,9},{9,8},{10,11... | collective-permute-start | bytes 1966088 | tf_op jit(solution)/shard_map/ppermute | solution.py:23
  9.7 14.3 %collective-permute-start.9 = (f32[2,16,5120]{2,1,0:T(8,128)S(1)}, f32[2,16,5120]{2,1,0:T(8,128)S(1)}, u32[]{:S(2)}, u32[]{:S(2)}) collective-permute-start(f32[2,16,5120]{2,1,0:T(8,128)S(1)} %add.99), channel_id=1, source_target_pairs={{0,8},{1,25},{2,10},{3,27},{4,12},{5,29},{6,14},{7,31},{8,0},{9,17... | collective-permute-start | bytes 1966088 | tf_op jit(solution)/shard_map/ppermute | solution.py:38
  10.6 20.4 %collective-permute-start.16 = (f32[2,16,5120]{2,1,0:T(8,128)S(1)}, f32[2,16,5120]{2,1,0:T(8,128)S(1)}, u32[]{:S(2)}, u32[]{:S(2)}) collective-permute-start(f32[2,16,5120]{2,1,0:T(8,128)S(1)} %add.108), channel_id=1, source_target_pairs={{0,8},{1,25},{2,10},{3,27},{4,12},{5,29},{6,14},{7,31},{8,0},{9,17... | collective-permute-start | bytes 1966088 | tf_op jit(solution)/shard_map/ppermute | solution.py:38
  17.0 33.3 %copy-start.1 = (f32[1,4,5120]{2,1,0:T(4,128)S(1)}, f32[1,4,5120]{2,1,0:T(4,128)}, u32[]{:S(2)}) copy-start(f32[1,4,5120]{2,1,0:T(4,128)} %param.8) | copy-start | bytes 245764
  17.0 33.4 %copy-start = (f32[1,4,5120]{2,1,0:T(4,128)S(1)}, f32[1,4,5120]{2,1,0:T(4,128)}, u32[]{:S(2)}) copy-start(f32[1,4,5120]{2,1,0:T(4,128)} %param.5) | copy-start | bytes 245764
  17.1 16.1 %collective-permute-start.3 = (f32[2,8,5120]{2,1,0:T(8,128)S(1)}, f32[2,8,5120]{2,1,0:T(8,128)S(1)}, u32[]{:S(2)}, u32[]{:S(2)}) collective-permute-start(f32[2,8,5120]{2,1,0:T(8,128)S(1)} %slice.85), channel_id=1, source_target_pairs={{0,2},{1,7},{2,0},{3,5},{4,6},{5,3},{6,4},{7,1},{8,10},{9,15},{10,... | collective-permute-start | bytes 983048 | tf_op jit(solution)/shard_map/ppermute | solution.py:38
  24.2 13.0 %collective-permute-start.10 = (f32[2,8,5120]{2,1,0:T(8,128)S(1)}, f32[2,8,5120]{2,1,0:T(8,128)S(1)}, u32[]{:S(2)}, u32[]{:S(2)}) collective-permute-start(f32[2,8,5120]{2,1,0:T(8,128)S(1)} %slice.91), channel_id=1, source_target_pairs={{0,2},{1,7},{2,0},{3,5},{4,6},{5,3},{6,4},{7,1},{8,10},{9,15},{10,... | collective-permute-start | bytes 983048 | tf_op jit(solution)/shard_map/ppermute | solution.py:38
  31.2 8.4 %collective-permute-start.17 = (f32[16,5120]{1,0:T(8,128)S(1)}, f32[16,5120]{1,0:T(8,128)S(1)}, u32[]{:S(2)}, u32[]{:S(2)}) collective-permute-start(f32[16,5120]{1,0:T(8,128)S(1)} %slice_bitcast_fusion), channel_id=1, source_target_pairs={{0,24},{1,9},{2,26},{3,11},{4,28},{5,13},{6,30},{7,15},{8,16},{9,1... | collective-permute-start | bytes 983048 | tf_op jit(solution)/shard_map/ppermute | solution.py:38
  33.3 9.7 %collective-permute-start.4 = (f32[8,5120]{1,0:T(8,128)S(1)}, f32[8,5120]{1,0:T(8,128)S(1)}, u32[]{:S(2)}, u32[]{:S(2)}) collective-permute-start(f32[8,5120]{1,0:T(8,128)S(1)} %slice_bitcast_fusion.4), channel_id=1, source_target_pairs={{0,24},{1,9},{2,26},{3,11},{4,28},{5,13},{6,30},{7,15},{8,16},{9,1... | collective-permute-start | bytes 491528 | tf_op jit(solution)/shard_map/ppermute | solution.py:38
  37.2 10.6 %collective-permute-start.11 = (f32[8,5120]{1,0:T(8,128)S(1)}, f32[8,5120]{1,0:T(8,128)S(1)}, u32[]{:S(2)}, u32[]{:S(2)}) collective-permute-start(f32[8,5120]{1,0:T(8,128)S(1)} %slice_bitcast_fusion.2), channel_id=1, source_target_pairs={{0,24},{1,9},{2,26},{3,11},{4,28},{5,13},{6,30},{7,15},{8,16},{9,1... | collective-permute-start | bytes 491528 | tf_op jit(solution)/shard_map/ppermute | solution.py:38
  39.6 9.9 %collective-permute-start.18 = (f32[8,5120]{1,0:T(8,128)S(1)}, f32[8,5120]{1,0:T(8,128)S(1)}, u32[]{:S(2)}, u32[]{:S(2)}) collective-permute-start(f32[8,5120]{1,0:T(8,128)S(1)} %slice.99), channel_id=1, source_target_pairs={{0,2},{1,7},{2,0},{3,5},{4,6},{5,3},{6,4},{7,1},{8,10},{9,15},{10,... | collective-permute-start | bytes 491528 | tf_op jit(solution)/shard_map/ppermute | solution.py:38
  43.0 7.3 %collective-permute-start.5 = (f32[4,5120]{1,0:T(4,128)S(1)}, f32[4,5120]{1,0:T(4,128)S(1)}, u32[]{:S(2)}, u32[]{:S(2)}) collective-permute-start(f32[4,5120]{1,0:T(4,128)S(1)} %slice.89), channel_id=1, source_target_pairs={{0,6},{1,3},{2,4},{3,1},{4,2},{5,7},{6,0},{7,5},{8,14},{9,11},{10,... | collective-permute-start | bytes 245768 | tf_op jit(solution)/shard_map/ppermute | solution.py:38
  47.8 10.1 %collective-permute-start.12 = (f32[4,5120]{1,0:T(4,128)S(1)}, f32[4,5120]{1,0:T(4,128)S(1)}, u32[]{:S(2)}, u32[]{:S(2)}) collective-permute-start(f32[4,5120]{1,0:T(4,128)S(1)} %slice.95), channel_id=1, source_target_pairs={{0,6},{1,3},{2,4},{3,1},{4,2},{5,7},{6,0},{7,5},{8,14},{9,11},{10,... | collective-permute-start | bytes 245768 | tf_op jit(solution)/shard_map/ppermute | solution.py:38
  50.5 7.5 %collective-permute-start.6 = (f32[1,4,5248]{2,1,0:T(4,128)S(1)}, f32[1,4,5248]{2,1,0:T(4,128)S(1)}, u32[]{:S(2)}, u32[]{:S(2)}) collective-permute-start(f32[1,4,5248]{2,1,0:T(4,128)S(1)} %get-tuple-element.31), channel_id=1, source_target_pairs={{0,32},{32,64},{64,96},{96,128},{128,160},{160,192},{192,224},{224... | collective-permute-start | bytes 251912 | tf_op jit(solution)/shard_map/ppermute | solution.py:23
  53.1 8.1 %collective-permute-start.19 = (f32[4,5120]{1,0:T(4,128)S(1)}, f32[4,5120]{1,0:T(4,128)S(1)}, u32[]{:S(2)}, u32[]{:S(2)}) collective-permute-start(f32[4,5120]{1,0:T(4,128)S(1)} %slice.101), channel_id=1, source_target_pairs={{0,6},{1,3},{2,4},{3,1},{4,2},{5,7},{6,0},{7,5},{8,14},{9,11},{10,... | collective-permute-start | bytes 245768 | tf_op jit(solution)/shard_map/ppermute | solution.py:38
  58.0 5.8 %collective-permute-start.13 = (f32[1,4,5248]{2,1,0:T(4,128)S(1)}, f32[1,4,5248]{2,1,0:T(4,128)S(1)}, u32[]{:S(2)}, u32[]{:S(2)}) collective-permute-start(f32[1,4,5248]{2,1,0:T(4,128)S(1)} %get-tuple-element.38), channel_id=1, source_target_pairs={{0,64},{32,96},{64,128},{96,160},{128,192},{160,224},{192,0},{224,... | collective-permute-start | bytes 251912 | tf_op jit(solution)/shard_map/ppermute | solution.py:23
  63.8 6.1 %collective-permute-start.20 = (f32[1,4,5248]{2,1,0:T(4,128)S(1)}, f32[1,4,5248]{2,1,0:T(4,128)S(1)}, u32[]{:S(2)}, u32[]{:S(2)}) collective-permute-start(f32[1,4,5248]{2,1,0:T(4,128)S(1)} %get-tuple-element.47), channel_id=1, source_target_pairs={{0,128},{32,160},{64,192},{96,224},{128,0},{160,32},{192,64},{224,... | collective-permute-start | bytes 251912 | tf_op jit(solution)/shard_map/ppermute | solution.py:23
